TPU v7x, 128 devices: a whole 4x4x4 slice. The times are simulated.
128 devices in a mesh: edge: 128 (over x, y, z, core).
Axes of the slice: x: 4, y: 4, z: 4, core: 2. Of those that a mesh axis runs over, the one named last changes fastest.
Arguments:
- edge_feats: bfloat16 [393216, 512], P('edge'), may hold values from -6 to 6
- node_feats: bfloat16 [40960, 512], P('edge'), may hold values from -6 to 6
- edge_cot: bfloat16 [393216, 512], P('edge'), may hold values from -6 to 6
- node_cot: bfloat16 [40960, 512], P('edge'), may hold values from -6 to 6
- requests: int32 [128, 384], P('edge'), may hold values from 0 to 319, as said below
- send_slot: int32 [3072, 128], P('edge'), may hold values from 0 to 383
- recv_slot: int32 [3072, 128], P('edge'), may hold values from 0 to 383
- w_input: bfloat16 [3, 512, 512], replicated, may hold values from -0.15625 to 0.15625
- w_output: bfloat16 [512, 512], replicated, may hold values from -0.25 to 0.25
- norm_gain: float32 [512], replicated, may hold values from 0.25 to 1.75
Outputs:
- grad_edges: bfloat16 [393216, 512], P('edge')
- grad_nodes: bfloat16 [40960, 512], P('edge')
- grad_w_input: float32 [3, 512, 512], replicated
- grad_w_output: float32 [512, 512], replicated
- grad_gain: float32 [512], replicated
Inputs may be any that keep to these rules, and one draw needn't show every extreme that they name: `requests`: within each row, each owner's block of 3 entries holds distinct local node indices.
All inputs are finite; a program needn't handle non-finite values.
Results may differ from a plain program's by a relative error of at most 0.011.
Values may be sent and summed in bfloat16 or wider, within the bound.
No kernel may reach another device: no remote copies, remote signals or barrier semaphores. Data moves between devices by JAX's collectives and lax.ppermute only.
A program may use at most 128 MiB of HBM per device.

v0:
```python
import functools

import jax
import jax.numpy as jnp
from jax import lax
from jax.experimental import pallas as pl
from jax.experimental.pallas import tpu as pltpu
from jax.sharding import Mesh, PartitionSpec as P

BF = jnp.bfloat16
F32 = jnp.float32
LANES = 128
CORES = 2
VMEM_BYTES = 56 * 1024 * 1024


def dot(left, right, over=((1,), (0,))):
    return lax.dot_general(left, right, (over, ((), ())), preferred_element_type=F32)


def whole(shape):
    return pl.BlockSpec(shape, lambda *_: (0,) * len(shape))


def smem():
    return pl.BlockSpec(memory_space=pltpu.SMEM)


def one_hot(left, right):
    return jnp.where(left == right, 1.0, 0.0).astype(BF)


def pick_kernel(asked_ref, feats_ref, cots_ref, out_ref, rows):
    devices, cap = asked_ref.shape
    nodes, width = feats_ref.shape
    blocks = width // LANES
    per = cap * 2 * blocks
    spot = lax.broadcasted_iota(jnp.int32, (devices, nodes), 1)
    for k in range(cap):
        hot = one_hot(asked_ref[:, k : k + 1], spot)
        for at, table in enumerate((feats_ref, cots_ref)):
            found = dot(hot, table[...])
            for j in range(blocks):
                rows[pl.ds(k * 2 * blocks + at * blocks + j, devices, stride=per), :] = found[
                    :, j * LANES : (j + 1) * LANES
                ]
    out_ref[...] = rows[...].astype(BF)


def pick_rows(asked, feats, cots):
    devices, cap = asked.shape
    width = feats.shape[1]
    total = devices * cap * 2 * width // LANES
    return pl.pallas_call(
        pick_kernel,
        out_shape=jax.ShapeDtypeStruct((total, LANES), BF),
        scratch_shapes=[pltpu.VMEM((total, LANES), F32)],
        compiler_params=pltpu.CompilerParams(vmem_limit_bytes=VMEM_BYTES),
        name="pick_rows",
    )(asked, feats, cots)


def slot_ids(position, chips, cap):
    half = cap * chips
    core = jnp.where(position >= half, 1, 0)
    rest = position - core * half
    k = jnp.where(rest >= chips, 1, 0) + jnp.where(rest >= 2 * chips, 1, 0)
    chip = rest - k * chips
    return chip * (CORES * cap) + core * cap + k


def edge_kernel(
    cap,
    core_ref,
    send_ref,
    recv_ref,
    rows_ref,
    w_in_ref,
    w_out_ref,
    gain_ref,
    feats_ref,
    cot_ref,
    grad_ref,
    own_ref,
    other_ref,
    rows32,
    feat_tab,
    cot_tab,
    pre_tab,
    sums,
    grads,
    gain_sum,
    nodes,
    tail,
):
    step, steps = pl.program_id(0), pl.num_programs(0)
    tile, width = feats_ref.shape
    slots = feat_tab.shape[0]
    chips = slots // (cap * CORES)
    blocks = width // LANES
    per = cap * 2 * blocks

    @pl.when(step == 0)
    def _():
        rows32[...] = rows_ref[...].astype(F32)
        for core in range(CORES):
            for k in range(cap):
                at = (core * cap + k) * chips
                for j in range(blocks):
                    cols = slice(j * LANES, (j + 1) * LANES)
                    first = core * per + k * 2 * blocks + j
                    feat_tab[at : at + chips, cols] = rows32[
                        pl.ds(first, chips, stride=CORES * per), :
                    ].astype(BF)
                    cot_tab[at : at + chips, cols] = rows32[
                        pl.ds(first + blocks, chips, stride=CORES * per), :
                    ].astype(BF)
        for part in range(2):
            pre_tab[part * slots : (part + 1) * slots, :] = dot(
                feat_tab[...], w_in_ref[part + 1]
            ).astype(BF)
        sums[...] = jnp.zeros_like(sums)
        grads[...] = jnp.zeros_like(grads)
        gain_sum[...] = jnp.zeros_like(gain_sum)

    lane_ids = slot_ids(lax.broadcasted_iota(jnp.int32, (1, slots), 1), chips, cap)
    row_ids = slot_ids(lax.broadcasted_iota(jnp.int32, (slots, LANES), 0), chips, cap)
    groups = tile // LANES
    hot_rows, hot_cols = [], []
    for ref in (send_ref, recv_ref):
        found_rows, found_cols = [], []
        for g in range(groups):
            line = ref[pl.ds(step * groups + g, 1), :]
            found_cols.append(one_hot(row_ids, line))
            upright = jnp.broadcast_to(line, (LANES, LANES)).T
            found_rows.append(
                jnp.concatenate(
                    [
                        one_hot(upright, lane_ids[:, b * LANES : (b + 1) * LANES])
                        for b in range(slots // LANES)
                    ],
                    axis=1,
                )
            )
        hot_rows.append(jnp.concatenate(found_rows, axis=0))
        hot_cols.append(jnp.concatenate(found_cols, axis=1))
    both_rows = jnp.concatenate(hot_rows, axis=1)
    both_cols = jnp.concatenate(hot_cols, axis=0)

    feats = feats_ref[...]
    preact = dot(feats, w_in_ref[0]) + dot(both_rows, pre_tab[...])
    logistic = 0.5 * jnp.tanh(0.5 * preact) + 0.5
    silu = preact * logistic
    hidden = silu.astype(BF)
    slope = logistic + silu * (1.0 - logistic)
    mixed = dot(hidden, w_out_ref[...])
    center = mixed - jnp.mean(mixed, axis=1, keepdims=True)
    inverse = lax.rsqrt(jnp.mean(center * center, axis=1, keepdims=True) + 1e-5)
    normed = center * inverse
    cots = cot_ref[...].astype(F32)
    upstream = cots + dot(hot_rows[1], cot_tab[...])
    scaled = upstream * gain_ref[...]
    d_mixed = (
        inverse
        * (
            scaled
            - jnp.mean(scaled, axis=1, keepdims=True)
            - normed * jnp.mean(scaled * normed, axis=1, keepdims=True)
        )
    ).astype(BF)
    product = upstream * normed
    gain_sum[...] += jnp.sum(product.reshape(tile // 8, 8, width), axis=0)
    d_hidden = dot(d_mixed, w_out_ref[...], ((1,), (1,)))
    d_preact = (d_hidden * slope).astype(BF)
    grad_ref[...] = (cots + dot(d_preact, w_in_ref[0], ((1,), (1,)))).astype(BF)
    sums[...] += dot(both_cols, d_preact)
    grads[0:width, :] += dot(feats, d_preact, ((0,), (0,)))
    grads[3 * width : 4 * width, :] += dot(hidden, d_mixed, ((0,), (0,)))

    @pl.when(step == steps - 1)
    def _():
        sender = sums[0:slots, :].astype(BF)
        receiver = sums[slots : 2 * slots, :].astype(BF)
        nodes[...] = dot(sender, w_in_ref[1], ((1,), (1,))) + dot(
            receiver, w_in_ref[2], ((1,), (1,))
        )
        grads[width : 2 * width, :] = dot(feat_tab[...], sender, ((0,), (0,)))
        grads[2 * width : 3 * width, :] = dot(feat_tab[...], receiver, ((0,), (0,)))
        gain = jnp.sum(gain_sum[...], axis=0, keepdims=True)
        core = core_ref[0]
        piece = 2 * width // chips
        body = piece * blocks
        for target, which in ((own_ref, core), (other_ref, 1 - core)):
            first = pl.multiple_of(which * (2 * width), 2 * width)
            for j in range(blocks):
                cols = slice(j * LANES, (j + 1) * LANES)
                target[:, j * piece : (j + 1) * piece, :] = (
                    grads[pl.ds(first, 2 * width), cols].reshape(chips, piece, LANES).astype(BF)
                )
                for k in range(cap):
                    begin = pl.multiple_of(which * (cap * chips) + k * chips, chips)
                    tail[pl.ds(k * blocks + j, chips, stride=16), :] = nodes[
                        pl.ds(begin, chips), cols
                    ]
                tail[pl.ds(cap * blocks + j, chips, stride=16), :] = jnp.broadcast_to(
                    gain[:, cols], (chips, LANES)
                )
            target[:, body : body + 16, :] = tail[...].reshape(chips, 16, LANES).astype(BF)


def edge_pass(core, send_slot, recv_slot, rows, w_input, w_output, gain, feats, cot, cap, tile):
    edges, width = feats.shape
    devices = rows.shape[0] * LANES // (cap * 2 * width)
    chips = devices // CORES
    slots = devices * cap
    blocks = width // LANES
    packet = 2 * width // chips * blocks + 16
    tiles = pl.BlockSpec((tile, width), lambda i: (i, 0))
    packets = jax.ShapeDtypeStruct((chips, packet, LANES), BF)
    return pl.pallas_call(
        functools.partial(edge_kernel, cap),
        grid=(edges // tile,),
        in_specs=[
            smem(),
            whole(send_slot.shape),
            whole(recv_slot.shape),
            whole(rows.shape),
            whole(w_input.shape),
            whole(w_output.shape),
            whole(gain.shape),
            tiles,
            tiles,
        ],
        out_specs=[tiles, whole(packets.shape), whole(packets.shape)],
        out_shape=[jax.ShapeDtypeStruct(feats.shape, BF), packets, packets],
        scratch_shapes=[
            pltpu.VMEM(rows.shape, F32),
            pltpu.VMEM((slots, width), BF),
            pltpu.VMEM((slots, width), BF),
            pltpu.VMEM((2 * slots, width), BF),
            pltpu.VMEM((2 * slots, width), F32),
            pltpu.VMEM((4 * width, width), F32),
            pltpu.VMEM((8, width), F32),
            pltpu.VMEM((slots, width), F32),
            pltpu.VMEM((chips * 16, LANES), F32),
        ],
        compiler_params=pltpu.CompilerParams(vmem_limit_bytes=VMEM_BYTES),
        name="edge_pass",
    )(core, send_slot, recv_slot, rows, w_input, w_output, gain, feats, cot)


def merge_kernel(own_ref, got_ref, out_ref):
    body = own_ref.shape[1] - 16
    out_ref[:, 0:body, :] = (
        own_ref[:, 0:body, :].astype(F32) + got_ref[:, 0:body, :].astype(F32)
    ).astype(BF)
    out_ref[:, body : body + 16, :] = own_ref[:, body : body + 16, :]
    out_ref[:, body + 16 : body + 32, :] = got_ref[:, body : body + 16, :]


def merge(own, got):
    chips, packet, _ = own.shape
    step = 8
    spec = pl.BlockSpec((step, packet, LANES), lambda i: (i, 0, 0))
    return pl.pallas_call(
        merge_kernel,
        grid=(chips // step,),
        in_specs=[spec, spec],
        out_specs=pl.BlockSpec((step, packet + 16, LANES), lambda i: (i, 0, 0)),
        out_shape=jax.ShapeDtypeStruct((chips, packet + 16, LANES), BF),
        name="merge",
    )(own, got)


def reduce_kernel(factor, gain_row, in_ref, out_ref, gain_ref):
    chips, packet, _ = in_ref.shape
    body = packet - 32
    total = jnp.sum(in_ref[:, 0:body, :].astype(F32), axis=0) * factor
    out_ref[...] = jnp.broadcast_to(total.astype(BF)[None], out_ref.shape)
    ends = jnp.sum(
        in_ref[:, body : body + 16, :].astype(F32) + in_ref[:, body + 16 : body + 32, :].astype(F32),
        axis=0,
    )
    gain_ref[...] = ends[gain_row:16, :] * factor


def reduce_packets(packets, factor, gain_row):
    chips, packet, _ = packets.shape
    return pl.pallas_call(
        functools.partial(reduce_kernel, factor, gain_row),
        out_shape=[
            jax.ShapeDtypeStruct((chips, packet - 32, LANES), BF),
            jax.ShapeDtypeStruct((16 - gain_row, LANES), F32),
        ],
        compiler_params=pltpu.CompilerParams(vmem_limit_bytes=VMEM_BYTES),
        name="reduce_packets",
    )(packets)


def node_kernel(core_ref, asked_ref, packets_ref, cots_ref, out_ref, ends, rows, hots):
    devices, cap = asked_ref.shape
    nodes, width = cots_ref.shape
    chips = devices // CORES
    blocks = width // LANES
    body = packets_ref.shape[1] - 32
    ends[...] = packets_ref[:, body : body + 32, :].astype(F32).reshape(chips * 32, LANES)
    spot = lax.broadcasted_iota(jnp.int32, (chips, nodes), 1)
    core = core_ref[0]
    for flag in range(CORES):
        asker = core if flag == 0 else 1 - core
        asked = asked_ref[pl.ds(asker, chips, stride=CORES), :]
        for k in range(cap):
            at = (flag * cap + k) * chips
            hots[at : at + chips, :] = one_hot(asked[:, k : k + 1], spot)
            for j in range(blocks):
                rows[at : at + chips, j * LANES : (j + 1) * LANES] = ends[
                    pl.ds(flag * 16 + k * blocks + j, chips, stride=32), :
                ].astype(BF)
    sums = dot(hots[...], rows[...], ((0,), (0,)))
    out_ref[...] = (cots_ref[...].astype(F32) + sums).astype(BF)


def node_grads(core, asked, packets, cots):
    devices, cap = asked.shape
    nodes, width = cots.shape
    slots = devices * cap
    vmem = pl.BlockSpec(memory_space=pltpu.VMEM)
    return pl.pallas_call(
        node_kernel,
        in_specs=[smem(), vmem, vmem, vmem],
        out_specs=vmem,
        out_shape=jax.ShapeDtypeStruct(cots.shape, BF),
        scratch_shapes=[
            pltpu.VMEM((devices // CORES * 32, LANES), F32),
            pltpu.VMEM((slots, width), BF),
            pltpu.VMEM((slots, nodes), BF),
        ],
        compiler_params=pltpu.CompilerParams(vmem_limit_bytes=VMEM_BYTES),
        name="node_grads",
    )(core, asked, packets, cots)


def unpack_kernel(core_ref, mine_ref, other_ref, input_ref, output_ref):
    chips, body, _ = mine_ref.shape
    width = output_ref.shape[0]
    blocks = width // LANES
    piece = body // blocks

    def write(low, high):
        for j in range(blocks):
            cols = slice(j * LANES, (j + 1) * LANES)
            lower = low[:, j * piece : (j + 1) * piece, :].astype(F32).reshape(2 * width, LANES)
            upper = high[:, j * piece : (j + 1) * piece, :].astype(F32).reshape(2 * width, LANES)
            input_ref[0 : 2 * width, cols] = lower
            input_ref[2 * width : 3 * width, cols] = upper[0:width]
            output_ref[:, cols] = upper[width : 2 * width]

    @pl.when(core_ref[0] == 0)
    def _():
        write(mine_ref, other_ref)

    @pl.when(core_ref[0] != 0)
    def _():
        write(other_ref, mine_ref)


def unpack(core, mine, other, width):
    vmem = pl.BlockSpec(memory_space=pltpu.VMEM)
    return pl.pallas_call(
        unpack_kernel,
        in_specs=[smem(), vmem, vmem],
        out_specs=[vmem, vmem],
        out_shape=[
            jax.ShapeDtypeStruct((3 * width, width), F32),
            jax.ShapeDtypeStruct((width, width), F32),
        ],
        compiler_params=pltpu.CompilerParams(vmem_limit_bytes=VMEM_BYTES),
        name="unpack",
    )(core, mine, other)


def on_device(
    edge_feats,
    node_feats,
    edge_cot,
    node_cot,
    requests,
    send_slot,
    recv_slot,
    w_input,
    w_output,
    norm_gain,
):
    chips, cores = lax.axis_size("chip"), lax.axis_size("core")
    devices = chips * cores
    both = ("chip", "core")
    cap = requests.shape[1] // devices
    edges, width = edge_feats.shape
    core = lax.axis_index("core").astype(jnp.int32).reshape(1)
    pairs = [(d, d ^ 1) for d in range(devices)]

    asked = lax.all_to_all(
        requests.reshape(devices, 1, cap), both, split_axis=0, concat_axis=0, tiled=True
    ).reshape(devices, cap)
    picked = pick_rows(asked, node_feats, node_cot).reshape(devices, -1, LANES)
    rows = lax.all_to_all(picked, both, split_axis=0, concat_axis=0, tiled=True).reshape(-1, LANES)
    grad_edges, own, other = edge_pass(
        core,
        send_slot,
        recv_slot,
        rows,
        w_input,
        w_output,
        norm_gain.reshape(1, width),
        edge_feats,
        edge_cot,
        cap,
        512,
    )
    got = lax.ppermute(other, both, pairs)
    packets = lax.all_to_all(merge(own, got), "chip", split_axis=0, concat_axis=0, tiled=True)
    factor = float(edges * devices) ** (-0.5)
    pieces, gain = reduce_packets(packets, factor, cap * width // LANES)
    mine = lax.all_to_all(pieces, "chip", split_axis=0, concat_axis=0, tiled=True)
    grad_nodes = node_grads(core, asked, packets, node_cot)
    partner = lax.ppermute(mine, both, pairs)
    grad_input, grad_output = unpack(core, mine, partner, width)
    return (
        grad_edges,
        grad_nodes,
        grad_input.reshape(3, width, width),
        grad_output,
        gain.reshape(width),
    )


def solution(mesh):
    pairs = Mesh(mesh.devices.reshape(-1, CORES), ("chip", "core"))
    rows = P(("chip", "core"), None)
    return jax.shard_map(
        on_device,
        mesh=pairs,
        in_specs=(rows,) * 7 + (P(),) * 3,
        out_specs=(rows, rows, P(), P(), P()),
        check_vma=False,
    )
```

profile of v0, /device:TPU:1, one launch (start us, length us, event | category | flops | bytes accessed | tf_op | source)
XLA Modules:
  0.0 150.5 jit_solution(5926376938507426309)
XLA Ops:
  0.6 0.7 reduce
  1.3 0.2 reshape.35
  1.5 21.2 %all_to_all.20 = s32[128,1,3]{2,1,0:T(1,128)} all-to-all(s32[128,1,3]{2,1,0:T(1,128)S(1)} %bitcast.12), channel_id=1, replica_groups=mesh['chip'=64,'core'=2] {'chip','core'}, dimensions={0} | all-to-all | bytes 3072 | tf_op jit(solution)/shard_map/all_to_all | solution.py:402
  22.7 2.6 %pick_rows.1 = bf16[3072,128]{1,0:T(8,128)(2,1)} custom-call(s32[128,3]{1,0:T(8,128)} %bitcast.10, bf16[320,512]{1,0:T(8,128)(2,1)} %feats_ref.2, bf16[320,512]{1,0:T(8,128)(2,1)} %cots_ref.3), custom_call_target="tpu_custom_call" | custom-call | tf_op jit(solution)/shard_map/pick_rows/pallas_call | solution.py:54
  25.3 4.6 %all-to-all-start.1 = ((bf16[128,24,128]{2,1,0:T(8,128)(2,1)}), bf16[128,24,128]{2,1,0:T(8,128)(2,1)S(1)}, u32[]{:S(2)}, u32[]{:S(2)}) async-start(bf16[128,24,128]{2,1,0:T(8,128)(2,1)} %bitcast.9), calls=%async_computation.1 | async-start | bytes 1572864 | tf_op jit(solution)/shard_map/all_to_all | solution.py:406
  29.9 16.5 %all-to-all-done.1 = bf16[128,24,128]{2,1,0:T(8,128)(2,1)S(1)} async-done(((bf16[128,24,128]{2,1,0:T(8,128)(2,1)}), bf16[128,24,128]{2,1,0:T(8,128)(2,1)S(1)}, u32[]{:S(2)}, u32[]{:S(2)}) %all-to-all-start.1) | async-done | bytes 786464 | tf_op jit(solution)/shard_map/all_to_all | solution.py:406
  46.5 0.0 copy-start.1
  46.5 0.9 copy-done.1
  47.3 27.8 %edge_pass.1 = (bf16[3072,512]{1,0:T(8,128)(2,1)}, bf16[64,80,128]{2,1,0:T(8,128)(2,1)}, bf16[64,80,128]{2,1,0:T(8,128)(2,1)}) custom-call(s32[1]{0:T(128)} %bitcast.core_ref, s32[24,128]{1,0:T(8,128)} %send_ref.1, s32[24,128]{1,0:T(8,128)} %recv_ref.1, bf16[3072,128]{1,0:T(8,128)(2,1)} %bitcast.8, bf16[3,512,512]{2,1,0:T(8,128)(2,1)} %w_in_ref.1, ...), custom_call_target="tpu_custom_call" | custom-call | tf_op jit(solution)/shard_map/edge_pass/pallas_call | solution.py:220
  75.1 1.2 collective-permute-start
  76.4 2.9 %collective-permute-done.got_ref = bf16[64,80,128]{2,1,0:T(8,128)(2,1)S(1)} collective-permute-done((bf16[64,80,128]{2,1,0:T(8,128)(2,1)}, bf16[64,80,128]{2,1,0:T(8,128)(2,1)S(1)}, u32[]{:S(2)}, u32[]{:S(2)}) %collective-permute-start) | collective-permute-done | bytes 1310752 | tf_op jit(solution)/shard_map/ppermute | solution.py:420
  79.2 0.0 copy-start.2
  79.2 1.1 copy-done.2
  80.3 5.8 %merge.1 = bf16[64,96,128]{2,1,0:T(8,128)(2,1)} custom-call(bf16[64,80,128]{2,1,0:T(8,128)(2,1)} %get-tuple-element.13.own_ref, bf16[64,80,128]{2,1,0:T(8,128)(2,1)} %copy-done.2), custom_call_target="tpu_custom_call" | custom-call | tf_op jit(solution)/shard_map/merge/pallas_call | solution.py:265
  86.1 27.9 %all_to_all.21.packets_ref.in_ref = bf16[64,96,128]{2,1,0:T(8,128)(2,1)} all-to-all(bf16[64,96,128]{2,1,0:T(8,128)(2,1)} %merge.1), channel_id=1, replica_groups=mesh['chip'=64,'core'=2] {'chip'}, dimensions={0} | all-to-all | bytes 3145728 | tf_op jit(solution)/shard_map/all_to_all | solution.py:421
  114.0 2.6 %reduce_packets.1 = (bf16[64,64,128]{2,1,0:T(8,128)(2,1)}, f32[4,128]{1,0:T(4,128)}) custom-call(bf16[64,96,128]{2,1,0:T(8,128)(2,1)} %all_to_all.21.packets_ref.in_ref), custom_call_target="tpu_custom_call" | custom-call | tf_op jit(solution)/shard_map/reduce_packets/pallas_call | solution.py:289
  116.6 22.2 %all_to_all.22.mine_ref = bf16[64,64,128]{2,1,0:T(8,128)(2,1)S(1)} all-to-all(bf16[64,64,128]{2,1,0:T(8,128)(2,1)} %get-tuple-element.15), channel_id=1, replica_groups=mesh['chip'=64,'core'=2] {'chip'}, dimensions={0} | all-to-all | bytes 2097152 | tf_op jit(solution)/shard_map/all_to_all | solution.py:424
  138.9 0.0 copy-start
  138.9 3.4 %collective-permute-start.1 = (bf16[64,64,128]{2,1,0:T(8,128)(2,1)S(1)}, bf16[64,64,128]{2,1,0:T(8,128)(2,1)S(1)}, u32[]{:S(2)}, u32[]{:S(2)}) collective-permute-start(bf16[64,64,128]{2,1,0:T(8,128)(2,1)S(1)} %all_to_all.22.mine_ref), channel_id=1, source_target_pairs={{0,1},{1,0},{2,3},{3,2},{4,5},{5,4},{6,7},{7,6},{8,9},{9,8},{10,11... | collective-permute-start | bytes 3145736 | tf_op jit(solution)/shard_map/ppermute | solution.py:426
  142.2 3.1 %node_grads.1 = bf16[320,512]{1,0:T(8,128)(2,1)} custom-call(s32[1]{0:T(128)} %bitcast.core_ref, s32[128,3]{1,0:T(8,128)} %bitcast.11, bf16[64,96,128]{2,1,0:T(8,128)(2,1)} %all_to_all.21.packets_ref.in_ref, bf16[320,512]{1,0:T(8,128)(2,1)} %cots_ref.3), custom_call_target="tpu_custom_call" | custom-call | tf_op jit(solution)/shard_map/node_grads/pallas_call | solution.py:328
  145.4 0.0 collective-permute-done.1.other_ref
  145.4 0.0 copy-done
  145.4 1.0 copy-done.3
  146.3 4.2 %unpack.1 = (f32[1536,512]{1,0:T(8,128)}, f32[512,512]{1,0:T(8,128)}) custom-call(s32[1]{0:T(128)} %bitcast.core_ref, bf16[64,64,128]{2,1,0:T(8,128)(2,1)} %copy-done, bf16[64,64,128]{2,1,0:T(8,128)(2,1)} %copy-done.3), custom_call_target="tpu_custom_call" | custom-call | tf_op jit(solution)/shard_map/unpack/pallas_call | solution.py:369
  (1 shorter events, 0.0 us)
Async XLA Ops:
  25.3 21.1 %all-to-all-start.1 = ((bf16[128,24,128]{2,1,0:T(8,128)(2,1)}), bf16[128,24,128]{2,1,0:T(8,128)(2,1)S(1)}, u32[]{:S(2)}, u32[]{:S(2)}) async-start(bf16[128,24,128]{2,1,0:T(8,128)(2,1)} %bitcast.9), calls=%async_computation.1 | async-start | bytes 1572864 | tf_op jit(solution)/shard_map/all_to_all | solution.py:406
  46.5 0.9 copy-start.1
  75.1 4.1 %collective-permute-start = (bf16[64,80,128]{2,1,0:T(8,128)(2,1)}, bf16[64,80,128]{2,1,0:T(8,128)(2,1)S(1)}, u32[]{:S(2)}, u32[]{:S(2)}) collective-permute-start(bf16[64,80,128]{2,1,0:T(8,128)(2,1)} %get-tuple-element.14), channel_id=1, source_target_pairs={{0,1},{1,0},{2,3},{3,2},{4,5},{5,4},{6,7},{7,6},{8,9},{9,8},{10,11... | collective-permute-start | bytes 3932168 | tf_op jit(solution)/shard_map/ppermute | solution.py:420
  79.2 1.1 copy-start.2
  138.9 6.5 %copy-start = (bf16[64,64,128]{2,1,0:T(8,128)(2,1)}, bf16[64,64,128]{2,1,0:T(8,128)(2,1)S(1)}, u32[]{:S(2)}) copy-start(bf16[64,64,128]{2,1,0:T(8,128)(2,1)S(1)} %all_to_all.22.mine_ref) | copy-start | bytes 3145732
  138.9 6.5 %collective-permute-start.1 = (bf16[64,64,128]{2,1,0:T(8,128)(2,1)S(1)}, bf16[64,64,128]{2,1,0:T(8,128)(2,1)S(1)}, u32[]{:S(2)}, u32[]{:S(2)}) collective-permute-start(bf16[64,64,128]{2,1,0:T(8,128)(2,1)S(1)} %all_to_all.22.mine_ref), channel_id=1, source_target_pairs={{0,1},{1,0},{2,3},{3,2},{4,5},{5,4},{6,7},{7,6},{8,9},{9,8},{10,11... | collective-permute-start | bytes 3145736 | tf_op jit(solution)/shard_map/ppermute | solution.py:426
  145.4 1.0 copy-start.3
where the time goes:
time: 151 us
  blocking collectives  71.3 us (47%)
  Pallas kernels  46.2 us (31%)
  waiting for transfers between devices  19.4 us (13%)
  starting transfers between devices  9.19 us (6%)
  local copies, waits for them, and re-layouts  3.11 us (2%)
    all_to_all x1, blocking collectives, on_device(): lax.all_to_all(merge(own, got), 'chip', split_axis=0, concat_axis=0, tile...  27.9 us
    pallas_call x1, Pallas kernels, edge_pass(): pl.pallas_call(functools.partial(edge_kernel, cap), grid=(edges // tile,)...  27.8 us
    all_to_all x1, blocking collectives, on_device(): lax.all_to_all(pieces, 'chip', split_axis=0, concat_axis=0, tiled=True)  22.2 us
    all_to_all x1, blocking collectives, on_device(): lax.all_to_all(requests.reshape(devices, 1, cap), both, split_axis=0, con...  21.2 us
    all_to_all x1, waiting for transfers between devices, on_device(): lax.all_to_all(picked, both, split_axis=0, concat_axis=0, tiled=True)  16.5 us
    pallas_call x1, Pallas kernels, merge(): pl.pallas_call(merge_kernel, grid=(chips // step,), in_specs=[spec, spec]...  5.8 us
    all_to_all x1, starting transfers between devices, on_device(): lax.all_to_all(picked, both, split_axis=0, concat_axis=0, tiled=True)  4.59 us
    pallas_call x1, Pallas kernels, unpack(): pl.pallas_call(unpack_kernel, in_specs=[smem(), vmem, vmem], out_specs=[v...  4.19 us
  transfers between devices with their start and end apart: 3, of which 2 were waited for; matrix products, arithmetic and copies ran while one was open for 0% of the time, Pallas kernels for 2%

commit v1 on v0

v1 whole, which is shorter than its diff:
```python
import functools

import jax
import jax.numpy as jnp
from jax import lax
from jax.experimental import pallas as pl
from jax.experimental.pallas import tpu as pltpu
from jax.sharding import Mesh, PartitionSpec as P

BF = jnp.bfloat16
F32 = jnp.float32
LANES = 128
CORES = 2
TILE = 768
PRE = F32
BIG_VMEM = 48 * 1024 * 1024
VMEM = pl.BlockSpec(memory_space=pltpu.VMEM)


def dot(left, right, over=((1,), (0,))):
    return lax.dot_general(left, right, (over, ((), ())), preferred_element_type=F32)


def whole(shape):
    return pl.BlockSpec(shape, lambda *_: (0,) * len(shape))


def smem():
    return pl.BlockSpec(memory_space=pltpu.SMEM)


def cost(flops, moved):
    return pl.CostEstimate(flops=flops, bytes_accessed=moved, transcendentals=0)


def one_hot(left, right):
    return jnp.where(left == right, 1.0, 0.0).astype(BF)


def pick_kernel(asked_ref, feats_ref, cots_ref, out_ref, rows):
    devices, cap = asked_ref.shape
    nodes, width = feats_ref.shape
    blocks = width // LANES
    per = cap * 2 * blocks
    spot = lax.broadcasted_iota(jnp.int32, (devices, nodes), 1)
    for k in range(cap):
        hot = one_hot(asked_ref[:, k : k + 1], spot)
        for at, table in enumerate((feats_ref, cots_ref)):
            found = dot(hot, table[...])
            for j in range(blocks):
                rows[pl.ds(k * 2 * blocks + at * blocks + j, devices, stride=per), :] = found[
                    :, j * LANES : (j + 1) * LANES
                ]
    out_ref[...] = rows[...].astype(BF)


def pick_rows(asked, feats, cots):
    devices, cap = asked.shape
    width = feats.shape[1]
    total = devices * cap * 2 * width // LANES
    return pl.pallas_call(
        pick_kernel,
        out_shape=jax.ShapeDtypeStruct((total, LANES), BF),
        scratch_shapes=[pltpu.VMEM((total, LANES), F32)],
        compiler_params=pltpu.CompilerParams(vmem_limit_bytes=BIG_VMEM),
        cost_estimate=cost(4 * devices * cap * feats.size, 4 * total * LANES),
        name="pick_rows",
    )(asked, feats, cots)


def slot_ids(position, chips, cap):
    half = cap * chips
    core = jnp.where(position >= half, 1, 0)
    rest = position - core * half
    k = jnp.where(rest >= chips, 1, 0) + jnp.where(rest >= 2 * chips, 1, 0)
    chip = rest - k * chips
    return chip * (CORES * cap) + core * cap + k


def prep_kernel(feats_ref, w_ref, pre_ref, turned_ref):
    feats = feats_ref[...]
    pre_ref[...] = dot(feats, w_ref[0]).astype(PRE)
    turned_ref[0] = feats.T


def prep_pass(feats, w_input, tile):
    edges, width = feats.shape
    tiles = edges // tile
    rows = pl.BlockSpec((tile, width), lambda i: (i, 0))
    return pl.pallas_call(
        prep_kernel,
        grid=(tiles,),
        in_specs=[rows, pl.BlockSpec((1, width, width), lambda i: (0, 0, 0))],
        out_specs=[rows, pl.BlockSpec((1, width, tile), lambda i: (i, 0, 0))],
        out_shape=[
            jax.ShapeDtypeStruct((edges, width), PRE),
            jax.ShapeDtypeStruct((tiles, width, tile), BF),
        ],
        compiler_params=pltpu.CompilerParams(vmem_limit_bytes=BIG_VMEM),
        cost_estimate=cost(2 * edges * width * width, 8 * feats.size),
        name="prep_pass",
    )(feats, w_input)


def grad_kernel(d_preact_ref, w_ref, cot_ref, out_ref):
    grad = dot(d_preact_ref[...], w_ref[0], ((1,), (1,)))
    out_ref[...] = (cot_ref[...].astype(F32) + grad).astype(BF)


def grad_pass(d_preact, w_input, cot, tile):
    edges, width = cot.shape
    tiles = pl.BlockSpec((tile, width), lambda i: (i, 0))
    return pl.pallas_call(
        grad_kernel,
        grid=(edges // tile,),
        in_specs=[tiles, pl.BlockSpec((1, width, width), lambda i: (0, 0, 0)), tiles],
        out_specs=tiles,
        out_shape=jax.ShapeDtypeStruct(cot.shape, BF),
        cost_estimate=cost(2 * edges * width * width, 6 * cot.size),
        name="grad_pass",
    )(d_preact, w_input, cot)


def edge_kernel(
    cap,
    core_ref,
    send_ref,
    recv_ref,
    gain_ref,
    rows_hbm,
    w_in_hbm,
    w_out_hbm,
    pre_hbm,
    turned_hbm,
    cot_hbm,
    d_preact_hbm,
    own_ref,
    other_ref,
    sums_ref,
    rows16,
    rows32,
    w_in,
    w_out,
    pre,
    turned,
    cot,
    d_preact,
    feat_tab,
    cot_tab,
    pre_tab,
    hot_rows,
    hot_cols,
    hidden,
    d_mixed,
    sums,
    grads,
    gain_sum,
    once,
    per_tile,
):
    tiles, _, tile = turned.shape
    slots, width = feat_tab.shape
    chips = slots // (cap * CORES)
    blocks = width // LANES
    per = cap * 2 * blocks
    groups = tile // LANES

    def span(t):
        return pl.ds(pl.multiple_of(t * tile, tile), tile)

    first = (
        pltpu.make_async_copy(rows_hbm, rows16, once.at[0]),
        pltpu.make_async_copy(w_in_hbm.at[pl.ds(1, 2)], w_in, once.at[1]),
        pltpu.make_async_copy(w_out_hbm, w_out, once.at[2]),
    )

    def load(t):
        return (
            pltpu.make_async_copy(pre_hbm.at[span(t)], pre.at[span(t)], per_tile.at[0, t]),
            pltpu.make_async_copy(cot_hbm.at[span(t)], cot.at[span(t)], per_tile.at[1, t]),
            pltpu.make_async_copy(turned_hbm.at[t], turned.at[t], per_tile.at[2, t]),
        )

    def leave(t):
        return pltpu.make_async_copy(d_preact.at[span(t)], d_preact_hbm.at[span(t)], per_tile.at[3, t])

    for copy in first:
        copy.start()
    for copy in load(0):
        copy.start()

    lane_ids = slot_ids(lax.broadcasted_iota(jnp.int32, (1, slots), 1), chips, cap)
    row_ids = slot_ids(lax.broadcasted_iota(jnp.int32, (slots, LANES), 0), chips, cap)

    def mark_rows(t):
        for g in range(groups):
            for at, ref in enumerate((send_ref, recv_ref)):
                upright = jnp.broadcast_to(ref[pl.ds(t * groups + g, 1), :], (LANES, LANES)).T
                for b in range(slots // LANES):
                    hot_rows[g * LANES : (g + 1) * LANES, at * slots + b * LANES : at * slots + (b + 1) * LANES] = (
                        one_hot(upright, lane_ids[:, b * LANES : (b + 1) * LANES])
                    )

    def mark_cols(t):
        for g in range(groups):
            for at, ref in enumerate((send_ref, recv_ref)):
                hot_cols[at * slots : (at + 1) * slots, g * LANES : (g + 1) * LANES] = one_hot(
                    row_ids, ref[pl.ds(t * groups + g, 1), :]
                )

    sums[...] = jnp.zeros_like(sums)
    grads[0:width, :] = jnp.zeros((width, width), F32)
    grads[3 * width : 4 * width, :] = jnp.zeros((width, width), F32)
    gain_sum[...] = jnp.zeros_like(gain_sum)
    mark_rows(0)
    first[0].wait()
    rows32[...] = rows16[...].astype(F32)
    for core in range(CORES):
        for k in range(cap):
            at = (core * cap + k) * chips
            for j in range(blocks):
                cols = slice(j * LANES, (j + 1) * LANES)
                begin = core * per + k * 2 * blocks + j
                feat_tab[at : at + chips, cols] = rows32[pl.ds(begin, chips, stride=CORES * per), :].astype(BF)
                cot_tab[at : at + chips, cols] = rows32[
                    pl.ds(begin + blocks, chips, stride=CORES * per), :
                ].astype(BF)
    first[1].wait()
    for t in range(1, tiles):
        for copy in load(t):
            copy.start()
    for part in range(2):
        pre_tab[part * slots : (part + 1) * slots, :] = dot(feat_tab[...], w_in[part]).astype(BF)
    first[2].wait()
    for copy in load(0):
        copy.wait()

    def contract(t):
        mark_cols(t)
        arrived = d_preact[span(t), :]
        sums[...] += dot(hot_cols[...], arrived)
        grads[0:width, :] += dot(turned[t], arrived)
        grads[3 * width : 4 * width, :] += dot(hidden[...], d_mixed[...], ((0,), (0,)))

    def chain(t):
        preact = pre[span(t), :].astype(F32) + dot(hot_rows[...], pre_tab[...])
        logistic = 0.5 * jnp.tanh(0.5 * preact) + 0.5
        silu = preact * logistic
        rounded = silu.astype(BF)
        hidden[...] = rounded
        slope = logistic + silu * (1.0 - logistic)
        mixed = dot(rounded, w_out[...])
        center = mixed - jnp.mean(mixed, axis=1, keepdims=True)
        inverse = lax.rsqrt(jnp.mean(center * center, axis=1, keepdims=True) + 1e-5)
        normed = center * inverse
        upstream = cot[span(t), :].astype(F32) + dot(hot_rows[:, slots:], cot_tab[...])
        scaled = upstream * gain_ref[...]
        turned_back = (
            inverse
            * (
                scaled
                - jnp.mean(scaled, axis=1, keepdims=True)
                - normed * jnp.mean(scaled * normed, axis=1, keepdims=True)
            )
        ).astype(BF)
        gain_sum[...] += jnp.sum((upstream * normed).reshape(tile // 8, 8, width), axis=0)
        d_mixed[...] = turned_back
        d_hidden = dot(turned_back, w_out[...], ((1,), (1,)))
        d_preact[span(t), :] = (d_hidden * slope).astype(BF)

    chain(0)

    @pl.loop(1, tiles)
    def _(t):
        for copy in load(t):
            copy.wait()
        leave(t - 1).start()
        contract(t - 1)
        mark_rows(t)
        chain(t)

    leave(tiles - 1).start()
    contract(tiles - 1)

    sums_ref[...] = sums[...].astype(BF)
    for part in range(2):
        grads[(part + 1) * width : (part + 2) * width, :] = dot(
            feat_tab[...], sums_ref[part * slots : (part + 1) * slots, :], ((0,), (0,))
        )
    gain = jnp.sum(gain_sum[...], axis=0, keepdims=True)
    core = core_ref[0]
    piece = 2 * width // chips
    body = piece * blocks
    for target, which in ((other_ref, 1 - core), (own_ref, core)):
        begin = pl.multiple_of(which * (2 * width), 2 * width)
        for j in range(blocks):
            target[:, j * piece : (j + 1) * piece, :] = (
                grads[pl.ds(begin, 2 * width), j * LANES : (j + 1) * LANES]
                .reshape(chips, piece, LANES)
                .astype(BF)
            )
        lines = [jnp.broadcast_to(gain[:, j * LANES : (j + 1) * LANES], (2, LANES)) for j in range(blocks)]
        target[:, body:, :] = jnp.broadcast_to(jnp.concatenate(lines, axis=0)[None].astype(BF), (chips, 8, LANES))
    for t in range(tiles):
        leave(t).wait()


def edge_pass(core, send_slot, recv_slot, gain, rows, w_input, w_output, pre, turned, cot, cap):
    edges, width = cot.shape
    tiles, _, tile = turned.shape
    devices = rows.shape[0] * LANES // (cap * 2 * width)
    slots = devices * cap
    chips = devices // CORES
    packets = jax.ShapeDtypeStruct((chips, 2 * width // chips * (width // LANES) + 8, LANES), BF)
    anywhere = pl.BlockSpec(memory_space=pl.ANY)
    return pl.pallas_call(
        functools.partial(edge_kernel, cap),
        in_specs=[smem()] + [VMEM] * 3 + [anywhere] * 6,
        out_specs=[anywhere] + [VMEM] * 3,
        out_shape=[
            jax.ShapeDtypeStruct(cot.shape, BF),
            packets,
            packets,
            jax.ShapeDtypeStruct((2 * slots, width), BF),
        ],
        scratch_shapes=[
            pltpu.VMEM(rows.shape, BF),
            pltpu.VMEM(rows.shape, F32),
            pltpu.VMEM((2, width, width), BF),
            pltpu.VMEM((width, width), BF),
            pltpu.VMEM(pre.shape, pre.dtype),
            pltpu.VMEM(turned.shape, BF),
            pltpu.VMEM(cot.shape, BF),
            pltpu.VMEM(cot.shape, BF),
            pltpu.VMEM((slots, width), BF),
            pltpu.VMEM((slots, width), BF),
            pltpu.VMEM((2 * slots, width), BF),
            pltpu.VMEM((tile, 2 * slots), BF),
            pltpu.VMEM((2 * slots, tile), BF),
            pltpu.VMEM((tile, width), BF),
            pltpu.VMEM((tile, width), BF),
            pltpu.VMEM((2 * slots, width), F32),
            pltpu.VMEM((4 * width, width), F32),
            pltpu.VMEM((8, width), F32),
            pltpu.SemaphoreType.DMA((3,)),
            pltpu.SemaphoreType.DMA((4, tiles)),
        ],
        compiler_params=pltpu.CompilerParams(vmem_limit_bytes=BIG_VMEM),
        cost_estimate=cost(16 * edges * width * width, 8 * cot.size),
        name="edge_pass",
    )(core, send_slot, recv_slot, gain, rows, w_input, w_output, pre, turned, cot)


def back_kernel(cap, core_ref, sums_ref, w_ref, own_ref, other_ref, tail):
    slots = sums_ref.shape[0] // 2
    width = sums_ref.shape[1]
    chips = slots // (cap * CORES)
    blocks = width // LANES
    nodes = dot(sums_ref[0:slots, :], w_ref[1], ((1,), (1,))) + dot(
        sums_ref[slots : 2 * slots, :], w_ref[2], ((1,), (1,))
    )
    core = core_ref[0]
    tail[...] = jnp.zeros_like(tail)
    for side in range(CORES):
        for k in range(cap):
            at = (side * cap + k) * chips
            for j in range(blocks):
                tail[side, pl.ds(core * (cap * blocks) + k * blocks + j, chips, stride=CORES * cap * blocks), :] = (
                    nodes[at : at + chips, j * LANES : (j + 1) * LANES]
                )
    own_ref[...] = tail[core].astype(BF).reshape(own_ref.shape)
    other_ref[...] = tail[1 - core].astype(BF).reshape(other_ref.shape)


def back_rows(core, sums, w_input, cap):
    slots, width = sums.shape[0] // 2, sums.shape[1]
    chips = slots // (cap * CORES)
    lines = CORES * cap * width // LANES
    return pl.pallas_call(
        functools.partial(back_kernel, cap),
        in_specs=[smem(), VMEM, VMEM],
        out_specs=[VMEM] * 2,
        out_shape=[jax.ShapeDtypeStruct((chips, lines, LANES), BF)] * 2,
        scratch_shapes=[pltpu.VMEM((CORES, chips * lines, LANES), F32)],
        compiler_params=pltpu.CompilerParams(vmem_limit_bytes=BIG_VMEM),
        cost_estimate=cost(2 * sums.size * width, 6 * sums.size),
        name="back_rows",
    )(core, sums, w_input)


def reduce_kernel(factor, in_ref, own_ref, got_ref, out_ref, gain_ref):
    total = jnp.sum(in_ref[...].astype(F32), axis=0) * factor
    body = total.shape[0] - 8
    out_ref[:, 0:body, :] = jnp.broadcast_to(total[0:body].astype(BF)[None], (in_ref.shape[0], body, LANES))
    out_ref[:, body:, :] = own_ref[...] + got_ref[...]
    gain_ref[...] = total[body:]


def reduce_packets(packets, own, got, factor):
    chips, lines, _ = packets.shape
    return pl.pallas_call(
        functools.partial(reduce_kernel, factor),
        out_shape=[
            jax.ShapeDtypeStruct((chips, lines - 8 + own.shape[1], LANES), BF),
            jax.ShapeDtypeStruct((8, LANES), F32),
        ],
        compiler_params=pltpu.CompilerParams(vmem_limit_bytes=BIG_VMEM),
        cost_estimate=cost(packets.size, 4 * packets.size),
        name="reduce_packets",
    )(packets, own, got)


def node_kernel(asked_ref, packets_ref, cots_ref, out_ref, ends, rows, hots):
    devices, cap = asked_ref.shape
    nodes, width = cots_ref.shape
    blocks = width // LANES
    body = packets_ref.shape[1] - CORES * cap * blocks
    ends[...] = packets_ref[:, body:, :].astype(F32).reshape(ends.shape)
    spot = lax.broadcasted_iota(jnp.int32, (devices, nodes), 1)
    for k in range(cap):
        at = k * devices
        hots[at : at + devices, :] = one_hot(asked_ref[:, k : k + 1], spot)
        for j in range(blocks):
            rows[at : at + devices, j * LANES : (j + 1) * LANES] = ends[
                pl.ds(k * blocks + j, devices, stride=cap * blocks), :
            ].astype(BF)
    sums = dot(hots[...], rows[...], ((0,), (0,)))
    out_ref[...] = (cots_ref[...].astype(F32) + sums).astype(BF)


def node_grads(asked, packets, cots):
    devices, cap = asked.shape
    nodes, width = cots.shape
    slots = devices * cap
    return pl.pallas_call(
        node_kernel,
        out_shape=jax.ShapeDtypeStruct(cots.shape, BF),
        scratch_shapes=[
            pltpu.VMEM((slots * width // LANES, LANES), F32),
            pltpu.VMEM((slots, width), BF),
            pltpu.VMEM((slots, nodes), BF),
        ],
        compiler_params=pltpu.CompilerParams(vmem_limit_bytes=BIG_VMEM),
        cost_estimate=cost(2 * slots * cots.size, 4 * cots.size + 2 * packets.size),
        name="node_grads",
    )(asked, packets, cots)


def unpack_kernel(is_mine, core_ref, packets_ref, *refs):
    input_ref, output_ref, values, sems = refs[-4:]
    width = output_ref.shape[1]
    blocks = width // LANES
    chips = packets_ref.shape[0]
    piece = 2 * width // chips
    half = core_ref[0] if is_mine else 1 - core_ref[0]

    def copy(upper, a):
        if not upper:
            target = input_ref.at[pl.ds(a * width, width)]
        else:
            target = output_ref if a else input_ref.at[pl.ds(2 * width, width)]
        return pltpu.make_async_copy(values.at[pl.ds(a * width, width)], target, sems.at[a])

    for a in range(2):
        chunk = slice(a * (chips // 2), (a + 1) * (chips // 2))
        for j in range(blocks):
            values[a * width : (a + 1) * width, j * LANES : (j + 1) * LANES] = (
                packets_ref[chunk, j * piece : (j + 1) * piece, :].astype(F32).reshape(width, LANES)
            )

        @pl.when(half == 0)
        def _():
            copy(False, a).start()

        @pl.when(half != 0)
        def _():
            copy(True, a).start()

    for a in range(2):

        @pl.when(half == 0)
        def _():
            copy(False, a).wait()

        @pl.when(half != 0)
        def _():
            copy(True, a).wait()


def unpack(is_mine, core, packets, width, earlier=()):
    anywhere = pl.BlockSpec(memory_space=pl.ANY)
    return pl.pallas_call(
        functools.partial(unpack_kernel, is_mine),
        in_specs=[smem(), VMEM] + [anywhere] * len(earlier),
        out_specs=[anywhere] * 2,
        out_shape=[
            jax.ShapeDtypeStruct((3 * width, width), F32),
            jax.ShapeDtypeStruct((width, width), F32),
        ],
        scratch_shapes=[pltpu.VMEM((2 * width, width), F32), pltpu.SemaphoreType.DMA((2,))],
        input_output_aliases={2 + a: a for a in range(len(earlier))},
        compiler_params=pltpu.CompilerParams(vmem_limit_bytes=BIG_VMEM),
        cost_estimate=cost(packets.size, 6 * packets.size),
        name="unpack_mine" if is_mine else "unpack_other",
    )(core, packets, *earlier)


def on_device(
    edge_feats,
    node_feats,
    edge_cot,
    node_cot,
    requests,
    send_slot,
    recv_slot,
    w_input,
    w_output,
    norm_gain,
):
    chips, cores = lax.axis_size("chip"), lax.axis_size("core")
    devices = chips * cores
    both = ("chip", "core")
    cap = requests.shape[1] // devices
    edges, width = edge_feats.shape
    core = lax.axis_index("core").astype(jnp.int32).reshape(1)
    pairs = [(d, d ^ 1) for d in range(devices)]

    asked = lax.all_to_all(
        requests.reshape(devices, 1, cap), both, split_axis=0, concat_axis=0, tiled=True
    ).reshape(devices, cap)
    picked = pick_rows(asked, node_feats, node_cot).reshape(devices, -1, LANES)
    rows = lax.all_to_all(picked, both, split_axis=0, concat_axis=0, tiled=True).reshape(-1, LANES)
    pre, turned = prep_pass(edge_feats, w_input, TILE)
    d_preact, own, other, sums = edge_pass(
        core,
        send_slot,
        recv_slot,
        norm_gain.reshape(1, width),
        rows,
        w_input,
        w_output,
        pre,
        turned,
        edge_cot,
        cap,
    )
    merged = own + lax.ppermute(other, both, pairs)
    packets = lax.all_to_all(merged, "chip", split_axis=0, concat_axis=0, tiled=True)
    back_own, back_other = back_rows(core, sums, w_input, cap)
    back_got = lax.ppermute(back_other, both, pairs)
    factor = float(edges * devices) ** (-0.5)
    pieces, gain = reduce_packets(packets, back_own, back_got, factor)
    d_preact, pieces = lax.optimization_barrier((d_preact, pieces))
    mine = lax.all_to_all(pieces, "chip", split_axis=0, concat_axis=0, tiled=True)
    grad_edges = grad_pass(d_preact, w_input, edge_cot, 1024)
    grad_edges, mine = lax.optimization_barrier((grad_edges, mine))
    partner = lax.ppermute(mine, both, pairs)
    grad_nodes = node_grads(asked, mine, node_cot)
    grads = unpack(True, core, mine, width)
    grad_input, grad_output = unpack(False, core, partner, width, grads)
    return (
        grad_edges,
        grad_nodes,
        grad_input.reshape(3, width, width),
        grad_output,
        gain[0:8:2].reshape(width),
    )


def solution(mesh):
    pairs = Mesh(mesh.devices.reshape(-1, CORES), ("chip", "core"))
    rows = P(("chip", "core"), None)
    return jax.shard_map(
        on_device,
        mesh=pairs,
        in_specs=(rows,) * 7 + (P(),) * 3,
        out_specs=(rows, rows, P(), P(), P()),
        check_vma=False,
    )
```

time: 151 us -> 134 us (0.89)
  blocking collectives: 71.3 us -> 20.7 us
  waiting for transfers between devices: 19.4 us -> 39.9 us
  starting transfers between devices: 9.19 us -> 20.4 us
  Pallas kernels: 46.2 us -> 40.8 us
  local copies, waits for them, and re-layouts: 3.11 us -> 8.29 us
    all_to_all x2 -> x0, blocking collectives: 50.1 us -> none  [the longest x1 27.9 us: on_device(): lax.all_to_all(merge(own, got), 'chip', split_axis=0, concat_axis=0, tile...]
    all_to_all x0 -> x2, waiting for transfers between devices: none -> 27.3 us  [the longest x1 13.7 us: on_device(): lax.all_to_all(merged, 'chip', split_axis=0, concat_axis=0, tiled=True)]
    all_to_all x0 -> x2, starting transfers between devices: none -> 10.3 us  [the longest x1 5.41 us: on_device(): lax.all_to_all(pieces, 'chip', split_axis=0, concat_axis=0, tiled=True)]
    all_to_all x1, waiting for transfers between devices: 16.5 us -> 8.7 us  [on_device(): lax.all_to_all(picked, both, split_axis=0, concat_axis=0, tiled=True)]
    unnamed x8 -> x26, local copies, waits for them, and re-layouts: 2.91 us -> 7.5 us
    pallas_call x5 -> x8, Pallas kernels: 43.5 us -> 39.2 us  [the longest x1 20.4 us: edge_pass(): pl.pallas_call(functools.partial(edge_kernel, cap), in_specs=[smem()] + [...]
    ppermute x1 -> x2, waiting for transfers between devices: 2.87 us -> 3.82 us  [the longest x1 2.47 us: on_device(): merged = own + lax.ppermute(other, both, pairs)]
  transfers between devices with their start and end apart: 3 -> 6, of which waited for: 2 -> 5; matrix products, arithmetic and copies ran while one was open for 0% -> 0% of each run, Pallas kernels for 2% -> 12%
where the time goes in v1:
time: 134 us; the launch traced here: 133 us
  Pallas kernels  40.8 us (30%)
  waiting for transfers between devices  39.9 us (30%)
  blocking collectives  20.7 us (15%)
  starting transfers between devices  20.4 us (15%)
  local copies, waits for them, and re-layouts  8.29 us (6%)
  other arithmetic  2.02 us (2%)
    all_to_all x1, blocking collectives, on_device(): lax.all_to_all(requests.reshape(devices, 1, cap), both, split_axis=0, con...  20.7 us
    pallas_call x1, Pallas kernels, edge_pass(): pl.pallas_call(functools.partial(edge_kernel, cap), in_specs=[smem()] + [...  20.4 us
    all_to_all x1, waiting for transfers between devices, on_device(): lax.all_to_all(merged, 'chip', split_axis=0, concat_axis=0, tiled=True)  13.7 us
    all_to_all x1, waiting for transfers between devices, on_device(): lax.all_to_all(pieces, 'chip', split_axis=0, concat_axis=0, tiled=True)  13.6 us
    all_to_all x1, waiting for transfers between devices, on_device(): lax.all_to_all(picked, both, split_axis=0, concat_axis=0, tiled=True)  8.7 us
    unnamed x26, local copies, waits for them, and re-layouts  7.5 us
    pallas_call x1, Pallas kernels, grad_pass(): pl.pallas_call(grad_kernel, grid=(edges // tile,), in_specs=[tiles, pl.Bl...  6.45 us
    pallas_call x1, Pallas kernels, prep_pass(): pl.pallas_call(prep_kernel, grid=(tiles,), in_specs=[rows, pl.BlockSpec((...  6.06 us
  transfers between devices with their start and end apart: 6, of which 5 were waited for; matrix products, arithmetic and copies ran while one was open for 0% of the time, Pallas kernels for 12%

profile of v1, /device:TPU:1, one launch (start us, length us, event | category | flops | bytes accessed | tf_op | source)
XLA Modules:
  0.0 133.0 jit_solution(584635322519274019)
XLA Ops:
  1.5 20.7 %all_to_all.20 = s32[128,1,3]{2,1,0:T(1,128)S(1)} all-to-all(s32[128,1,3]{2,1,0:T(1,128)S(1)} %bitcast.13), channel_id=1, replica_groups=mesh['chip'=64,'core'=2] {'chip','core'}, dimensions={0} | all-to-all | bytes 3072 | tf_op jit(solution)/shard_map/all_to_all | solution.py:528
  22.2 1.1 copy-done.1
  24.3 1.5 %pick_rows.1 = bf16[3072,128]{1,0:T(8,128)(2,1)} custom-call(s32[128,3]{1,0:T(8,128)S(1)} %bitcast.9, bf16[320,512]{1,0:T(8,128)(2,1)S(1)} %copy-done.7, bf16[320,512]{1,0:T(8,128)(2,1)S(1)} %copy-done.1), custom_call_target="tpu_custom_call" | custom-call | flops 251658240 | bytes 1572864 | tf_op jit(solution)/shard_map/pick_rows/pallas_call | solution.py:61
  25.8 4.8 %all-to-all-start.1 = ((bf16[128,24,128]{2,1,0:T(8,128)(2,1)}), bf16[128,24,128]{2,1,0:T(8,128)(2,1)S(1)}, u32[]{:S(2)}, u32[]{:S(2)}) async-start(bf16[128,24,128]{2,1,0:T(8,128)(2,1)} %bitcast.4), calls=%async_computation.1 | async-start | bytes 1572864 | tf_op jit(solution)/shard_map/all_to_all | solution.py:532
  30.6 6.1 %prep_pass.1 = (f32[3072,512]{1,0:T(8,128)}, bf16[4,512,768]{2,1,0:T(8,128)(2,1)S(1)}) custom-call(bf16[3072,512]{1,0:T(8,128)(2,1)} %feats_ref.3, bf16[3,512,512]{2,1,0:T(8,128)(2,1)S(1)} %copy-done), custom_call_target="tpu_custom_call" | custom-call | flops 1610612736 | bytes 12582912 | tf_op jit(solution)/shard_map/prep_pass/pallas_call | solution.py:90
  36.7 1.7 %copy-done.12 = bf16[4,512,768]{2,1,0:T(8,128)(2,1)} copy-done((bf16[4,512,768]{2,1,0:T(8,128)(2,1)}, bf16[4,512,768]{2,1,0:T(8,128)(2,1)S(1)}, u32[]{:S(2)}) %copy-start.12) | copy-done | bytes 3145752
  38.4 8.7 %all-to-all-done.1 = bf16[128,24,128]{2,1,0:T(8,128)(2,1)S(1)} async-done(((bf16[128,24,128]{2,1,0:T(8,128)(2,1)}), bf16[128,24,128]{2,1,0:T(8,128)(2,1)S(1)}, u32[]{:S(2)}, u32[]{:S(2)}) %all-to-all-start.1) | async-done | bytes 786464 | tf_op jit(solution)/shard_map/all_to_all | solution.py:532
  47.1 20.4 %edge_pass.1 = (bf16[3072,512]{1,0:T(8,128)(2,1)}, bf16[64,72,128]{2,1,0:T(8,128)(2,1)S(1)}, bf16[64,72,128]{2,1,0:T(8,128)(2,1)S(1)}, bf16[768,512]{1,0:T(8,128)(2,1)S(1)}) custom-call(s32[1]{0:T(128)} %bitcast.core_ref, s32[24,128]{1,0:T(8,128)S(1)} %copy-done.9, s32[24,128]{1,0:T(8,128)S(1)} %copy-done.10, f32[1,512]{1,0:T(1,128)S(1)} %bitcast.11, ...), custom_call_target="tpu_custom_call" | custom-call | flops 12884901888 | bytes 12582912 | tf_op jit(solution)/shard_map/edge_pass/pallas_call | solution.py:316
  68.3 1.2 collective-permute-start
  69.5 2.5 %collective-permute-done = bf16[64,72,128]{2,1,0:T(8,128)(2,1)S(1)} collective-permute-done((bf16[64,72,128]{2,1,0:T(8,128)(2,1)S(1)}, bf16[64,72,128]{2,1,0:T(8,128)(2,1)S(1)}, u32[]{:S(2)}, u32[]{:S(2)}) %collective-permute-start) | collective-permute-done | bytes 1179680 | tf_op jit(solution)/shard_map/ppermute | solution.py:547
  72.0 1.3 add.3
  73.3 4.8 %all-to-all-start.2 = ((bf16[64,72,128]{2,1,0:T(8,128)(2,1)}), bf16[64,72,128]{2,1,0:T(8,128)(2,1)S(1)}, u32[]{:S(2)}, u32[]{:S(2)}) async-start(bf16[64,72,128]{2,1,0:T(8,128)(2,1)} %add.3), calls=%async_computation.2 | async-start | bytes 2359296 | tf_op jit(solution)/shard_map/all_to_all | solution.py:548
  78.2 1.1 copy-done.4
  81.3 1.3 %collective-permute-done.1.got_ref = bf16[64,24,128]{2,1,0:T(8,128)(2,1)S(1)} collective-permute-done((bf16[64,24,128]{2,1,0:T(8,128)(2,1)S(1)}, bf16[64,24,128]{2,1,0:T(8,128)(2,1)S(1)}, u32[]{:S(2)}, u32[]{:S(2)}) %collective-permute-start.1) | collective-permute-done | bytes 393248 | tf_op jit(solution)/shard_map/ppermute | solution.py:550
  82.6 13.7 %all-to-all-done.2.in_ref = bf16[64,72,128]{2,1,0:T(8,128)(2,1)S(1)} async-done(((bf16[64,72,128]{2,1,0:T(8,128)(2,1)}), bf16[64,72,128]{2,1,0:T(8,128)(2,1)S(1)}, u32[]{:S(2)}, u32[]{:S(2)}) %all-to-all-start.2) | async-done | bytes 1179680 | tf_op jit(solution)/shard_map/all_to_all | solution.py:548
  96.3 1.0 copy-done.6
  97.3 1.4 %reduce_packets.1 = (bf16[64,88,128]{2,1,0:T(8,128)(2,1)}, f32[8,128]{1,0:T(8,128)S(1)}) custom-call(bf16[64,72,128]{2,1,0:T(8,128)(2,1)S(1)} %all-to-all-done.2.in_ref, bf16[64,24,128]{2,1,0:T(8,128)(2,1)S(1)} %copy-done.6, bf16[64,24,128]{2,1,0:T(8,128)(2,1)S(1)} %collective-permute-done.1.got_ref), custom_call_target="tpu_custom_call" | custom-call | flops 589824 | bytes 2359296 | tf_op jit(solution)/shard_map/reduce_packets/pallas_call | solution.py:401
  98.7 5.4 %all-to-all-start.3 = ((bf16[64,88,128]{2,1,0:T(8,128)(2,1)}), bf16[64,88,128]{2,1,0:T(8,128)(2,1)S(1)}, u32[]{:S(2)}, u32[]{:S(2)}) async-start(bf16[64,88,128]{2,1,0:T(8,128)(2,1)} %get-tuple-element.33), calls=%async_computation.3 | async-start | bytes 2883584 | tf_op jit(solution)/shard_map/all_to_all | solution.py:554
  104.2 6.5 %grad_pass.1 = bf16[3072,512]{1,0:T(8,128)(2,1)} custom-call(bf16[3072,512]{1,0:T(8,128)(2,1)} %get-tuple-element.32.d_preact_ref, bf16[3,512,512]{2,1,0:T(8,128)(2,1)} %w_ref.5, bf16[3072,512]{1,0:T(8,128)(2,1)} %cot_ref.1), custom_call_target="tpu_custom_call" | custom-call | flops 1610612736 | bytes 9437184 | tf_op jit(solution)/shard_map/grad_pass/pallas_call | solution.py:113
  110.6 13.6 %all-to-all-done.3.packets_ref = bf16[64,88,128]{2,1,0:T(8,128)(2,1)S(1)} async-done(((bf16[64,88,128]{2,1,0:T(8,128)(2,1)}), bf16[64,88,128]{2,1,0:T(8,128)(2,1)S(1)}, u32[]{:S(2)}, u32[]{:S(2)}) %all-to-all-start.3) | async-done | bytes 1441824 | tf_op jit(solution)/shard_map/all_to_all | solution.py:554
  124.2 3.7 %collective-permute-start.2 = (bf16[64,88,128]{2,1,0:T(8,128)(2,1)S(1)}, bf16[64,88,128]{2,1,0:T(8,128)(2,1)S(1)}, u32[]{:S(2)}, u32[]{:S(2)}) collective-permute-start(bf16[64,88,128]{2,1,0:T(8,128)(2,1)S(1)} %all-to-all-done.3.packets_ref), channel_id=1, source_target_pairs={{0,1},{1,0},{2,3},{3,2},{4,5},{5,4},{6,7},{7,6},{8,9},{9,8},{10,11... | collective-permute-start | bytes 4325384 | tf_op jit(solution)/shard_map/ppermute | solution.py:557
  128.6 1.5 %unpack_mine.1 = (f32[1536,512]{1,0:T(8,128)}, f32[512,512]{1,0:T(8,128)}) custom-call(s32[1]{0:T(128)} %bitcast.core_ref, bf16[64,88,128]{2,1,0:T(8,128)(2,1)S(1)} %all-to-all-done.3.packets_ref), custom_call_target="tpu_custom_call" | custom-call | flops 720896 | bytes 4325376 | tf_op jit(solution)/shard_map/unpack_mine/pallas_call | solution.py:492
  130.0 1.3 node_grads.1
  131.3 1.5 %unpack_other.1 = (f32[1536,512]{1,0:T(8,128)}, f32[512,512]{1,0:T(8,128)}) custom-call(s32[1]{0:T(128)} %bitcast.core_ref, bf16[64,88,128]{2,1,0:T(8,128)(2,1)S(1)} %collective-permute-done.2.packets_ref, f32[1536,512]{1,0:T(8,128)} %get-tuple-element.36.refs_0_, f32[512,512]{1,0:T(8,128)} %get-tuple-element.37.refs_1_), custom_call_target="tpu_custom_call", output_to_operand_aliasing={{0}: (2, {}), {1}: (3, {})} | custom-call | flops 720896 | bytes 4325376 | tf_op jit(solution)/shard_map/unpack_other/pallas_call | solution.py:492
  (28 shorter events, 5.3 us)
Async XLA Ops:
  22.2 8.4 %copy-start = (bf16[3,512,512]{2,1,0:T(8,128)(2,1)S(1)}, bf16[3,512,512]{2,1,0:T(8,128)(2,1)}, u32[]{:S(2)}) copy-start(bf16[3,512,512]{2,1,0:T(8,128)(2,1)} %w_ref.5) | copy-start | bytes 4718596
  22.2 1.1 copy-start.1
  23.3 1.0 copy-start.7
  25.8 21.3 %all-to-all-start.1 = ((bf16[128,24,128]{2,1,0:T(8,128)(2,1)}), bf16[128,24,128]{2,1,0:T(8,128)(2,1)S(1)}, u32[]{:S(2)}, u32[]{:S(2)}) async-start(bf16[128,24,128]{2,1,0:T(8,128)(2,1)} %bitcast.4), calls=%async_computation.1 | async-start | bytes 1572864 | tf_op jit(solution)/shard_map/all_to_all | solution.py:532
  30.6 16.5 %copy-start.8 = (bf16[512,512]{1,0:T(8,128)(2,1)S(1)}, bf16[512,512]{1,0:T(8,128)(2,1)}, u32[]{:S(2)}) copy-start(bf16[512,512]{1,0:T(8,128)(2,1)} %w_out_hbm.1) | copy-start | bytes 1572868
  30.6 16.5 %copy-start.9 = (s32[24,128]{1,0:T(8,128)S(1)}, s32[24,128]{1,0:T(8,128)}, u32[]{:S(2)}) copy-start(s32[24,128]{1,0:T(8,128)} %send_ref.1) | copy-start | bytes 36868
  30.6 16.5 %copy-start.10 = (s32[24,128]{1,0:T(8,128)S(1)}, s32[24,128]{1,0:T(8,128)}, u32[]{:S(2)}) copy-start(s32[24,128]{1,0:T(8,128)} %recv_ref.1) | copy-start | bytes 36868
  30.6 16.5 %copy-start.11 = (f32[512]{0:T(512)S(1)}, f32[512]{0:T(512)}, u32[]{:S(2)}) copy-start(f32[512]{0:T(512)} %param.19) | copy-start | bytes 6148
  36.7 1.7 %copy-start.12 = (bf16[4,512,768]{2,1,0:T(8,128)(2,1)}, bf16[4,512,768]{2,1,0:T(8,128)(2,1)S(1)}, u32[]{:S(2)}) copy-start(bf16[4,512,768]{2,1,0:T(8,128)(2,1)S(1)} %get-tuple-element.24.turned_hbm) | copy-start | bytes 9437188
  67.5 0.9 copy-start.3
  68.3 3.6 %collective-permute-start = (bf16[64,72,128]{2,1,0:T(8,128)(2,1)S(1)}, bf16[64,72,128]{2,1,0:T(8,128)(2,1)S(1)}, u32[]{:S(2)}, u32[]{:S(2)}) collective-permute-start(bf16[64,72,128]{2,1,0:T(8,128)(2,1)S(1)} %get-tuple-element.27), channel_id=1, source_target_pairs={{0,1},{1,0},{2,3},{3,2},{4,5},{5,4},{6,7},{7,6},{8,9},{9,8},{10,11... | collective-permute-start | bytes 3538952 | tf_op jit(solution)/shard_map/ppermute | solution.py:547
  73.3 23.0 %all-to-all-start.2 = ((bf16[64,72,128]{2,1,0:T(8,128)(2,1)}), bf16[64,72,128]{2,1,0:T(8,128)(2,1)S(1)}, u32[]{:S(2)}, u32[]{:S(2)}) async-start(bf16[64,72,128]{2,1,0:T(8,128)(2,1)} %add.3), calls=%async_computation.2 | async-start | bytes 2359296 | tf_op jit(solution)/shard_map/all_to_all | solution.py:548
  78.1 1.1 copy-start.4
  80.0 0.7 copy-start.5
  80.7 1.9 %collective-permute-start.1 = (bf16[64,24,128]{2,1,0:T(8,128)(2,1)S(1)}, bf16[64,24,128]{2,1,0:T(8,128)(2,1)S(1)}, u32[]{:S(2)}, u32[]{:S(2)}) collective-permute-start(bf16[64,24,128]{2,1,0:T(8,128)(2,1)S(1)} %get-tuple-element.30), channel_id=1, source_target_pairs={{0,1},{1,0},{2,3},{3,2},{4,5},{5,4},{6,7},{7,6},{8,9},{9,8},{10,11... | collective-permute-start | bytes 1179656 | tf_op jit(solution)/shard_map/ppermute | solution.py:550
  96.3 1.0 copy-start.6
  98.7 25.5 %all-to-all-start.3 = ((bf16[64,88,128]{2,1,0:T(8,128)(2,1)}), bf16[64,88,128]{2,1,0:T(8,128)(2,1)S(1)}, u32[]{:S(2)}, u32[]{:S(2)}) async-start(bf16[64,88,128]{2,1,0:T(8,128)(2,1)} %get-tuple-element.33), calls=%async_computation.3 | async-start | bytes 2883584 | tf_op jit(solution)/shard_map/all_to_all | solution.py:554
  110.6 19.4 %copy-start.2 = (bf16[320,512]{1,0:T(8,128)(2,1)S(1)}, bf16[320,512]{1,0:T(8,128)(2,1)}, u32[]{:S(2)}) copy-start(bf16[320,512]{1,0:T(8,128)(2,1)} %cots_ref.3) | copy-start | bytes 983044
  124.2 7.1 %collective-permute-start.2 = (bf16[64,88,128]{2,1,0:T(8,128)(2,1)S(1)}, bf16[64,88,128]{2,1,0:T(8,128)(2,1)S(1)}, u32[]{:S(2)}, u32[]{:S(2)}) collective-permute-start(bf16[64,88,128]{2,1,0:T(8,128)(2,1)S(1)} %all-to-all-done.3.packets_ref), channel_id=1, source_target_pairs={{0,1},{1,0},{2,3},{3,2},{4,5},{5,4},{6,7},{7,6},{8,9},{9,8},{10,11... | collective-permute-start | bytes 4325384 | tf_op jit(solution)/shard_map/ppermute | solution.py:557

commit v2 on v1

--- a/solution.py
+++ b/solution.py
@@ -14,59 +14,66 @@
 TILE = 768
 PRE = F32
 BIG_VMEM = 48 * 1024 * 1024
+
 VMEM = pl.BlockSpec(memory_space=pltpu.VMEM)
-
+ANYWHERE = pl.BlockSpec(memory_space=pl.ANY)
 
 def dot(left, right, over=((1,), (0,))):
     return lax.dot_general(left, right, (over, ((), ())), preferred_element_type=F32)
 
-
 def whole(shape):
     return pl.BlockSpec(shape, lambda *_: (0,) * len(shape))
 
-
 def smem():
     return pl.BlockSpec(memory_space=pltpu.SMEM)
 
-
 def cost(flops, moved):
     return pl.CostEstimate(flops=flops, bytes_accessed=moved, transcendentals=0)
 
-
 def one_hot(left, right):
     return jnp.where(left == right, 1.0, 0.0).astype(BF)
 
-
-def pick_kernel(asked_ref, feats_ref, cots_ref, out_ref, rows):
+def pick_kernel(asked_ref, feats_hbm, cots_hbm, out_ref, feats, cots, rows, sems):
     devices, cap = asked_ref.shape
-    nodes, width = feats_ref.shape
+    nodes, width = feats.shape
     blocks = width // LANES
     per = cap * 2 * blocks
+    copies = [
+        pltpu.make_async_copy(feats_hbm, feats, sems.at[0]),
+        pltpu.make_async_copy(cots_hbm, cots, sems.at[1]),
+    ]
+    for copy in copies:
+        copy.start()
     spot = lax.broadcasted_iota(jnp.int32, (devices, nodes), 1)
-    for k in range(cap):
-        hot = one_hot(asked_ref[:, k : k + 1], spot)
-        for at, table in enumerate((feats_ref, cots_ref)):
-            found = dot(hot, table[...])
+    hots = [one_hot(asked_ref[:, k : k + 1], spot) for k in range(cap)]
+    for at, table in enumerate((feats, cots)):
+        copies[at].wait()
+        for k in range(cap):
+            found = dot(hots[k], table[...])
             for j in range(blocks):
                 rows[pl.ds(k * 2 * blocks + at * blocks + j, devices, stride=per), :] = found[
                     :, j * LANES : (j + 1) * LANES
                 ]
     out_ref[...] = rows[...].astype(BF)
 
-
 def pick_rows(asked, feats, cots):
     devices, cap = asked.shape
     width = feats.shape[1]
     total = devices * cap * 2 * width // LANES
     return pl.pallas_call(
         pick_kernel,
+        in_specs=[VMEM, ANYWHERE, ANYWHERE],
         out_shape=jax.ShapeDtypeStruct((total, LANES), BF),
-        scratch_shapes=[pltpu.VMEM((total, LANES), F32)],
+        scratch_shapes=[
+            pltpu.VMEM(feats.shape, BF),
+            pltpu.VMEM(cots.shape, BF),
+            pltpu.VMEM((total, LANES), F32),
+            pltpu.SemaphoreType.DMA((2,)),
+        ],
         compiler_params=pltpu.CompilerParams(vmem_limit_bytes=BIG_VMEM),
         cost_estimate=cost(4 * devices * cap * feats.size, 4 * total * LANES),
         name="pick_rows",
     )(asked, feats, cots)
-
 
 def slot_ids(position, chips, cap):
     half = cap * chips
@@ -76,12 +83,10 @@
     chip = rest - k * chips
     return chip * (CORES * cap) + core * cap + k
 
-
 def prep_kernel(feats_ref, w_ref, pre_ref, turned_ref):
     feats = feats_ref[...]
     pre_ref[...] = dot(feats, w_ref[0]).astype(PRE)
     turned_ref[0] = feats.T
-
 
 def prep_pass(feats, w_input, tile):
     edges, width = feats.shape
@@ -101,11 +106,9 @@
         name="prep_pass",
     )(feats, w_input)
 
-
 def grad_kernel(d_preact_ref, w_ref, cot_ref, out_ref):
     grad = dot(d_preact_ref[...], w_ref[0], ((1,), (1,)))
     out_ref[...] = (cot_ref[...].astype(F32) + grad).astype(BF)
-
 
 def grad_pass(d_preact, w_input, cot, tile):
     edges, width = cot.shape
@@ -119,7 +122,6 @@
         cost_estimate=cost(2 * edges * width * width, 6 * cot.size),
         name="grad_pass",
     )(d_preact, w_input, cot)
-
 
 def edge_kernel(
     cap,
@@ -136,29 +138,29 @@
     d_preact_hbm,
     own_ref,
     other_ref,
-    sums_ref,
+    sums_hbm,
     rows16,
     rows32,
     w_in,
     w_out,
     pre,
-    turned,
+    left,
     cot,
     d_preact,
     feat_tab,
     cot_tab,
     pre_tab,
     hot_rows,
-    hot_cols,
     hidden,
     d_mixed,
     sums,
+    sums16,
     grads,
     gain_sum,
     once,
     per_tile,
 ):
-    tiles, _, tile = turned.shape
+    tiles, _, tile = turned_hbm.shape
     slots, width = feat_tab.shape
     chips = slots // (cap * CORES)
     blocks = width // LANES
@@ -166,7 +168,7 @@
     groups = tile // LANES
 
     def span(t):
-        return pl.ds(pl.multiple_of(t * tile, tile), tile)
+        return pl.ds(t * tile, tile)
 
     first = (
         pltpu.make_async_copy(rows_hbm, rows16, once.at[0]),
@@ -178,7 +180,7 @@
         return (
             pltpu.make_async_copy(pre_hbm.at[span(t)], pre.at[span(t)], per_tile.at[0, t]),
             pltpu.make_async_copy(cot_hbm.at[span(t)], cot.at[span(t)], per_tile.at[1, t]),
-            pltpu.make_async_copy(turned_hbm.at[t], turned.at[t], per_tile.at[2, t]),
+            pltpu.make_async_copy(turned_hbm.at[t], left.at[t, pl.ds(2 * slots, width)], per_tile.at[2, t]),
         )
 
     def leave(t):
@@ -197,22 +199,20 @@
             for at, ref in enumerate((send_ref, recv_ref)):
                 upright = jnp.broadcast_to(ref[pl.ds(t * groups + g, 1), :], (LANES, LANES)).T
                 for b in range(slots // LANES):
-                    hot_rows[g * LANES : (g + 1) * LANES, at * slots + b * LANES : at * slots + (b + 1) * LANES] = (
+                    hot_rows[t % 2, g * LANES : (g + 1) * LANES, at * slots + b * LANES : at * slots + (b + 1) * LANES] = (
                         one_hot(upright, lane_ids[:, b * LANES : (b + 1) * LANES])
                     )
 
     def mark_cols(t):
         for g in range(groups):
             for at, ref in enumerate((send_ref, recv_ref)):
-                hot_cols[at * slots : (at + 1) * slots, g * LANES : (g + 1) * LANES] = one_hot(
+                left[t, at * slots : (at + 1) * slots, g * LANES : (g + 1) * LANES] = one_hot(
                     row_ids, ref[pl.ds(t * groups + g, 1), :]
                 )
 
     sums[...] = jnp.zeros_like(sums)
-    grads[0:width, :] = jnp.zeros((width, width), F32)
     grads[3 * width : 4 * width, :] = jnp.zeros((width, width), F32)
     gain_sum[...] = jnp.zeros_like(gain_sum)
-    mark_rows(0)
     first[0].wait()
     rows32[...] = rows16[...].astype(F32)
     for core in range(CORES):
@@ -235,25 +235,34 @@
     for copy in load(0):
         copy.wait()
 
-    def contract(t):
+    def gather(t):
+        mark_rows(t)
+        return pre[span(t), :].astype(F32) + dot(hot_rows[t % 2], pre_tab[...])
+
+    def contract_output(t):
+        grads[3 * width : 4 * width, :] += dot(hidden[t % 2], d_mixed[t % 2], ((0,), (0,)))
+
+    def contract_input(t):
         mark_cols(t)
-        arrived = d_preact[span(t), :]
-        sums[...] += dot(hot_cols[...], arrived)
-        grads[0:width, :] += dot(turned[t], arrived)
-        grads[3 * width : 4 * width, :] += dot(hidden[...], d_mixed[...], ((0,), (0,)))
-
-    def chain(t):
-        preact = pre[span(t), :].astype(F32) + dot(hot_rows[...], pre_tab[...])
+        sums[...] += dot(left[t], d_preact[span(t), :])
+
+    preact = gather(0)
+    for t in range(tiles):
+        if t:
+            contract_output(t - 1)
         logistic = 0.5 * jnp.tanh(0.5 * preact) + 0.5
         silu = preact * logistic
         rounded = silu.astype(BF)
-        hidden[...] = rounded
+        hidden[t % 2] = rounded
         slope = logistic + silu * (1.0 - logistic)
         mixed = dot(rounded, w_out[...])
+        found = dot(hot_rows[t % 2, :, slots:], cot_tab[...])
+        if t:
+            contract_input(t - 1)
         center = mixed - jnp.mean(mixed, axis=1, keepdims=True)
         inverse = lax.rsqrt(jnp.mean(center * center, axis=1, keepdims=True) + 1e-5)
         normed = center * inverse
-        upstream = cot[span(t), :].astype(F32) + dot(hot_rows[:, slots:], cot_tab[...])
+        upstream = cot[span(t), :].astype(F32) + found
         scaled = upstream * gain_ref[...]
         turned_back = (
             inverse
@@ -264,28 +273,24 @@
             )
         ).astype(BF)
         gain_sum[...] += jnp.sum((upstream * normed).reshape(tile // 8, 8, width), axis=0)
-        d_mixed[...] = turned_back
+        d_mixed[t % 2] = turned_back
         d_hidden = dot(turned_back, w_out[...], ((1,), (1,)))
+        if t + 1 < tiles:
+            for copy in load(t + 1):
+                copy.wait()
+            preact = gather(t + 1)
         d_preact[span(t), :] = (d_hidden * slope).astype(BF)
-
-    chain(0)
-
-    @pl.loop(1, tiles)
-    def _(t):
-        for copy in load(t):
-            copy.wait()
-        leave(t - 1).start()
-        contract(t - 1)
-        mark_rows(t)
-        chain(t)
-
-    leave(tiles - 1).start()
-    contract(tiles - 1)
-
-    sums_ref[...] = sums[...].astype(BF)
+        leave(t).start()
+    contract_output(tiles - 1)
+    contract_input(tiles - 1)
+
+    sums16[...] = sums[0 : 2 * slots, :].astype(BF)
+    summed = pltpu.make_async_copy(sums16, sums_hbm, once.at[3])
+    summed.start()
+    grads[0:width, :] = sums[2 * slots :, :]
     for part in range(2):
         grads[(part + 1) * width : (part + 2) * width, :] = dot(
-            feat_tab[...], sums_ref[part * slots : (part + 1) * slots, :], ((0,), (0,))
+            feat_tab[...], sums16[part * slots : (part + 1) * slots, :], ((0,), (0,))
         )
     gain = jnp.sum(gain_sum[...], axis=0, keepdims=True)
     core = core_ref[0]
@@ -301,9 +306,9 @@
             )
         lines = [jnp.broadcast_to(gain[:, j * LANES : (j + 1) * LANES], (2, LANES)) for j in range(blocks)]
         target[:, body:, :] = jnp.broadcast_to(jnp.concatenate(lines, axis=0)[None].astype(BF), (chips, 8, LANES))
+    summed.wait()
     for t in range(tiles):
         leave(t).wait()
-
 
 def edge_pass(core, send_slot, recv_slot, gain, rows, w_input, w_output, pre, turned, cot, cap):
     edges, width = cot.shape
@@ -312,11 +317,10 @@
     slots = devices * cap
     chips = devices // CORES
     packets = jax.ShapeDtypeStruct((chips, 2 * width // chips * (width // LANES) + 8, LANES), BF)
-    anywhere = pl.BlockSpec(memory_space=pl.ANY)
     return pl.pallas_call(
         functools.partial(edge_kernel, cap),
-        in_specs=[smem()] + [VMEM] * 3 + [anywhere] * 6,
-        out_specs=[anywhere] + [VMEM] * 3,
+        in_specs=[smem()] + [VMEM] * 3 + [ANYWHERE] * 6,
+        out_specs=[ANYWHERE, VMEM, VMEM, ANYWHERE],
         out_shape=[
             jax.ShapeDtypeStruct(cot.shape, BF),
             packets,
@@ -329,20 +333,20 @@
             pltpu.VMEM((2, width, width), BF),
             pltpu.VMEM((width, width), BF),
             pltpu.VMEM(pre.shape, pre.dtype),
-            pltpu.VMEM(turned.shape, BF),
+            pltpu.VMEM((tiles, 2 * slots + width, tile), BF),
             pltpu.VMEM(cot.shape, BF),
             pltpu.VMEM(cot.shape, BF),
             pltpu.VMEM((slots, width), BF),
             pltpu.VMEM((slots, width), BF),
             pltpu.VMEM((2 * slots, width), BF),
-            pltpu.VMEM((tile, 2 * slots), BF),
-            pltpu.VMEM((2 * slots, tile), BF),
-            pltpu.VMEM((tile, width), BF),
-            pltpu.VMEM((tile, width), BF),
-            pltpu.VMEM((2 * slots, width), F32),
+            pltpu.VMEM((2, tile, 2 * slots), BF),
+            pltpu.VMEM((2, tile, width), BF),
+            pltpu.VMEM((2, tile, width), BF),
+            pltpu.VMEM((2 * slots + width, width), F32),
+            pltpu.VMEM((2 * slots, width), BF),
             pltpu.VMEM((4 * width, width), F32),
             pltpu.VMEM((8, width), F32),
-            pltpu.SemaphoreType.DMA((3,)),
+            pltpu.SemaphoreType.DMA((4,)),
             pltpu.SemaphoreType.DMA((4, tiles)),
         ],
         compiler_params=pltpu.CompilerParams(vmem_limit_bytes=BIG_VMEM),
@@ -350,8 +354,7 @@
         name="edge_pass",
     )(core, send_slot, recv_slot, gain, rows, w_input, w_output, pre, turned, cot)
 
-
-def back_kernel(cap, core_ref, sums_ref, w_ref, own_ref, other_ref, tail):
+def back_kernel(cap, core_ref, sums_ref, w_ref, own_hbm, other_ref, tail, own, sem):
     slots = sums_ref.shape[0] // 2
     width = sums_ref.shape[1]
     chips = slots // (cap * CORES)
@@ -368,9 +371,11 @@
                 tail[side, pl.ds(core * (cap * blocks) + k * blocks + j, chips, stride=CORES * cap * blocks), :] = (
                     nodes[at : at + chips, j * LANES : (j + 1) * LANES]
                 )
-    own_ref[...] = tail[core].astype(BF).reshape(own_ref.shape)
+    own[...] = tail[core].astype(BF).reshape(own.shape)
+    copy = pltpu.make_async_copy(own, own_hbm, sem)
+    copy.start()
     other_ref[...] = tail[1 - core].astype(BF).reshape(other_ref.shape)
-
+    copy.wait()
 
 def back_rows(core, sums, w_input, cap):
     slots, width = sums.shape[0] // 2, sums.shape[1]
@@ -379,22 +384,27 @@
     return pl.pallas_call(
         functools.partial(back_kernel, cap),
         in_specs=[smem(), VMEM, VMEM],
-        out_specs=[VMEM] * 2,
+        out_specs=[ANYWHERE, VMEM],
         out_shape=[jax.ShapeDtypeStruct((chips, lines, LANES), BF)] * 2,
-        scratch_shapes=[pltpu.VMEM((CORES, chips * lines, LANES), F32)],
+        scratch_shapes=[
+            pltpu.VMEM((CORES, chips * lines, LANES), F32),
+            pltpu.VMEM((chips, lines, LANES), BF),
+            pltpu.SemaphoreType.DMA,
+        ],
         compiler_params=pltpu.CompilerParams(vmem_limit_bytes=BIG_VMEM),
         cost_estimate=cost(2 * sums.size * width, 6 * sums.size),
         name="back_rows",
     )(core, sums, w_input)
 
-
-def reduce_kernel(factor, in_ref, own_ref, got_ref, out_ref, gain_ref):
+def reduce_kernel(factor, in_ref, own_hbm, got_ref, out_ref, gain_ref, own, sem):
+    copy = pltpu.make_async_copy(own_hbm, own, sem)
+    copy.start()
     total = jnp.sum(in_ref[...].astype(F32), axis=0) * factor
     body = total.shape[0] - 8
     out_ref[:, 0:body, :] = jnp.broadcast_to(total[0:body].astype(BF)[None], (in_ref.shape[0], body, LANES))
-    out_ref[:, body:, :] = own_ref[...] + got_ref[...]
-    gain_ref[...] = total[body:]
-
+    gain_ref[...] = jnp.concatenate([total[body + 2 * j : body + 2 * j + 1] for j in range(4)], axis=1)
+    copy.wait()
+    out_ref[:, body:, :] = own[...] + got_ref[...]
 
 def reduce_packets(packets, own, got, factor):
     chips, lines, _ = packets.shape
@@ -402,13 +412,14 @@
         functools.partial(reduce_kernel, factor),
         out_shape=[
             jax.ShapeDtypeStruct((chips, lines - 8 + own.shape[1], LANES), BF),
-            jax.ShapeDtypeStruct((8, LANES), F32),
-        ],
+            jax.ShapeDtypeStruct((1, 4 * LANES), F32),
+        ],
+        in_specs=[VMEM, ANYWHERE, VMEM],
+        scratch_shapes=[pltpu.VMEM(own.shape, BF), pltpu.SemaphoreType.DMA],
         compiler_params=pltpu.CompilerParams(vmem_limit_bytes=BIG_VMEM),
         cost_estimate=cost(packets.size, 4 * packets.size),
         name="reduce_packets",
     )(packets, own, got)
-
 
 def node_kernel(asked_ref, packets_ref, cots_ref, out_ref, ends, rows, hots):
     devices, cap = asked_ref.shape
@@ -427,7 +438,6 @@
     sums = dot(hots[...], rows[...], ((0,), (0,)))
     out_ref[...] = (cots_ref[...].astype(F32) + sums).astype(BF)
 
-
 def node_grads(asked, packets, cots):
     devices, cap = asked.shape
     nodes, width = cots.shape
@@ -444,7 +454,6 @@
         cost_estimate=cost(2 * slots * cots.size, 4 * cots.size + 2 * packets.size),
         name="node_grads",
     )(asked, packets, cots)
-
 
 def unpack_kernel(is_mine, core_ref, packets_ref, *refs):
     input_ref, output_ref, values, sems = refs[-4:]
@@ -486,13 +495,11 @@
         def _():
             copy(True, a).wait()
 
-
 def unpack(is_mine, core, packets, width, earlier=()):
-    anywhere = pl.BlockSpec(memory_space=pl.ANY)
     return pl.pallas_call(
         functools.partial(unpack_kernel, is_mine),
-        in_specs=[smem(), VMEM] + [anywhere] * len(earlier),
-        out_specs=[anywhere] * 2,
+        in_specs=[smem(), VMEM] + [ANYWHERE] * len(earlier),
+        out_specs=[ANYWHERE] * 2,
         out_shape=[
             jax.ShapeDtypeStruct((3 * width, width), F32),
             jax.ShapeDtypeStruct((width, width), F32),
@@ -503,7 +510,6 @@
         cost_estimate=cost(packets.size, 6 * packets.size),
         name="unpack_mine" if is_mine else "unpack_other",
     )(core, packets, *earlier)
-
 
 def on_device(
     edge_feats,
@@ -563,9 +569,8 @@
         grad_nodes,
         grad_input.reshape(3, width, width),
         grad_output,
-        gain[0:8:2].reshape(width),
+        gain.reshape(width),
     )
-
 
 def solution(mesh):
     pairs = Mesh(mesh.devices.reshape(-1, CORES), ("chip", "core"))

time: 134 us -> 133 us (level)
  local copies, waits for them, and re-layouts: 8.29 us -> 5.96 us
    unnamed x26 -> x22, local copies, waits for them, and re-layouts: 7.5 us -> 5.76 us
  transfers between devices with their start and end apart: 6 -> 6, of which waited for: 5 -> 6; matrix products, arithmetic and copies ran while one was open for 0% -> 0% of each run, Pallas kernels for 12% -> 12%
where the time goes in v2:
time: 133 us; the launch traced here: 132 us
  Pallas kernels  41.8 us (31%)
  waiting for transfers between devices  40.4 us (30%)
  blocking collectives  20.7 us (16%)
  starting transfers between devices  20.5 us (15%)
  local copies, waits for them, and re-layouts  5.96 us (4%)
  other arithmetic  2.02 us (2%)
    all_to_all x1, blocking collectives, on_device(): lax.all_to_all(requests.reshape(devices, 1, cap), both, split_axis=0, con...  20.7 us
    pallas_call x1, Pallas kernels, edge_pass(): pl.pallas_call(functools.partial(edge_kernel, cap), in_specs=[smem()] + [...  20.5 us
    all_to_all x1, waiting for transfers between devices, on_device(): lax.all_to_all(merged, 'chip', split_axis=0, concat_axis=0, tiled=True)  14.4 us
    all_to_all x1, waiting for transfers between devices, on_device(): lax.all_to_all(pieces, 'chip', split_axis=0, concat_axis=0, tiled=True)  13.4 us
    all_to_all x1, waiting for transfers between devices, on_device(): lax.all_to_all(picked, both, split_axis=0, concat_axis=0, tiled=True)  8.72 us
    pallas_call x1, Pallas kernels, grad_pass(): pl.pallas_call(grad_kernel, grid=(edges // tile,), in_specs=[tiles, pl.Bl...  6.45 us
    pallas_call x1, Pallas kernels, prep_pass(): pl.pallas_call(prep_kernel, grid=(tiles,), in_specs=[rows, pl.BlockSpec((...  6.05 us
    unnamed x22, local copies, waits for them, and re-layouts  5.76 us
  transfers between devices with their start and end apart: 6, of which 6 were waited for; matrix products, arithmetic and copies ran while one was open for 0% of the time, Pallas kernels for 12%

profile of v2, /device:TPU:1, one launch (start us, length us, event | category | flops | bytes accessed | tf_op | source)
XLA Modules:
  0.0 132.3 jit_solution(4228393011622779086)
XLA Ops:
  1.5 20.7 %all_to_all.20 = s32[128,1,3]{2,1,0:T(1,128)S(1)} all-to-all(s32[128,1,3]{2,1,0:T(1,128)S(1)} %bitcast.13), channel_id=1, replica_groups=mesh['chip'=64,'core'=2] {'chip','core'}, dimensions={0} | all-to-all | bytes 3072 | tf_op jit(solution)/shard_map/all_to_all | solution.py:534
  22.2 1.1 copy-done.1
  23.3 1.0 copy-done.5
  24.3 2.0 %pick_rows.1 = bf16[3072,128]{1,0:T(8,128)(2,1)} custom-call(s32[128,3]{1,0:T(8,128)S(1)} %bitcast.9, bf16[320,512]{1,0:T(8,128)(2,1)S(1)} %copy-done.5, bf16[320,512]{1,0:T(8,128)(2,1)S(1)} %copy-done.1), custom_call_target="tpu_custom_call" | custom-call | flops 251658240 | bytes 1572864 | tf_op jit(solution)/shard_map/pick_rows/pallas_call | solution.py:63
  26.3 4.8 %all-to-all-start.1 = ((bf16[128,24,128]{2,1,0:T(8,128)(2,1)}), bf16[128,24,128]{2,1,0:T(8,128)(2,1)S(1)}, u32[]{:S(2)}, u32[]{:S(2)}) async-start(bf16[128,24,128]{2,1,0:T(8,128)(2,1)} %bitcast.4), calls=%async_computation.1 | async-start | bytes 1572864 | tf_op jit(solution)/shard_map/all_to_all | solution.py:538
  31.1 6.1 %prep_pass.1 = (f32[3072,512]{1,0:T(8,128)}, bf16[4,512,768]{2,1,0:T(8,128)(2,1)S(1)}) custom-call(bf16[3072,512]{1,0:T(8,128)(2,1)} %feats_ref.1, bf16[3,512,512]{2,1,0:T(8,128)(2,1)S(1)} %copy-done), custom_call_target="tpu_custom_call" | custom-call | flops 1610612736 | bytes 12582912 | tf_op jit(solution)/shard_map/prep_pass/pallas_call | solution.py:95
  37.2 1.7 %copy-done.10 = bf16[4,512,768]{2,1,0:T(8,128)(2,1)} copy-done((bf16[4,512,768]{2,1,0:T(8,128)(2,1)}, bf16[4,512,768]{2,1,0:T(8,128)(2,1)S(1)}, u32[]{:S(2)}) %copy-start.10) | copy-done | bytes 3145752
  38.8 8.7 %all-to-all-done.1 = bf16[128,24,128]{2,1,0:T(8,128)(2,1)S(1)} async-done(((bf16[128,24,128]{2,1,0:T(8,128)(2,1)}), bf16[128,24,128]{2,1,0:T(8,128)(2,1)S(1)}, u32[]{:S(2)}, u32[]{:S(2)}) %all-to-all-start.1) | async-done | bytes 786464 | tf_op jit(solution)/shard_map/all_to_all | solution.py:538
  47.6 20.5 %edge_pass.1 = (bf16[3072,512]{1,0:T(8,128)(2,1)}, bf16[64,72,128]{2,1,0:T(8,128)(2,1)S(1)}, bf16[64,72,128]{2,1,0:T(8,128)(2,1)S(1)}, bf16[768,512]{1,0:T(8,128)(2,1)S(1)}) custom-call(s32[1]{0:T(128)} %bitcast.core_ref, s32[24,128]{1,0:T(8,128)S(1)} %copy-done.7, s32[24,128]{1,0:T(8,128)S(1)} %copy-done.8, f32[1,512]{1,0:T(1,128)S(1)} %bitcast.11, ...), custom_call_target="tpu_custom_call" | custom-call | flops 12884901888 | bytes 12582912 | tf_op jit(solution)/shard_map/edge_pass/pallas_call | solution.py:320
  69.0 1.2 collective-permute-start
  70.2 2.5 %collective-permute-done = bf16[64,72,128]{2,1,0:T(8,128)(2,1)S(1)} collective-permute-done((bf16[64,72,128]{2,1,0:T(8,128)(2,1)S(1)}, bf16[64,72,128]{2,1,0:T(8,128)(2,1)S(1)}, u32[]{:S(2)}, u32[]{:S(2)}) %collective-permute-start) | collective-permute-done | bytes 1179680 | tf_op jit(solution)/shard_map/ppermute | solution.py:553
  72.7 1.3 add.3
  74.0 4.7 %all-to-all-start.2 = ((bf16[64,72,128]{2,1,0:T(8,128)(2,1)}), bf16[64,72,128]{2,1,0:T(8,128)(2,1)S(1)}, u32[]{:S(2)}, u32[]{:S(2)}) async-start(bf16[64,72,128]{2,1,0:T(8,128)(2,1)} %add.3), calls=%async_computation.2 | async-start | bytes 2359296 | tf_op jit(solution)/shard_map/all_to_all | solution.py:554
  78.7 1.1 copy-done.4
  81.3 1.3 %collective-permute-done.1.got_ref = bf16[64,24,128]{2,1,0:T(8,128)(2,1)S(1)} collective-permute-done((bf16[64,24,128]{2,1,0:T(8,128)(2,1)S(1)}, bf16[64,24,128]{2,1,0:T(8,128)(2,1)S(1)}, u32[]{:S(2)}, u32[]{:S(2)}) %collective-permute-start.1) | collective-permute-done | bytes 393248 | tf_op jit(solution)/shard_map/ppermute | solution.py:556
  82.7 14.4 %all-to-all-done.2.in_ref = bf16[64,72,128]{2,1,0:T(8,128)(2,1)S(1)} async-done(((bf16[64,72,128]{2,1,0:T(8,128)(2,1)}), bf16[64,72,128]{2,1,0:T(8,128)(2,1)S(1)}, u32[]{:S(2)}, u32[]{:S(2)}) %all-to-all-start.2) | async-done | bytes 1179680 | tf_op jit(solution)/shard_map/all_to_all | solution.py:554
  97.0 1.6 %reduce_packets.1 = (bf16[64,88,128]{2,1,0:T(8,128)(2,1)}, f32[1,512]{1,0:T(1,128)}) custom-call(bf16[64,72,128]{2,1,0:T(8,128)(2,1)S(1)} %all-to-all-done.2.in_ref, bf16[64,24,128]{2,1,0:T(8,128)(2,1)S(1)} %get-tuple-element.29.own_hbm, bf16[64,24,128]{2,1,0:T(8,128)(2,1)S(1)} %collective-permute-done.1.got_ref), custom_call_target="tpu_custom_call" | custom-call | flops 589824 | bytes 2359296 | tf_op jit(solution)/shard_map/reduce_packets/pallas_call | solution.py:411
  98.7 5.3 %all-to-all-start.3 = ((bf16[64,88,128]{2,1,0:T(8,128)(2,1)}), bf16[64,88,128]{2,1,0:T(8,128)(2,1)S(1)}, u32[]{:S(2)}, u32[]{:S(2)}) async-start(bf16[64,88,128]{2,1,0:T(8,128)(2,1)} %get-tuple-element.33), calls=%async_computation.3 | async-start | bytes 2883584 | tf_op jit(solution)/shard_map/all_to_all | solution.py:560
  104.0 6.5 %grad_pass.1 = bf16[3072,512]{1,0:T(8,128)(2,1)} custom-call(bf16[3072,512]{1,0:T(8,128)(2,1)} %get-tuple-element.32.d_preact_ref, bf16[3,512,512]{2,1,0:T(8,128)(2,1)} %w_ref.5, bf16[3072,512]{1,0:T(8,128)(2,1)} %cot_ref.1), custom_call_target="tpu_custom_call" | custom-call | flops 1610612736 | bytes 9437184 | tf_op jit(solution)/shard_map/grad_pass/pallas_call | solution.py:116
  110.5 13.4 %all-to-all-done.3.packets_ref = bf16[64,88,128]{2,1,0:T(8,128)(2,1)S(1)} async-done(((bf16[64,88,128]{2,1,0:T(8,128)(2,1)}), bf16[64,88,128]{2,1,0:T(8,128)(2,1)S(1)}, u32[]{:S(2)}, u32[]{:S(2)}) %all-to-all-start.3) | async-done | bytes 1441824 | tf_op jit(solution)/shard_map/all_to_all | solution.py:560
  123.8 4.0 %collective-permute-start.2 = (bf16[64,88,128]{2,1,0:T(8,128)(2,1)S(1)}, bf16[64,88,128]{2,1,0:T(8,128)(2,1)S(1)}, u32[]{:S(2)}, u32[]{:S(2)}) collective-permute-start(bf16[64,88,128]{2,1,0:T(8,128)(2,1)S(1)} %all-to-all-done.3.packets_ref), channel_id=1, source_target_pairs={{0,1},{1,0},{2,3},{3,2},{4,5},{5,4},{6,7},{7,6},{8,9},{9,8},{10,11... | collective-permute-start | bytes 4325384 | tf_op jit(solution)/shard_map/ppermute | solution.py:563
  127.8 1.5 %unpack_mine.1 = (f32[1536,512]{1,0:T(8,128)}, f32[512,512]{1,0:T(8,128)}) custom-call(s32[1]{0:T(128)} %bitcast.core_ref, bf16[64,88,128]{2,1,0:T(8,128)(2,1)S(1)} %all-to-all-done.3.packets_ref), custom_call_target="tpu_custom_call" | custom-call | flops 720896 | bytes 4325376 | tf_op jit(solution)/shard_map/unpack_mine/pallas_call | solution.py:499
  129.3 1.3 node_grads.1
  130.7 1.5 %unpack_other.1 = (f32[1536,512]{1,0:T(8,128)}, f32[512,512]{1,0:T(8,128)}) custom-call(s32[1]{0:T(128)} %bitcast.core_ref, bf16[64,88,128]{2,1,0:T(8,128)(2,1)S(1)} %collective-permute-done.2.packets_ref, f32[1536,512]{1,0:T(8,128)} %get-tuple-element.36.refs_0_, f32[512,512]{1,0:T(8,128)} %get-tuple-element.37.refs_1_), custom_call_target="tpu_custom_call", output_to_operand_aliasing={{0}: (2, {}), {1}: (3, {})} | custom-call | flops 720896 | bytes 4325376 | tf_op jit(solution)/shard_map/unpack_other/pallas_call | solution.py:499
  (23 shorter events, 3.4 us)
Async XLA Ops:
  22.2 8.9 %copy-start = (bf16[3,512,512]{2,1,0:T(8,128)(2,1)S(1)}, bf16[3,512,512]{2,1,0:T(8,128)(2,1)}, u32[]{:S(2)}) copy-start(bf16[3,512,512]{2,1,0:T(8,128)(2,1)} %w_ref.5) | copy-start | bytes 4718596
  22.2 1.1 copy-start.1
  23.3 1.0 copy-start.5
  26.3 21.3 %all-to-all-start.1 = ((bf16[128,24,128]{2,1,0:T(8,128)(2,1)}), bf16[128,24,128]{2,1,0:T(8,128)(2,1)S(1)}, u32[]{:S(2)}, u32[]{:S(2)}) async-start(bf16[128,24,128]{2,1,0:T(8,128)(2,1)} %bitcast.4), calls=%async_computation.1 | async-start | bytes 1572864 | tf_op jit(solution)/shard_map/all_to_all | solution.py:538
  31.1 16.5 %copy-start.6 = (bf16[512,512]{1,0:T(8,128)(2,1)S(1)}, bf16[512,512]{1,0:T(8,128)(2,1)}, u32[]{:S(2)}) copy-start(bf16[512,512]{1,0:T(8,128)(2,1)} %w_out_hbm.1) | copy-start | bytes 1572868
  31.1 16.5 %copy-start.7 = (s32[24,128]{1,0:T(8,128)S(1)}, s32[24,128]{1,0:T(8,128)}, u32[]{:S(2)}) copy-start(s32[24,128]{1,0:T(8,128)} %send_ref.1) | copy-start | bytes 36868
  31.1 16.5 %copy-start.8 = (s32[24,128]{1,0:T(8,128)S(1)}, s32[24,128]{1,0:T(8,128)}, u32[]{:S(2)}) copy-start(s32[24,128]{1,0:T(8,128)} %recv_ref.1) | copy-start | bytes 36868
  31.1 16.5 %copy-start.9 = (f32[512]{0:T(512)S(1)}, f32[512]{0:T(512)}, u32[]{:S(2)}) copy-start(f32[512]{0:T(512)} %param.19) | copy-start | bytes 6148
  37.2 1.7 %copy-start.10 = (bf16[4,512,768]{2,1,0:T(8,128)(2,1)}, bf16[4,512,768]{2,1,0:T(8,128)(2,1)S(1)}, u32[]{:S(2)}) copy-start(bf16[4,512,768]{2,1,0:T(8,128)(2,1)S(1)} %get-tuple-element.24.turned_hbm) | copy-start | bytes 9437188
  68.1 0.9 copy-start.3
  69.0 3.6 %collective-permute-start = (bf16[64,72,128]{2,1,0:T(8,128)(2,1)S(1)}, bf16[64,72,128]{2,1,0:T(8,128)(2,1)S(1)}, u32[]{:S(2)}, u32[]{:S(2)}) collective-permute-start(bf16[64,72,128]{2,1,0:T(8,128)(2,1)S(1)} %get-tuple-element.27), channel_id=1, source_target_pairs={{0,1},{1,0},{2,3},{3,2},{4,5},{5,4},{6,7},{7,6},{8,9},{9,8},{10,11... | collective-permute-start | bytes 3538952 | tf_op jit(solution)/shard_map/ppermute | solution.py:553
  74.0 23.0 %all-to-all-start.2 = ((bf16[64,72,128]{2,1,0:T(8,128)(2,1)}), bf16[64,72,128]{2,1,0:T(8,128)(2,1)S(1)}, u32[]{:S(2)}, u32[]{:S(2)}) async-start(bf16[64,72,128]{2,1,0:T(8,128)(2,1)} %add.3), calls=%async_computation.2 | async-start | bytes 2359296 | tf_op jit(solution)/shard_map/all_to_all | solution.py:554
  78.7 1.1 copy-start.4
  80.7 2.0 %collective-permute-start.1 = (bf16[64,24,128]{2,1,0:T(8,128)(2,1)S(1)}, bf16[64,24,128]{2,1,0:T(8,128)(2,1)S(1)}, u32[]{:S(2)}, u32[]{:S(2)}) collective-permute-start(bf16[64,24,128]{2,1,0:T(8,128)(2,1)S(1)} %get-tuple-element.30), channel_id=1, source_target_pairs={{0,1},{1,0},{2,3},{3,2},{4,5},{5,4},{6,7},{7,6},{8,9},{9,8},{10,11... | collective-permute-start | bytes 1179656 | tf_op jit(solution)/shard_map/ppermute | solution.py:556
  98.7 25.2 %all-to-all-start.3 = ((bf16[64,88,128]{2,1,0:T(8,128)(2,1)}), bf16[64,88,128]{2,1,0:T(8,128)(2,1)S(1)}, u32[]{:S(2)}, u32[]{:S(2)}) async-start(bf16[64,88,128]{2,1,0:T(8,128)(2,1)} %get-tuple-element.33), calls=%async_computation.3 | async-start | bytes 2883584 | tf_op jit(solution)/shard_map/all_to_all | solution.py:560
  110.5 18.8 %copy-start.2 = (bf16[320,512]{1,0:T(8,128)(2,1)S(1)}, bf16[320,512]{1,0:T(8,128)(2,1)}, u32[]{:S(2)}) copy-start(bf16[320,512]{1,0:T(8,128)(2,1)} %cots_ref.1) | copy-start | bytes 983044
  123.8 6.8 %collective-permute-start.2 = (bf16[64,88,128]{2,1,0:T(8,128)(2,1)S(1)}, bf16[64,88,128]{2,1,0:T(8,128)(2,1)S(1)}, u32[]{:S(2)}, u32[]{:S(2)}) collective-permute-start(bf16[64,88,128]{2,1,0:T(8,128)(2,1)S(1)} %all-to-all-done.3.packets_ref), channel_id=1, source_target_pairs={{0,1},{1,0},{2,3},{3,2},{4,5},{5,4},{6,7},{7,6},{8,9},{9,8},{10,11... | collective-permute-start | bytes 4325384 | tf_op jit(solution)/shard_map/ppermute | solution.py:563

commit v3 on v2

--- a/solution.py
+++ b/solution.py
@@ -12,17 +12,19 @@
 LANES = 128
 CORES = 2
 TILE = 768
+CHUNKS = 2
 PRE = F32
 BIG_VMEM = 48 * 1024 * 1024
 
 VMEM = pl.BlockSpec(memory_space=pltpu.VMEM)
 ANYWHERE = pl.BlockSpec(memory_space=pl.ANY)
+HBM = pl.BlockSpec(memory_space=pltpu.HBM)
 
 def dot(left, right, over=((1,), (0,))):
     return lax.dot_general(left, right, (over, ((), ())), preferred_element_type=F32)
 
-def whole(shape):
-    return pl.BlockSpec(shape, lambda *_: (0,) * len(shape))
+def in_hbm(array):
+    return pltpu.with_memory_space_constraint(array, pltpu.HBM)
 
 def smem():
     return pl.BlockSpec(memory_space=pltpu.SMEM)
@@ -62,7 +64,7 @@
     total = devices * cap * 2 * width // LANES
     return pl.pallas_call(
         pick_kernel,
-        in_specs=[VMEM, ANYWHERE, ANYWHERE],
+        in_specs=[VMEM, HBM, HBM],
         out_shape=jax.ShapeDtypeStruct((total, LANES), BF),
         scratch_shapes=[
             pltpu.VMEM(feats.shape, BF),
@@ -73,7 +75,7 @@
         compiler_params=pltpu.CompilerParams(vmem_limit_bytes=BIG_VMEM),
         cost_estimate=cost(4 * devices * cap * feats.size, 4 * total * LANES),
         name="pick_rows",
-    )(asked, feats, cots)
+    )(asked, in_hbm(feats), in_hbm(cots))
 
 def slot_ids(position, chips, cap):
     half = cap * chips
@@ -121,7 +123,7 @@
         out_shape=jax.ShapeDtypeStruct(cot.shape, BF),
         cost_estimate=cost(2 * edges * width * width, 6 * cot.size),
         name="grad_pass",
-    )(d_preact, w_input, cot)
+    )(in_hbm(d_preact), w_input, in_hbm(cot))
 
 def edge_kernel(
     cap,
@@ -129,20 +131,17 @@
     send_ref,
     recv_ref,
     gain_ref,
-    rows_hbm,
-    w_in_hbm,
-    w_out_hbm,
+    rows_ref,
+    w_in,
+    w_out,
     pre_hbm,
     turned_hbm,
     cot_hbm,
     d_preact_hbm,
     own_ref,
     other_ref,
-    sums_hbm,
-    rows16,
+    sums_ref,
     rows32,
-    w_in,
-    w_out,
     pre,
     left,
     cot,
@@ -154,10 +153,8 @@
     hidden,
     d_mixed,
     sums,
-    sums16,
     grads,
     gain_sum,
-    once,
     per_tile,
 ):
     tiles, _, tile = turned_hbm.shape
@@ -170,12 +167,6 @@
     def span(t):
         return pl.ds(t * tile, tile)
 
-    first = (
-        pltpu.make_async_copy(rows_hbm, rows16, once.at[0]),
-        pltpu.make_async_copy(w_in_hbm.at[pl.ds(1, 2)], w_in, once.at[1]),
-        pltpu.make_async_copy(w_out_hbm, w_out, once.at[2]),
-    )
-
     def load(t):
         return (
             pltpu.make_async_copy(pre_hbm.at[span(t)], pre.at[span(t)], per_tile.at[0, t]),
@@ -186,10 +177,9 @@
     def leave(t):
         return pltpu.make_async_copy(d_preact.at[span(t)], d_preact_hbm.at[span(t)], per_tile.at[3, t])
 
-    for copy in first:
-        copy.start()
-    for copy in load(0):
-        copy.start()
+    for t in range(tiles):
+        for copy in load(t):
+            copy.start()
 
     lane_ids = slot_ids(lax.broadcasted_iota(jnp.int32, (1, slots), 1), chips, cap)
     row_ids = slot_ids(lax.broadcasted_iota(jnp.int32, (slots, LANES), 0), chips, cap)
@@ -213,8 +203,7 @@
     sums[...] = jnp.zeros_like(sums)
     grads[3 * width : 4 * width, :] = jnp.zeros((width, width), F32)
     gain_sum[...] = jnp.zeros_like(gain_sum)
-    first[0].wait()
-    rows32[...] = rows16[...].astype(F32)
+    rows32[...] = rows_ref[...].astype(F32)
     for core in range(CORES):
         for k in range(cap):
             at = (core * cap + k) * chips
@@ -225,13 +214,8 @@
                 cot_tab[at : at + chips, cols] = rows32[
                     pl.ds(begin + blocks, chips, stride=CORES * per), :
                 ].astype(BF)
-    first[1].wait()
-    for t in range(1, tiles):
-        for copy in load(t):
-            copy.start()
     for part in range(2):
-        pre_tab[part * slots : (part + 1) * slots, :] = dot(feat_tab[...], w_in[part]).astype(BF)
-    first[2].wait()
+        pre_tab[part * slots : (part + 1) * slots, :] = dot(feat_tab[...], w_in[part + 1]).astype(BF)
     for copy in load(0):
         copy.wait()
 
@@ -242,9 +226,10 @@
     def contract_output(t):
         grads[3 * width : 4 * width, :] += dot(hidden[t % 2], d_mixed[t % 2], ((0,), (0,)))
 
-    def contract_input(t):
-        mark_cols(t)
-        sums[...] += dot(left[t], d_preact[span(t), :])
+    def contract_input(t, c):
+        lines = (2 * slots + width) // CHUNKS
+        part = slice(c * lines, (c + 1) * lines)
+        sums[part, :] += dot(left[t, part, :], d_preact[span(t), :])
 
     preact = gather(0)
     for t in range(tiles):
@@ -258,23 +243,26 @@
         mixed = dot(rounded, w_out[...])
         found = dot(hot_rows[t % 2, :, slots:], cot_tab[...])
         if t:
-            contract_input(t - 1)
-        center = mixed - jnp.mean(mixed, axis=1, keepdims=True)
-        inverse = lax.rsqrt(jnp.mean(center * center, axis=1, keepdims=True) + 1e-5)
-        normed = center * inverse
-        upstream = cot[span(t), :].astype(F32) + found
-        scaled = upstream * gain_ref[...]
-        turned_back = (
-            inverse
-            * (
-                scaled
-                - jnp.mean(scaled, axis=1, keepdims=True)
-                - normed * jnp.mean(scaled * normed, axis=1, keepdims=True)
-            )
-        ).astype(BF)
-        gain_sum[...] += jnp.sum((upstream * normed).reshape(tile // 8, 8, width), axis=0)
-        d_mixed[t % 2] = turned_back
-        d_hidden = dot(turned_back, w_out[...], ((1,), (1,)))
+            mark_cols(t - 1)
+        for c in range(CHUNKS):
+            if t:
+                contract_input(t - 1, c)
+            part = slice(c * (tile // CHUNKS), (c + 1) * (tile // CHUNKS))
+            center = mixed[part] - jnp.mean(mixed[part], axis=1, keepdims=True)
+            inverse = lax.rsqrt(jnp.mean(center * center, axis=1, keepdims=True) + 1e-5)
+            normed = center * inverse
+            scaled = (cot[pl.ds(t * tile + part.start, tile // CHUNKS), :].astype(F32) + found[part]) * gain_ref[...]
+            product = scaled * normed
+            d_mixed[t % 2, part, :] = (
+                inverse
+                * (
+                    scaled
+                    - jnp.mean(scaled, axis=1, keepdims=True)
+                    - normed * jnp.mean(product, axis=1, keepdims=True)
+                )
+            ).astype(BF)
+            gain_sum[...] += jnp.sum(product.reshape(-1, 8, width), axis=0)
+        d_hidden = dot(d_mixed[t % 2], w_out[...], ((1,), (1,)))
         if t + 1 < tiles:
             for copy in load(t + 1):
                 copy.wait()
@@ -282,17 +270,17 @@
         d_preact[span(t), :] = (d_hidden * slope).astype(BF)
         leave(t).start()
     contract_output(tiles - 1)
-    contract_input(tiles - 1)
-
-    sums16[...] = sums[0 : 2 * slots, :].astype(BF)
-    summed = pltpu.make_async_copy(sums16, sums_hbm, once.at[3])
-    summed.start()
+    mark_cols(tiles - 1)
+    for c in range(CHUNKS):
+        contract_input(tiles - 1, c)
+
+    sums_ref[...] = sums[0 : 2 * slots, :].astype(BF)
     grads[0:width, :] = sums[2 * slots :, :]
     for part in range(2):
         grads[(part + 1) * width : (part + 2) * width, :] = dot(
-            feat_tab[...], sums16[part * slots : (part + 1) * slots, :], ((0,), (0,))
+            feat_tab[...], sums_ref[part * slots : (part + 1) * slots, :], ((0,), (0,))
         )
-    gain = jnp.sum(gain_sum[...], axis=0, keepdims=True)
+    gain = jnp.sum(gain_sum[...], axis=0, keepdims=True) / gain_ref[...]
     core = core_ref[0]
     piece = 2 * width // chips
     body = piece * blocks
@@ -306,7 +294,6 @@
             )
         lines = [jnp.broadcast_to(gain[:, j * LANES : (j + 1) * LANES], (2, LANES)) for j in range(blocks)]
         target[:, body:, :] = jnp.broadcast_to(jnp.concatenate(lines, axis=0)[None].astype(BF), (chips, 8, LANES))
-    summed.wait()
     for t in range(tiles):
         leave(t).wait()
 
@@ -319,8 +306,8 @@
     packets = jax.ShapeDtypeStruct((chips, 2 * width // chips * (width // LANES) + 8, LANES), BF)
     return pl.pallas_call(
         functools.partial(edge_kernel, cap),
-        in_specs=[smem()] + [VMEM] * 3 + [ANYWHERE] * 6,
-        out_specs=[ANYWHERE, VMEM, VMEM, ANYWHERE],
+        in_specs=[smem()] + [VMEM] * 6 + [HBM] * 3,
+        out_specs=[HBM, VMEM, VMEM, VMEM],
         out_shape=[
             jax.ShapeDtypeStruct(cot.shape, BF),
             packets,
@@ -328,10 +315,7 @@
             jax.ShapeDtypeStruct((2 * slots, width), BF),
         ],
         scratch_shapes=[
-            pltpu.VMEM(rows.shape, BF),
             pltpu.VMEM(rows.shape, F32),
-            pltpu.VMEM((2, width, width), BF),
-            pltpu.VMEM((width, width), BF),
             pltpu.VMEM(pre.shape, pre.dtype),
             pltpu.VMEM((tiles, 2 * slots + width, tile), BF),
             pltpu.VMEM(cot.shape, BF),
@@ -343,16 +327,14 @@
             pltpu.VMEM((2, tile, width), BF),
             pltpu.VMEM((2, tile, width), BF),
             pltpu.VMEM((2 * slots + width, width), F32),
-            pltpu.VMEM((2 * slots, width), BF),
             pltpu.VMEM((4 * width, width), F32),
             pltpu.VMEM((8, width), F32),
-            pltpu.SemaphoreType.DMA((4,)),
             pltpu.SemaphoreType.DMA((4, tiles)),
         ],
         compiler_params=pltpu.CompilerParams(vmem_limit_bytes=BIG_VMEM),
         cost_estimate=cost(16 * edges * width * width, 8 * cot.size),
         name="edge_pass",
-    )(core, send_slot, recv_slot, gain, rows, w_input, w_output, pre, turned, cot)
+    )(core, send_slot, recv_slot, gain, rows, w_input, w_output, in_hbm(pre), in_hbm(turned), in_hbm(cot))
 
 def back_kernel(cap, core_ref, sums_ref, w_ref, own_hbm, other_ref, tail, own, sem):
     slots = sums_ref.shape[0] // 2
@@ -419,7 +401,7 @@
         compiler_params=pltpu.CompilerParams(vmem_limit_bytes=BIG_VMEM),
         cost_estimate=cost(packets.size, 4 * packets.size),
         name="reduce_packets",
-    )(packets, own, got)
+    )(packets, in_hbm(own), got)
 
 def node_kernel(asked_ref, packets_ref, cots_ref, out_ref, ends, rows, hots):
     devices, cap = asked_ref.shape
@@ -550,9 +532,10 @@
         edge_cot,
         cap,
     )
-    merged = own + lax.ppermute(other, both, pairs)
-    packets = lax.all_to_all(merged, "chip", split_axis=0, concat_axis=0, tiled=True)
+    got = lax.ppermute(other, both, pairs)
     back_own, back_other = back_rows(core, sums, w_input, cap)
+    got, back_own, back_other = lax.optimization_barrier((got, back_own, back_other))
+    packets = lax.all_to_all(own + got, "chip", split_axis=0, concat_axis=0, tiled=True)
     back_got = lax.ppermute(back_other, both, pairs)
     factor = float(edges * devices) ** (-0.5)
     pieces, gain = reduce_packets(packets, back_own, back_got, factor)

time: 133 us -> 131 us (0.985)
  local copies, waits for them, and re-layouts: 5.96 us -> 2.64 us
    unnamed x22 -> x16, local copies, waits for them, and re-layouts: 5.76 us -> 2.44 us
    all_to_all x1, waiting for transfers between devices: 14.4 us -> 16.4 us  [on_device(): lax.all_to_all(own + got, 'chip', split_axis=0, concat_axis=0, tiled=True)]
    ppermute x1, waiting for transfers between devices: 2.47 us -> 0.82 us  [on_device(): got = lax.ppermute(other, both, pairs)]
where the time goes in v3:
time: 131 us
  Pallas kernels  43.1 us (33%)
  waiting for transfers between devices  40.7 us (31%)
  blocking collectives  20.7 us (16%)
  starting transfers between devices  20.6 us (16%)
  local copies, waits for them, and re-layouts  2.64 us (2%)
  other arithmetic  2.07 us (2%)
    all_to_all x1, blocking collectives, on_device(): lax.all_to_all(requests.reshape(devices, 1, cap), both, split_axis=0, con...  20.7 us
    pallas_call x1, Pallas kernels, edge_pass(): pl.pallas_call(functools.partial(edge_kernel, cap), in_specs=[smem()] + [...  20.4 us
    all_to_all x1, waiting for transfers between devices, on_device(): lax.all_to_all(own + got, 'chip', split_axis=0, concat_axis=0, tiled=True)  16.4 us
    all_to_all x1, waiting for transfers between devices, on_device(): lax.all_to_all(pieces, 'chip', split_axis=0, concat_axis=0, tiled=True)  13.4 us
    all_to_all x1, waiting for transfers between devices, on_device(): lax.all_to_all(picked, both, split_axis=0, concat_axis=0, tiled=True)  8.7 us
    pallas_call x1, Pallas kernels, grad_pass(): pl.pallas_call(grad_kernel, grid=(edges // tile,), in_specs=[tiles, pl.Bl...  6.46 us
    pallas_call x1, Pallas kernels, prep_pass(): pl.pallas_call(prep_kernel, grid=(tiles,), in_specs=[rows, pl.BlockSpec((...  6.07 us
    all_to_all x1, starting transfers between devices, on_device(): lax.all_to_all(pieces, 'chip', split_axis=0, concat_axis=0, tiled=True)  5.34 us
  transfers between devices with their start and end apart: 6, of which 6 were waited for; matrix products, arithmetic and copies ran while one was open for 0% of the time, Pallas kernels for 12%

profile of v3, /device:TPU:1, one launch (start us, length us, event | category | flops | bytes accessed | tf_op | source)
XLA Modules:
  0.0 130.7 jit_solution(14233671569550416295)
XLA Ops:
  0.6 0.7 reduce
  1.5 20.7 %all_to_all.20 = s32[128,1,3]{2,1,0:T(1,128)S(1)} all-to-all(s32[128,1,3]{2,1,0:T(1,128)S(1)} %bitcast.13), channel_id=1, replica_groups=mesh['chip'=64,'core'=2] {'chip','core'}, dimensions={0} | all-to-all | bytes 3072 | tf_op jit(solution)/shard_map/all_to_all | solution.py:516
  22.2 2.8 %pick_rows.1 = bf16[3072,128]{1,0:T(8,128)(2,1)} custom-call(s32[128,3]{1,0:T(8,128)S(1)} %bitcast.9, bf16[320,512]{1,0:T(8,128)(2,1)} %feats_hbm.1, bf16[320,512]{1,0:T(8,128)(2,1)} %cots_ref.1), custom_call_target="tpu_custom_call" | custom-call | flops 251658240 | bytes 1572864 | tf_op jit(solution)/shard_map/pick_rows/pallas_call | solution.py:65
  25.0 4.8 %all-to-all-start.1 = ((bf16[128,24,128]{2,1,0:T(8,128)(2,1)}), bf16[128,24,128]{2,1,0:T(8,128)(2,1)S(1)}, u32[]{:S(2)}, u32[]{:S(2)}) async-start(bf16[128,24,128]{2,1,0:T(8,128)(2,1)} %bitcast.4), calls=%async_computation.1 | async-start | bytes 1572864 | tf_op jit(solution)/shard_map/all_to_all | solution.py:520
  29.8 6.1 %prep_pass.1 = (f32[3072,512]{1,0:T(8,128)}, bf16[4,512,768]{2,1,0:T(8,128)(2,1)S(1)}) custom-call(bf16[3072,512]{1,0:T(8,128)(2,1)} %feats_ref.1, bf16[3,512,512]{2,1,0:T(8,128)(2,1)S(1)} %copy-done), custom_call_target="tpu_custom_call" | custom-call | flops 1610612736 | bytes 12582912 | tf_op jit(solution)/shard_map/prep_pass/pallas_call | solution.py:97
  35.9 1.7 %copy-done.7 = bf16[4,512,768]{2,1,0:T(8,128)(2,1)} copy-done((bf16[4,512,768]{2,1,0:T(8,128)(2,1)}, bf16[4,512,768]{2,1,0:T(8,128)(2,1)S(1)}, u32[]{:S(2)}) %copy-start.7) | copy-done | bytes 3145752
  37.6 8.7 %all-to-all-done.1 = bf16[128,24,128]{2,1,0:T(8,128)(2,1)S(1)} async-done(((bf16[128,24,128]{2,1,0:T(8,128)(2,1)}), bf16[128,24,128]{2,1,0:T(8,128)(2,1)S(1)}, u32[]{:S(2)}, u32[]{:S(2)}) %all-to-all-start.1) | async-done | bytes 786464 | tf_op jit(solution)/shard_map/all_to_all | solution.py:520
  46.3 20.4 %edge_pass.1 = (bf16[3072,512]{1,0:T(8,128)(2,1)}, bf16[64,72,128]{2,1,0:T(8,128)(2,1)S(1)}, bf16[64,72,128]{2,1,0:T(8,128)(2,1)S(1)}, bf16[768,512]{1,0:T(8,128)(2,1)S(1)}) custom-call(s32[1]{0:T(128)} %bitcast.core_ref, s32[24,128]{1,0:T(8,128)S(1)} %copy-done.4, s32[24,128]{1,0:T(8,128)S(1)} %copy-done.5, f32[1,512]{1,0:T(1,128)S(1)} %bitcast.11, ...), custom_call_target="tpu_custom_call" | custom-call | flops 12884901888 | bytes 12582912 | tf_op jit(solution)/shard_map/edge_pass/pallas_call | solution.py:307
  66.7 1.2 collective-permute-start
  68.0 0.9 back_rows.1
  68.9 0.7 copy-done.2
  69.6 0.8 collective-permute-done
  70.4 1.4 %add.3 = bf16[64,72,128]{2,1,0:T(8,128)(2,1)} add(bf16[64,72,128]{2,1,0:T(8,128)(2,1)S(1)} %get-tuple-element.29, bf16[64,72,128]{2,1,0:T(8,128)(2,1)S(1)} %collective-permute-done) | non-fusion elementwise | flops 589824 | bytes 3538944 | tf_op jit(solution)/shard_map/add | solution.py:538
  71.8 4.7 %all-to-all-start.2 = ((bf16[64,72,128]{2,1,0:T(8,128)(2,1)}), bf16[64,72,128]{2,1,0:T(8,128)(2,1)S(1)}, u32[]{:S(2)}, u32[]{:S(2)}) async-start(bf16[64,72,128]{2,1,0:T(8,128)(2,1)} %add.3), calls=%async_computation.2 | async-start | bytes 2359296 | tf_op jit(solution)/shard_map/all_to_all | solution.py:538
  77.1 1.3 %collective-permute-done.1.got_ref = bf16[64,24,128]{2,1,0:T(8,128)(2,1)S(1)} collective-permute-done((bf16[64,24,128]{2,1,0:T(8,128)(2,1)S(1)}, bf16[64,24,128]{2,1,0:T(8,128)(2,1)S(1)}, u32[]{:S(2)}, u32[]{:S(2)}) %collective-permute-start.1) | collective-permute-done | bytes 393248 | tf_op jit(solution)/shard_map/ppermute | solution.py:539
  78.4 16.4 %all-to-all-done.2.in_ref = bf16[64,72,128]{2,1,0:T(8,128)(2,1)S(1)} async-done(((bf16[64,72,128]{2,1,0:T(8,128)(2,1)}), bf16[64,72,128]{2,1,0:T(8,128)(2,1)S(1)}, u32[]{:S(2)}, u32[]{:S(2)}) %all-to-all-start.2) | async-done | bytes 1179680 | tf_op jit(solution)/shard_map/all_to_all | solution.py:538
  94.9 2.2 %reduce_packets.1 = (bf16[64,88,128]{2,1,0:T(8,128)(2,1)}, f32[1,512]{1,0:T(1,128)}) custom-call(bf16[64,72,128]{2,1,0:T(8,128)(2,1)S(1)} %all-to-all-done.2.in_ref, bf16[64,24,128]{2,1,0:T(8,128)(2,1)} %copy-done.2, bf16[64,24,128]{2,1,0:T(8,128)(2,1)S(1)} %collective-permute-done.1.got_ref), custom_call_target="tpu_custom_call" | custom-call | flops 589824 | bytes 2359296 | tf_op jit(solution)/shard_map/reduce_packets/pallas_call | solution.py:393
  97.1 5.3 %all-to-all-start.3 = ((bf16[64,88,128]{2,1,0:T(8,128)(2,1)}), bf16[64,88,128]{2,1,0:T(8,128)(2,1)S(1)}, u32[]{:S(2)}, u32[]{:S(2)}) async-start(bf16[64,88,128]{2,1,0:T(8,128)(2,1)} %get-tuple-element.39), calls=%async_computation.3 | async-start | bytes 2883584 | tf_op jit(solution)/shard_map/all_to_all | solution.py:543
  102.4 6.5 %grad_pass.1 = bf16[3072,512]{1,0:T(8,128)(2,1)} custom-call(bf16[3072,512]{1,0:T(8,128)(2,1)} %get-tuple-element.38.d_preact_ref, bf16[3,512,512]{2,1,0:T(8,128)(2,1)} %w_ref.5, bf16[3072,512]{1,0:T(8,128)(2,1)} %cot_ref.1), custom_call_target="tpu_custom_call" | custom-call | flops 1610612736 | bytes 9437184 | tf_op jit(solution)/shard_map/grad_pass/pallas_call | solution.py:118
  108.9 13.4 %all-to-all-done.3.packets_ref = bf16[64,88,128]{2,1,0:T(8,128)(2,1)S(1)} async-done(((bf16[64,88,128]{2,1,0:T(8,128)(2,1)}), bf16[64,88,128]{2,1,0:T(8,128)(2,1)S(1)}, u32[]{:S(2)}, u32[]{:S(2)}) %all-to-all-start.3) | async-done | bytes 1441824 | tf_op jit(solution)/shard_map/all_to_all | solution.py:543
  122.2 4.0 %collective-permute-start.2 = (bf16[64,88,128]{2,1,0:T(8,128)(2,1)S(1)}, bf16[64,88,128]{2,1,0:T(8,128)(2,1)S(1)}, u32[]{:S(2)}, u32[]{:S(2)}) collective-permute-start(bf16[64,88,128]{2,1,0:T(8,128)(2,1)S(1)} %all-to-all-done.3.packets_ref), channel_id=1, source_target_pairs={{0,1},{1,0},{2,3},{3,2},{4,5},{5,4},{6,7},{7,6},{8,9},{9,8},{10,11... | collective-permute-start | bytes 4325384 | tf_op jit(solution)/shard_map/ppermute | solution.py:546
  126.2 1.5 %unpack_mine.1 = (f32[1536,512]{1,0:T(8,128)}, f32[512,512]{1,0:T(8,128)}) custom-call(s32[1]{0:T(128)} %bitcast.core_ref, bf16[64,88,128]{2,1,0:T(8,128)(2,1)S(1)} %all-to-all-done.3.packets_ref), custom_call_target="tpu_custom_call" | custom-call | flops 720896 | bytes 4325376 | tf_op jit(solution)/shard_map/unpack_mine/pallas_call | solution.py:481
  127.7 1.3 node_grads.1
  129.1 1.5 %unpack_other.1 = (f32[1536,512]{1,0:T(8,128)}, f32[512,512]{1,0:T(8,128)}) custom-call(s32[1]{0:T(128)} %bitcast.core_ref, bf16[64,88,128]{2,1,0:T(8,128)(2,1)S(1)} %collective-permute-done.2.packets_ref, f32[1536,512]{1,0:T(8,128)} %get-tuple-element.42.refs_0_, f32[512,512]{1,0:T(8,128)} %get-tuple-element.43.refs_1_), custom_call_target="tpu_custom_call", output_to_operand_aliasing={{0}: (2, {}), {1}: (3, {})} | custom-call | flops 720896 | bytes 4325376 | tf_op jit(solution)/shard_map/unpack_other/pallas_call | solution.py:481
  (17 shorter events, 0.9 us)
Async XLA Ops:
  22.2 7.6 %copy-start = (bf16[3,512,512]{2,1,0:T(8,128)(2,1)S(1)}, bf16[3,512,512]{2,1,0:T(8,128)(2,1)}, u32[]{:S(2)}) copy-start(bf16[3,512,512]{2,1,0:T(8,128)(2,1)} %w_ref.5) | copy-start | bytes 4718596
  25.0 21.3 %all-to-all-start.1 = ((bf16[128,24,128]{2,1,0:T(8,128)(2,1)}), bf16[128,24,128]{2,1,0:T(8,128)(2,1)S(1)}, u32[]{:S(2)}, u32[]{:S(2)}) async-start(bf16[128,24,128]{2,1,0:T(8,128)(2,1)} %bitcast.4), calls=%async_computation.1 | async-start | bytes 1572864 | tf_op jit(solution)/shard_map/all_to_all | solution.py:520
  29.8 16.5 %copy-start.3 = (bf16[512,512]{1,0:T(8,128)(2,1)S(1)}, bf16[512,512]{1,0:T(8,128)(2,1)}, u32[]{:S(2)}) copy-start(bf16[512,512]{1,0:T(8,128)(2,1)} %w_out.1) | copy-start | bytes 1572868
  29.8 16.5 %copy-start.4 = (s32[24,128]{1,0:T(8,128)S(1)}, s32[24,128]{1,0:T(8,128)}, u32[]{:S(2)}) copy-start(s32[24,128]{1,0:T(8,128)} %send_ref.1) | copy-start | bytes 36868
  29.8 16.5 %copy-start.5 = (s32[24,128]{1,0:T(8,128)S(1)}, s32[24,128]{1,0:T(8,128)}, u32[]{:S(2)}) copy-start(s32[24,128]{1,0:T(8,128)} %recv_ref.1) | copy-start | bytes 36868
  29.8 16.5 %copy-start.6 = (f32[512]{0:T(512)S(1)}, f32[512]{0:T(512)}, u32[]{:S(2)}) copy-start(f32[512]{0:T(512)} %param.19) | copy-start | bytes 6148
  35.9 1.7 %copy-start.7 = (bf16[4,512,768]{2,1,0:T(8,128)(2,1)}, bf16[4,512,768]{2,1,0:T(8,128)(2,1)S(1)}, u32[]{:S(2)}) copy-start(bf16[4,512,768]{2,1,0:T(8,128)(2,1)S(1)} %get-tuple-element.27.turned_hbm) | copy-start | bytes 9437188
  66.7 3.7 %collective-permute-start = (bf16[64,72,128]{2,1,0:T(8,128)(2,1)S(1)}, bf16[64,72,128]{2,1,0:T(8,128)(2,1)S(1)}, u32[]{:S(2)}, u32[]{:S(2)}) collective-permute-start(bf16[64,72,128]{2,1,0:T(8,128)(2,1)S(1)} %get-tuple-element.30), channel_id=1, source_target_pairs={{0,1},{1,0},{2,3},{3,2},{4,5},{5,4},{6,7},{7,6},{8,9},{9,8},{10,11... | collective-permute-start | bytes 3538952 | tf_op jit(solution)/shard_map/ppermute | solution.py:535
  68.9 0.7 copy-start.2
  71.8 23.0 %all-to-all-start.2 = ((bf16[64,72,128]{2,1,0:T(8,128)(2,1)}), bf16[64,72,128]{2,1,0:T(8,128)(2,1)S(1)}, u32[]{:S(2)}, u32[]{:S(2)}) async-start(bf16[64,72,128]{2,1,0:T(8,128)(2,1)} %add.3), calls=%async_computation.2 | async-start | bytes 2359296 | tf_op jit(solution)/shard_map/all_to_all | solution.py:538
  76.5 2.0 %collective-permute-start.1 = (bf16[64,24,128]{2,1,0:T(8,128)(2,1)S(1)}, bf16[64,24,128]{2,1,0:T(8,128)(2,1)S(1)}, u32[]{:S(2)}, u32[]{:S(2)}) collective-permute-start(bf16[64,24,128]{2,1,0:T(8,128)(2,1)S(1)} %get-tuple-element.36), channel_id=1, source_target_pairs={{0,1},{1,0},{2,3},{3,2},{4,5},{5,4},{6,7},{7,6},{8,9},{9,8},{10,11... | collective-permute-start | bytes 1179656 | tf_op jit(solution)/shard_map/ppermute | solution.py:539
  97.1 25.2 %all-to-all-start.3 = ((bf16[64,88,128]{2,1,0:T(8,128)(2,1)}), bf16[64,88,128]{2,1,0:T(8,128)(2,1)S(1)}, u32[]{:S(2)}, u32[]{:S(2)}) async-start(bf16[64,88,128]{2,1,0:T(8,128)(2,1)} %get-tuple-element.39), calls=%async_computation.3 | async-start | bytes 2883584 | tf_op jit(solution)/shard_map/all_to_all | solution.py:543
  108.9 18.8 %copy-start.1 = (bf16[320,512]{1,0:T(8,128)(2,1)S(1)}, bf16[320,512]{1,0:T(8,128)(2,1)}, u32[]{:S(2)}) copy-start(bf16[320,512]{1,0:T(8,128)(2,1)} %cots_ref.1) | copy-start | bytes 983044
  122.2 6.8 %collective-permute-start.2 = (bf16[64,88,128]{2,1,0:T(8,128)(2,1)S(1)}, bf16[64,88,128]{2,1,0:T(8,128)(2,1)S(1)}, u32[]{:S(2)}, u32[]{:S(2)}) collective-permute-start(bf16[64,88,128]{2,1,0:T(8,128)(2,1)S(1)} %all-to-all-done.3.packets_ref), channel_id=1, source_target_pairs={{0,1},{1,0},{2,3},{3,2},{4,5},{5,4},{6,7},{7,6},{8,9},{9,8},{10,11... | collective-permute-start | bytes 4325384 | tf_op jit(solution)/shard_map/ppermute | solution.py:546

commit v4 on v3

--- a/solution.py
+++ b/solution.py
@@ -65,6 +65,7 @@
     return pl.pallas_call(
         pick_kernel,
         in_specs=[VMEM, HBM, HBM],
+        out_specs=VMEM,
         out_shape=jax.ShapeDtypeStruct((total, LANES), BF),
         scratch_shapes=[
             pltpu.VMEM(feats.shape, BF),
@@ -378,6 +379,22 @@
         name="back_rows",
     )(core, sums, w_input)
 
+def merge_kernel(own_ref, got_ref, out_ref):
+    out_ref[...] = own_ref[...] + got_ref[...]
+
+
+def merge(own, got):
+    return pl.pallas_call(
+        merge_kernel,
+        in_specs=[VMEM, VMEM],
+        out_specs=VMEM,
+        out_shape=jax.ShapeDtypeStruct(own.shape, BF),
+        compiler_params=pltpu.CompilerParams(vmem_limit_bytes=BIG_VMEM),
+        cost_estimate=cost(own.size, 6 * own.size),
+        name="merge",
+    )(own, got)
+
+
 def reduce_kernel(factor, in_ref, own_hbm, got_ref, out_ref, gain_ref, own, sem):
     copy = pltpu.make_async_copy(own_hbm, own, sem)
     copy.start()
@@ -397,6 +414,7 @@
             jax.ShapeDtypeStruct((1, 4 * LANES), F32),
         ],
         in_specs=[VMEM, ANYWHERE, VMEM],
+        out_specs=[VMEM, VMEM],
         scratch_shapes=[pltpu.VMEM(own.shape, BF), pltpu.SemaphoreType.DMA],
         compiler_params=pltpu.CompilerParams(vmem_limit_bytes=BIG_VMEM),
         cost_estimate=cost(packets.size, 4 * packets.size),
@@ -535,7 +553,7 @@
     got = lax.ppermute(other, both, pairs)
     back_own, back_other = back_rows(core, sums, w_input, cap)
     got, back_own, back_other = lax.optimization_barrier((got, back_own, back_other))
-    packets = lax.all_to_all(own + got, "chip", split_axis=0, concat_axis=0, tiled=True)
+    packets = lax.all_to_all(merge(own, got), "chip", split_axis=0, concat_axis=0, tiled=True)
     back_got = lax.ppermute(back_other, both, pairs)
     factor = float(edges * devices) ** (-0.5)
     pieces, gain = reduce_packets(packets, back_own, back_got, factor)

time: 131 us -> 131 us (level)
  other arithmetic: 2.07 us -> 0.7 us
    add x1 -> x0, other arithmetic: 1.37 us -> none  [on_device(): own + got]
    pallas_call x1 -> x2, Pallas kernels: 2.8 us -> 4.07 us  [the longest x1 2.8 us: pick_rows(): pl.pallas_call(pick_kernel, in_specs=[VMEM, HBM, HBM], out_specs=VMEM, ou...]
where the time goes in v4:
time: 131 us
  Pallas kernels  44.3 us (34%)
  waiting for transfers between devices  40.7 us (31%)
  blocking collectives  20.7 us (16%)
  starting transfers between devices  20.6 us (16%)
  local copies, waits for them, and re-layouts  2.64 us (2%)
    all_to_all x1, blocking collectives, on_device(): lax.all_to_all(requests.reshape(devices, 1, cap), both, split_axis=0, con...  20.7 us
    pallas_call x1, Pallas kernels, edge_pass(): pl.pallas_call(functools.partial(edge_kernel, cap), in_specs=[smem()] + [...  20.4 us
    all_to_all x1, waiting for transfers between devices, on_device(): lax.all_to_all(merge(own, got), 'chip', split_axis=0, concat_axis=0, tile...  16.4 us
    all_to_all x1, waiting for transfers between devices, on_device(): lax.all_to_all(pieces, 'chip', split_axis=0, concat_axis=0, tiled=True)  13.4 us
    all_to_all x1, waiting for transfers between devices, on_device(): lax.all_to_all(picked, both, split_axis=0, concat_axis=0, tiled=True)  8.7 us
    pallas_call x1, Pallas kernels, grad_pass(): pl.pallas_call(grad_kernel, grid=(edges // tile,), in_specs=[tiles, pl.Bl...  6.46 us
    pallas_call x1, Pallas kernels, prep_pass(): pl.pallas_call(prep_kernel, grid=(tiles,), in_specs=[rows, pl.BlockSpec((...  6.07 us
    all_to_all x1, starting transfers between devices, on_device(): lax.all_to_all(pieces, 'chip', split_axis=0, concat_axis=0, tiled=True)  5.34 us
  transfers between devices with their start and end apart: 6, of which 6 were waited for; matrix products, arithmetic and copies ran while one was open for 0% of the time, Pallas kernels for 12%

profile of v4, /device:TPU:1, one launch (start us, length us, event | category | flops | bytes accessed | tf_op | source)
XLA Modules:
  0.0 130.6 jit_solution(13205565563153021327)
XLA Ops:
  0.6 0.7 reduce
  1.5 20.7 %all_to_all.20 = s32[128,1,3]{2,1,0:T(1,128)S(1)} all-to-all(s32[128,1,3]{2,1,0:T(1,128)S(1)} %bitcast.13), channel_id=1, replica_groups=mesh['chip'=64,'core'=2] {'chip','core'}, dimensions={0} | all-to-all | bytes 3072 | tf_op jit(solution)/shard_map/all_to_all | solution.py:534
  22.2 2.8 %pick_rows.1 = bf16[3072,128]{1,0:T(8,128)(2,1)} custom-call(s32[128,3]{1,0:T(8,128)S(1)} %bitcast.9, bf16[320,512]{1,0:T(8,128)(2,1)} %feats_hbm.1, bf16[320,512]{1,0:T(8,128)(2,1)} %cots_ref.1), custom_call_target="tpu_custom_call" | custom-call | flops 251658240 | bytes 1572864 | tf_op jit(solution)/shard_map/pick_rows/pallas_call | solution.py:65
  25.0 4.8 %all-to-all-start.1 = ((bf16[128,24,128]{2,1,0:T(8,128)(2,1)}), bf16[128,24,128]{2,1,0:T(8,128)(2,1)S(1)}, u32[]{:S(2)}, u32[]{:S(2)}) async-start(bf16[128,24,128]{2,1,0:T(8,128)(2,1)} %bitcast.4), calls=%async_computation.1 | async-start | bytes 1572864 | tf_op jit(solution)/shard_map/all_to_all | solution.py:538
  29.8 6.1 %prep_pass.1 = (f32[3072,512]{1,0:T(8,128)}, bf16[4,512,768]{2,1,0:T(8,128)(2,1)S(1)}) custom-call(bf16[3072,512]{1,0:T(8,128)(2,1)} %feats_ref.1, bf16[3,512,512]{2,1,0:T(8,128)(2,1)S(1)} %copy-done), custom_call_target="tpu_custom_call" | custom-call | flops 1610612736 | bytes 12582912 | tf_op jit(solution)/shard_map/prep_pass/pallas_call | solution.py:98
  35.9 1.7 %copy-done.7 = bf16[4,512,768]{2,1,0:T(8,128)(2,1)} copy-done((bf16[4,512,768]{2,1,0:T(8,128)(2,1)}, bf16[4,512,768]{2,1,0:T(8,128)(2,1)S(1)}, u32[]{:S(2)}) %copy-start.7) | copy-done | bytes 3145752
  37.6 8.7 %all-to-all-done.1 = bf16[128,24,128]{2,1,0:T(8,128)(2,1)S(1)} async-done(((bf16[128,24,128]{2,1,0:T(8,128)(2,1)}), bf16[128,24,128]{2,1,0:T(8,128)(2,1)S(1)}, u32[]{:S(2)}, u32[]{:S(2)}) %all-to-all-start.1) | async-done | bytes 786464 | tf_op jit(solution)/shard_map/all_to_all | solution.py:538
  46.3 20.4 %edge_pass.1 = (bf16[3072,512]{1,0:T(8,128)(2,1)}, bf16[64,72,128]{2,1,0:T(8,128)(2,1)S(1)}, bf16[64,72,128]{2,1,0:T(8,128)(2,1)S(1)}, bf16[768,512]{1,0:T(8,128)(2,1)S(1)}) custom-call(s32[1]{0:T(128)} %bitcast.core_ref, s32[24,128]{1,0:T(8,128)S(1)} %copy-done.4, s32[24,128]{1,0:T(8,128)S(1)} %copy-done.5, f32[1,512]{1,0:T(1,128)S(1)} %bitcast.11, ...), custom_call_target="tpu_custom_call" | custom-call | flops 12884901888 | bytes 12582912 | tf_op jit(solution)/shard_map/edge_pass/pallas_call | solution.py:308
  66.7 1.2 collective-permute-start
  67.9 0.9 back_rows.1
  68.9 0.7 copy-done.2
  69.6 0.8 collective-permute-done.got_ref
  70.4 1.3 merge.1
  71.7 4.7 %all-to-all-start.2 = ((bf16[64,72,128]{2,1,0:T(8,128)(2,1)}), bf16[64,72,128]{2,1,0:T(8,128)(2,1)S(1)}, u32[]{:S(2)}, u32[]{:S(2)}) async-start(bf16[64,72,128]{2,1,0:T(8,128)(2,1)} %merge.1), calls=%async_computation.2 | async-start | bytes 2359296 | tf_op jit(solution)/shard_map/all_to_all | solution.py:556
  77.0 1.3 %collective-permute-done.1.got_ref = bf16[64,24,128]{2,1,0:T(8,128)(2,1)S(1)} collective-permute-done((bf16[64,24,128]{2,1,0:T(8,128)(2,1)S(1)}, bf16[64,24,128]{2,1,0:T(8,128)(2,1)S(1)}, u32[]{:S(2)}, u32[]{:S(2)}) %collective-permute-start.1) | collective-permute-done | bytes 393248 | tf_op jit(solution)/shard_map/ppermute | solution.py:557
  78.3 16.4 %all-to-all-done.2.in_ref = bf16[64,72,128]{2,1,0:T(8,128)(2,1)S(1)} async-done(((bf16[64,72,128]{2,1,0:T(8,128)(2,1)}), bf16[64,72,128]{2,1,0:T(8,128)(2,1)S(1)}, u32[]{:S(2)}, u32[]{:S(2)}) %all-to-all-start.2) | async-done | bytes 1179680 | tf_op jit(solution)/shard_map/all_to_all | solution.py:556
  94.7 2.2 %reduce_packets.1 = (bf16[64,88,128]{2,1,0:T(8,128)(2,1)}, f32[1,512]{1,0:T(1,128)}) custom-call(bf16[64,72,128]{2,1,0:T(8,128)(2,1)S(1)} %all-to-all-done.2.in_ref, bf16[64,24,128]{2,1,0:T(8,128)(2,1)} %copy-done.2, bf16[64,24,128]{2,1,0:T(8,128)(2,1)S(1)} %collective-permute-done.1.got_ref), custom_call_target="tpu_custom_call" | custom-call | flops 589824 | bytes 2359296 | tf_op jit(solution)/shard_map/reduce_packets/pallas_call | solution.py:410
  96.9 5.3 %all-to-all-start.3 = ((bf16[64,88,128]{2,1,0:T(8,128)(2,1)}), bf16[64,88,128]{2,1,0:T(8,128)(2,1)S(1)}, u32[]{:S(2)}, u32[]{:S(2)}) async-start(bf16[64,88,128]{2,1,0:T(8,128)(2,1)} %get-tuple-element.39), calls=%async_computation.3 | async-start | bytes 2883584 | tf_op jit(solution)/shard_map/all_to_all | solution.py:561
  102.3 6.5 %grad_pass.1 = bf16[3072,512]{1,0:T(8,128)(2,1)} custom-call(bf16[3072,512]{1,0:T(8,128)(2,1)} %get-tuple-element.38.d_preact_ref, bf16[3,512,512]{2,1,0:T(8,128)(2,1)} %w_ref.5, bf16[3072,512]{1,0:T(8,128)(2,1)} %cot_ref.1), custom_call_target="tpu_custom_call" | custom-call | flops 1610612736 | bytes 9437184 | tf_op jit(solution)/shard_map/grad_pass/pallas_call | solution.py:119
  108.7 13.4 %all-to-all-done.3.packets_ref = bf16[64,88,128]{2,1,0:T(8,128)(2,1)S(1)} async-done(((bf16[64,88,128]{2,1,0:T(8,128)(2,1)}), bf16[64,88,128]{2,1,0:T(8,128)(2,1)S(1)}, u32[]{:S(2)}, u32[]{:S(2)}) %all-to-all-start.3) | async-done | bytes 1441824 | tf_op jit(solution)/shard_map/all_to_all | solution.py:561
  122.1 4.0 %collective-permute-start.2 = (bf16[64,88,128]{2,1,0:T(8,128)(2,1)S(1)}, bf16[64,88,128]{2,1,0:T(8,128)(2,1)S(1)}, u32[]{:S(2)}, u32[]{:S(2)}) collective-permute-start(bf16[64,88,128]{2,1,0:T(8,128)(2,1)S(1)} %all-to-all-done.3.packets_ref), channel_id=1, source_target_pairs={{0,1},{1,0},{2,3},{3,2},{4,5},{5,4},{6,7},{7,6},{8,9},{9,8},{10,11... | collective-permute-start | bytes 4325384 | tf_op jit(solution)/shard_map/ppermute | solution.py:564
  126.1 1.5 %unpack_mine.1 = (f32[1536,512]{1,0:T(8,128)}, f32[512,512]{1,0:T(8,128)}) custom-call(s32[1]{0:T(128)} %bitcast.core_ref, bf16[64,88,128]{2,1,0:T(8,128)(2,1)S(1)} %all-to-all-done.3.packets_ref), custom_call_target="tpu_custom_call" | custom-call | flops 720896 | bytes 4325376 | tf_op jit(solution)/shard_map/unpack_mine/pallas_call | solution.py:499
  127.6 1.3 node_grads.1
  128.9 1.5 %unpack_other.1 = (f32[1536,512]{1,0:T(8,128)}, f32[512,512]{1,0:T(8,128)}) custom-call(s32[1]{0:T(128)} %bitcast.core_ref, bf16[64,88,128]{2,1,0:T(8,128)(2,1)S(1)} %collective-permute-done.2.packets_ref, f32[1536,512]{1,0:T(8,128)} %get-tuple-element.42.refs_0_, f32[512,512]{1,0:T(8,128)} %get-tuple-element.43.refs_1_), custom_call_target="tpu_custom_call", output_to_operand_aliasing={{0}: (2, {}), {1}: (3, {})} | custom-call | flops 720896 | bytes 4325376 | tf_op jit(solution)/shard_map/unpack_other/pallas_call | solution.py:499
  (17 shorter events, 0.9 us)
Async XLA Ops:
  22.2 7.6 %copy-start = (bf16[3,512,512]{2,1,0:T(8,128)(2,1)S(1)}, bf16[3,512,512]{2,1,0:T(8,128)(2,1)}, u32[]{:S(2)}) copy-start(bf16[3,512,512]{2,1,0:T(8,128)(2,1)} %w_ref.5) | copy-start | bytes 4718596
  25.0 21.3 %all-to-all-start.1 = ((bf16[128,24,128]{2,1,0:T(8,128)(2,1)}), bf16[128,24,128]{2,1,0:T(8,128)(2,1)S(1)}, u32[]{:S(2)}, u32[]{:S(2)}) async-start(bf16[128,24,128]{2,1,0:T(8,128)(2,1)} %bitcast.4), calls=%async_computation.1 | async-start | bytes 1572864 | tf_op jit(solution)/shard_map/all_to_all | solution.py:538
  29.8 16.5 %copy-start.3 = (bf16[512,512]{1,0:T(8,128)(2,1)S(1)}, bf16[512,512]{1,0:T(8,128)(2,1)}, u32[]{:S(2)}) copy-start(bf16[512,512]{1,0:T(8,128)(2,1)} %w_out.1) | copy-start | bytes 1572868
  29.8 16.5 %copy-start.4 = (s32[24,128]{1,0:T(8,128)S(1)}, s32[24,128]{1,0:T(8,128)}, u32[]{:S(2)}) copy-start(s32[24,128]{1,0:T(8,128)} %send_ref.1) | copy-start | bytes 36868
  29.8 16.5 %copy-start.5 = (s32[24,128]{1,0:T(8,128)S(1)}, s32[24,128]{1,0:T(8,128)}, u32[]{:S(2)}) copy-start(s32[24,128]{1,0:T(8,128)} %recv_ref.1) | copy-start | bytes 36868
  29.8 16.5 %copy-start.6 = (f32[512]{0:T(512)S(1)}, f32[512]{0:T(512)}, u32[]{:S(2)}) copy-start(f32[512]{0:T(512)} %param.19) | copy-start | bytes 6148
  35.9 1.7 %copy-start.7 = (bf16[4,512,768]{2,1,0:T(8,128)(2,1)}, bf16[4,512,768]{2,1,0:T(8,128)(2,1)S(1)}, u32[]{:S(2)}) copy-start(bf16[4,512,768]{2,1,0:T(8,128)(2,1)S(1)} %get-tuple-element.27.turned_hbm) | copy-start | bytes 9437188
  66.7 3.7 %collective-permute-start = (bf16[64,72,128]{2,1,0:T(8,128)(2,1)S(1)}, bf16[64,72,128]{2,1,0:T(8,128)(2,1)S(1)}, u32[]{:S(2)}, u32[]{:S(2)}) collective-permute-start(bf16[64,72,128]{2,1,0:T(8,128)(2,1)S(1)} %get-tuple-element.30), channel_id=1, source_target_pairs={{0,1},{1,0},{2,3},{3,2},{4,5},{5,4},{6,7},{7,6},{8,9},{9,8},{10,11... | collective-permute-start | bytes 3538952 | tf_op jit(solution)/shard_map/ppermute | solution.py:553
  68.9 0.7 copy-start.2
  71.7 23.0 %all-to-all-start.2 = ((bf16[64,72,128]{2,1,0:T(8,128)(2,1)}), bf16[64,72,128]{2,1,0:T(8,128)(2,1)S(1)}, u32[]{:S(2)}, u32[]{:S(2)}) async-start(bf16[64,72,128]{2,1,0:T(8,128)(2,1)} %merge.1), calls=%async_computation.2 | async-start | bytes 2359296 | tf_op jit(solution)/shard_map/all_to_all | solution.py:556
  76.4 2.0 %collective-permute-start.1 = (bf16[64,24,128]{2,1,0:T(8,128)(2,1)S(1)}, bf16[64,24,128]{2,1,0:T(8,128)(2,1)S(1)}, u32[]{:S(2)}, u32[]{:S(2)}) collective-permute-start(bf16[64,24,128]{2,1,0:T(8,128)(2,1)S(1)} %get-tuple-element.36), channel_id=1, source_target_pairs={{0,1},{1,0},{2,3},{3,2},{4,5},{5,4},{6,7},{7,6},{8,9},{9,8},{10,11... | collective-permute-start | bytes 1179656 | tf_op jit(solution)/shard_map/ppermute | solution.py:557
  96.9 25.2 %all-to-all-start.3 = ((bf16[64,88,128]{2,1,0:T(8,128)(2,1)}), bf16[64,88,128]{2,1,0:T(8,128)(2,1)S(1)}, u32[]{:S(2)}, u32[]{:S(2)}) async-start(bf16[64,88,128]{2,1,0:T(8,128)(2,1)} %get-tuple-element.39), calls=%async_computation.3 | async-start | bytes 2883584 | tf_op jit(solution)/shard_map/all_to_all | solution.py:561
  108.7 18.8 %copy-start.1 = (bf16[320,512]{1,0:T(8,128)(2,1)S(1)}, bf16[320,512]{1,0:T(8,128)(2,1)}, u32[]{:S(2)}) copy-start(bf16[320,512]{1,0:T(8,128)(2,1)} %cots_ref.1) | copy-start | bytes 983044
  122.1 6.8 %collective-permute-start.2 = (bf16[64,88,128]{2,1,0:T(8,128)(2,1)S(1)}, bf16[64,88,128]{2,1,0:T(8,128)(2,1)S(1)}, u32[]{:S(2)}, u32[]{:S(2)}) collective-permute-start(bf16[64,88,128]{2,1,0:T(8,128)(2,1)S(1)} %all-to-all-done.3.packets_ref), channel_id=1, source_target_pairs={{0,1},{1,0},{2,3},{3,2},{4,5},{5,4},{6,7},{7,6},{8,9},{9,8},{10,11... | collective-permute-start | bytes 4325384 | tf_op jit(solution)/shard_map/ppermute | solution.py:564

commit v5 on v4

--- a/solution.py
+++ b/solution.py
@@ -395,33 +395,56 @@
     )(own, got)
 
 
-def reduce_kernel(factor, in_ref, own_hbm, got_ref, out_ref, gain_ref, own, sem):
-    copy = pltpu.make_async_copy(own_hbm, own, sem)
-    copy.start()
+def tail_kernel(own_ref, got_ref, out_ref):
+    out_ref[:, out_ref.shape[1] - own_ref.shape[1] :, :] = own_ref[...] + got_ref[...]
+
+
+def tail_packets(own, got, body):
+    chips, lines, _ = own.shape
+    return pl.pallas_call(
+        tail_kernel,
+        out_shape=jax.ShapeDtypeStruct((chips, body + lines, LANES), BF),
+        compiler_params=pltpu.CompilerParams(vmem_limit_bytes=BIG_VMEM),
+        cost_estimate=cost(own.size, 10 * own.size),
+        name="tail_packets",
+    )(own, got)
+
+
+def reduce_kernel(factor, in_ref, tails_hbm, out_hbm, gain_ref, piece, sems):
+    del tails_hbm
+    body = piece.shape[0]
     total = jnp.sum(in_ref[...].astype(F32), axis=0) * factor
-    body = total.shape[0] - 8
-    out_ref[:, 0:body, :] = jnp.broadcast_to(total[0:body].astype(BF)[None], (in_ref.shape[0], body, LANES))
+    piece[...] = total[0:body].astype(BF)
+    copies = [
+        pltpu.make_async_copy(piece, out_hbm.at[chip, pl.ds(0, body)], sems.at[chip])
+        for chip in range(in_ref.shape[0])
+    ]
+    for copy in copies:
+        copy.start()
     gain_ref[...] = jnp.concatenate([total[body + 2 * j : body + 2 * j + 1] for j in range(4)], axis=1)
-    copy.wait()
-    out_ref[:, body:, :] = own[...] + got_ref[...]
-
-def reduce_packets(packets, own, got, factor):
+    for copy in copies:
+        copy.wait()
+
+
+def reduce_packets(packets, tails, factor):
     chips, lines, _ = packets.shape
     return pl.pallas_call(
         functools.partial(reduce_kernel, factor),
         out_shape=[
-            jax.ShapeDtypeStruct((chips, lines - 8 + own.shape[1], LANES), BF),
+            jax.ShapeDtypeStruct(tails.shape, BF),
             jax.ShapeDtypeStruct((1, 4 * LANES), F32),
         ],
-        in_specs=[VMEM, ANYWHERE, VMEM],
-        out_specs=[VMEM, VMEM],
-        scratch_shapes=[pltpu.VMEM(own.shape, BF), pltpu.SemaphoreType.DMA],
+        in_specs=[VMEM, HBM],
+        out_specs=[HBM, VMEM],
+        scratch_shapes=[pltpu.VMEM((lines - 8, LANES), BF), pltpu.SemaphoreType.DMA((chips,))],
+        input_output_aliases={1: 0},
         compiler_params=pltpu.CompilerParams(vmem_limit_bytes=BIG_VMEM),
         cost_estimate=cost(packets.size, 4 * packets.size),
         name="reduce_packets",
-    )(packets, in_hbm(own), got)
-
-def node_kernel(asked_ref, packets_ref, cots_ref, out_ref, ends, rows, hots):
+    )(packets, in_hbm(tails))
+
+
+def node_sums(asked_ref, packets_ref, cots_ref, out_ref, ends, rows, hots):
     devices, cap = asked_ref.shape
     nodes, width = cots_ref.shape
     blocks = width // LANES
@@ -438,30 +461,12 @@
     sums = dot(hots[...], rows[...], ((0,), (0,)))
     out_ref[...] = (cots_ref[...].astype(F32) + sums).astype(BF)
 
-def node_grads(asked, packets, cots):
-    devices, cap = asked.shape
-    nodes, width = cots.shape
-    slots = devices * cap
-    return pl.pallas_call(
-        node_kernel,
-        out_shape=jax.ShapeDtypeStruct(cots.shape, BF),
-        scratch_shapes=[
-            pltpu.VMEM((slots * width // LANES, LANES), F32),
-            pltpu.VMEM((slots, width), BF),
-            pltpu.VMEM((slots, nodes), BF),
-        ],
-        compiler_params=pltpu.CompilerParams(vmem_limit_bytes=BIG_VMEM),
-        cost_estimate=cost(2 * slots * cots.size, 4 * cots.size + 2 * packets.size),
-        name="node_grads",
-    )(asked, packets, cots)
-
-def unpack_kernel(is_mine, core_ref, packets_ref, *refs):
-    input_ref, output_ref, values, sems = refs[-4:]
+
+def spread(half, packets_ref, input_ref, output_ref, values, sems):
     width = output_ref.shape[1]
     blocks = width // LANES
     chips = packets_ref.shape[0]
     piece = 2 * width // chips
-    half = core_ref[0] if is_mine else 1 - core_ref[0]
 
     def copy(upper, a):
         if not upper:
@@ -485,31 +490,75 @@
         def _():
             copy(True, a).start()
 
-    for a in range(2):
-
-        @pl.when(half == 0)
-        def _():
-            copy(False, a).wait()
-
-        @pl.when(half != 0)
-        def _():
-            copy(True, a).wait()
-
-def unpack(is_mine, core, packets, width, earlier=()):
-    return pl.pallas_call(
-        functools.partial(unpack_kernel, is_mine),
-        in_specs=[smem(), VMEM] + [ANYWHERE] * len(earlier),
-        out_specs=[ANYWHERE] * 2,
+    def finish():
+        for a in range(2):
+
+            @pl.when(half == 0)
+            def _():
+                copy(False, a).wait()
+
+            @pl.when(half != 0)
+            def _():
+                copy(True, a).wait()
+
+    return finish
+
+
+def mine_kernel(core_ref, packets_ref, asked_ref, cots_ref, input_ref, output_ref, nodes_ref, values, sems, *work):
+    finish = spread(core_ref[0], packets_ref, input_ref, output_ref, values, sems)
+    node_sums(asked_ref, packets_ref, cots_ref, nodes_ref, *work)
+    finish()
+
+
+def other_kernel(core_ref, packets_ref, _, __, input_ref, output_ref, values, sems):
+    spread(1 - core_ref[0], packets_ref, input_ref, output_ref, values, sems)()
+
+
+def unpack_mine(core, packets, asked, cots):
+    devices, cap = asked.shape
+    nodes, width = cots.shape
+    slots = devices * cap
+    return pl.pallas_call(
+        mine_kernel,
+        in_specs=[smem(), VMEM, VMEM, VMEM],
+        out_specs=[HBM, HBM, VMEM],
         out_shape=[
             jax.ShapeDtypeStruct((3 * width, width), F32),
             jax.ShapeDtypeStruct((width, width), F32),
-        ],
-        scratch_shapes=[pltpu.VMEM((2 * width, width), F32), pltpu.SemaphoreType.DMA((2,))],
-        input_output_aliases={2 + a: a for a in range(len(earlier))},
+            jax.ShapeDtypeStruct(cots.shape, BF),
+        ],
+        scratch_shapes=[
+            pltpu.VMEM((2 * width, width), F32),
+            pltpu.SemaphoreType.DMA((2,)),
+            pltpu.VMEM((slots * width // LANES, LANES), F32),
+            pltpu.VMEM((slots, width), BF),
+            pltpu.VMEM((slots, nodes), BF),
+        ],
+        compiler_params=pltpu.CompilerParams(vmem_limit_bytes=BIG_VMEM),
+        cost_estimate=cost(2 * slots * cots.size, 6 * packets.size),
+        name="unpack_mine",
+    )(core, packets, asked, cots)
+
+
+def unpack_other(core, packets, grad_input, grad_output):
+    return pl.pallas_call(
+        other_kernel,
+        in_specs=[smem(), VMEM, HBM, HBM],
+        out_specs=[HBM, HBM],
+        out_shape=[
+            jax.ShapeDtypeStruct(grad_input.shape, F32),
+            jax.ShapeDtypeStruct(grad_output.shape, F32),
+        ],
+        scratch_shapes=[
+            pltpu.VMEM((2 * grad_output.shape[0], grad_output.shape[1]), F32),
+            pltpu.SemaphoreType.DMA((2,)),
+        ],
+        input_output_aliases={2: 0, 3: 1},
         compiler_params=pltpu.CompilerParams(vmem_limit_bytes=BIG_VMEM),
         cost_estimate=cost(packets.size, 6 * packets.size),
-        name="unpack_mine" if is_mine else "unpack_other",
-    )(core, packets, *earlier)
+        name="unpack_other",
+    )(core, packets, grad_input, grad_output)
+
 
 def on_device(
     edge_feats,
@@ -556,15 +605,15 @@
     packets = lax.all_to_all(merge(own, got), "chip", split_axis=0, concat_axis=0, tiled=True)
     back_got = lax.ppermute(back_other, both, pairs)
     factor = float(edges * devices) ** (-0.5)
-    pieces, gain = reduce_packets(packets, back_own, back_got, factor)
+    tails = tail_packets(back_own, back_got, packets.shape[1] - 8)
+    pieces, gain = reduce_packets(packets, tails, factor)
     d_preact, pieces = lax.optimization_barrier((d_preact, pieces))
     mine = lax.all_to_all(pieces, "chip", split_axis=0, concat_axis=0, tiled=True)
     grad_edges = grad_pass(d_preact, w_input, edge_cot, 1024)
     grad_edges, mine = lax.optimization_barrier((grad_edges, mine))
     partner = lax.ppermute(mine, both, pairs)
-    grad_nodes = node_grads(asked, mine, node_cot)
-    grads = unpack(True, core, mine, width)
-    grad_input, grad_output = unpack(False, core, partner, width, grads)
+    grad_input, grad_output, grad_nodes = unpack_mine(core, mine, asked, node_cot)
+    grad_input, grad_output = unpack_other(core, partner, grad_input, grad_output)
     return (
         grad_edges,
         grad_nodes,

time: 131 us -> 131 us (level)
  no operation moved by 1% of the time
where the time goes in v5:
time: 131 us
  Pallas kernels  44.4 us (34%)
  waiting for transfers between devices  40.3 us (31%)
  blocking collectives  20.7 us (16%)
  starting transfers between devices  20.6 us (16%)
  local copies, waits for them, and re-layouts  2.99 us (2%)
    all_to_all x1, blocking collectives, on_device(): lax.all_to_all(requests.reshape(devices, 1, cap), both, split_axis=0, con...  20.7 us
    pallas_call x1, Pallas kernels, edge_pass(): pl.pallas_call(functools.partial(edge_kernel, cap), in_specs=[smem()] + [...  20.4 us
    all_to_all x1, waiting for transfers between devices, on_device(): lax.all_to_all(merge(own, got), 'chip', split_axis=0, concat_axis=0, tile...  15.2 us
    all_to_all x1, waiting for transfers between devices, on_device(): lax.all_to_all(pieces, 'chip', split_axis=0, concat_axis=0, tiled=True)  13.3 us
    all_to_all x1, waiting for transfers between devices, on_device(): lax.all_to_all(picked, both, split_axis=0, concat_axis=0, tiled=True)  8.7 us
    pallas_call x1, Pallas kernels, grad_pass(): pl.pallas_call(grad_kernel, grid=(edges // tile,), in_specs=[tiles, pl.Bl...  6.5 us
    pallas_call x1, Pallas kernels, prep_pass(): pl.pallas_call(prep_kernel, grid=(tiles,), in_specs=[rows, pl.BlockSpec((...  6.07 us
    all_to_all x1, starting transfers between devices, on_device(): lax.all_to_all(pieces, 'chip', split_axis=0, concat_axis=0, tiled=True)  5.34 us
  transfers between devices with their start and end apart: 6, of which 6 were waited for; matrix products, arithmetic and copies ran while one was open for 0% of the time, Pallas kernels for 12%

profile of v5, /device:TPU:1, one launch (start us, length us, event | category | flops | bytes accessed | tf_op | source)
XLA Modules:
  0.0 130.7 jit_solution(15229827954423355841)
XLA Ops:
  0.6 0.7 reduce
  1.5 20.7 %all_to_all.20 = s32[128,1,3]{2,1,0:T(1,128)S(1)} all-to-all(s32[128,1,3]{2,1,0:T(1,128)S(1)} %bitcast.13), channel_id=1, replica_groups=mesh['chip'=64,'core'=2] {'chip','core'}, dimensions={0} | all-to-all | bytes 3072 | tf_op jit(solution)/shard_map/all_to_all | solution.py:583
  22.2 2.8 %pick_rows.1 = bf16[3072,128]{1,0:T(8,128)(2,1)} custom-call(s32[128,3]{1,0:T(8,128)S(1)} %bitcast.9, bf16[320,512]{1,0:T(8,128)(2,1)} %feats_hbm.1, bf16[320,512]{1,0:T(8,128)(2,1)} %cots_ref.1), custom_call_target="tpu_custom_call" | custom-call | flops 251658240 | bytes 1572864 | tf_op jit(solution)/shard_map/pick_rows/pallas_call | solution.py:65
  25.0 4.8 %all-to-all-start.1 = ((bf16[128,24,128]{2,1,0:T(8,128)(2,1)}), bf16[128,24,128]{2,1,0:T(8,128)(2,1)S(1)}, u32[]{:S(2)}, u32[]{:S(2)}) async-start(bf16[128,24,128]{2,1,0:T(8,128)(2,1)} %bitcast.4), calls=%async_computation.1 | async-start | bytes 1572864 | tf_op jit(solution)/shard_map/all_to_all | solution.py:587
  29.8 6.1 %prep_pass.1 = (f32[3072,512]{1,0:T(8,128)}, bf16[4,512,768]{2,1,0:T(8,128)(2,1)S(1)}) custom-call(bf16[3072,512]{1,0:T(8,128)(2,1)} %feats_ref.1, bf16[3,512,512]{2,1,0:T(8,128)(2,1)S(1)} %copy-done.1), custom_call_target="tpu_custom_call" | custom-call | flops 1610612736 | bytes 12582912 | tf_op jit(solution)/shard_map/prep_pass/pallas_call | solution.py:98
  35.9 1.7 %copy-done.7 = bf16[4,512,768]{2,1,0:T(8,128)(2,1)} copy-done((bf16[4,512,768]{2,1,0:T(8,128)(2,1)}, bf16[4,512,768]{2,1,0:T(8,128)(2,1)S(1)}, u32[]{:S(2)}) %copy-start.7) | copy-done | bytes 3145752
  37.6 8.7 %all-to-all-done.1 = bf16[128,24,128]{2,1,0:T(8,128)(2,1)S(1)} async-done(((bf16[128,24,128]{2,1,0:T(8,128)(2,1)}), bf16[128,24,128]{2,1,0:T(8,128)(2,1)S(1)}, u32[]{:S(2)}, u32[]{:S(2)}) %all-to-all-start.1) | async-done | bytes 786464 | tf_op jit(solution)/shard_map/all_to_all | solution.py:587
  46.3 20.4 %edge_pass.1 = (bf16[3072,512]{1,0:T(8,128)(2,1)}, bf16[64,72,128]{2,1,0:T(8,128)(2,1)S(1)}, bf16[64,72,128]{2,1,0:T(8,128)(2,1)S(1)}, bf16[768,512]{1,0:T(8,128)(2,1)S(1)}) custom-call(s32[1]{0:T(128)} %bitcast.core_ref, s32[24,128]{1,0:T(8,128)S(1)} %copy-done.4, s32[24,128]{1,0:T(8,128)S(1)} %copy-done.5, f32[1,512]{1,0:T(1,128)S(1)} %bitcast.11, ...), custom_call_target="tpu_custom_call" | custom-call | flops 12884901888 | bytes 12582912 | tf_op jit(solution)/shard_map/edge_pass/pallas_call | solution.py:308
  66.7 1.2 collective-permute-start
  67.9 0.9 back_rows.1
  68.9 1.6 %collective-permute-done.got_ref = bf16[64,72,128]{2,1,0:T(8,128)(2,1)S(1)} collective-permute-done((bf16[64,72,128]{2,1,0:T(8,128)(2,1)S(1)}, bf16[64,72,128]{2,1,0:T(8,128)(2,1)S(1)}, u32[]{:S(2)}, u32[]{:S(2)}) %collective-permute-start) | collective-permute-done | bytes 1179680 | tf_op jit(solution)/shard_map/ppermute | solution.py:602
  70.4 1.3 merge.1
  71.7 4.7 %all-to-all-start.2 = ((bf16[64,72,128]{2,1,0:T(8,128)(2,1)}), bf16[64,72,128]{2,1,0:T(8,128)(2,1)S(1)}, u32[]{:S(2)}, u32[]{:S(2)}) async-start(bf16[64,72,128]{2,1,0:T(8,128)(2,1)} %merge.1), calls=%async_computation.2 | async-start | bytes 2359296 | tf_op jit(solution)/shard_map/all_to_all | solution.py:605
  76.4 0.6 collective-permute-start.1
  77.0 1.3 %collective-permute-done.1.got_ref = bf16[64,24,128]{2,1,0:T(8,128)(2,1)S(1)} collective-permute-done((bf16[64,24,128]{2,1,0:T(8,128)(2,1)S(1)}, bf16[64,24,128]{2,1,0:T(8,128)(2,1)S(1)}, u32[]{:S(2)}, u32[]{:S(2)}) %collective-permute-start.1) | collective-permute-done | bytes 393248 | tf_op jit(solution)/shard_map/ppermute | solution.py:606
  78.4 1.1 copy-done
  79.5 15.2 %all-to-all-done.2.in_ref = bf16[64,72,128]{2,1,0:T(8,128)(2,1)S(1)} async-done(((bf16[64,72,128]{2,1,0:T(8,128)(2,1)}), bf16[64,72,128]{2,1,0:T(8,128)(2,1)S(1)}, u32[]{:S(2)}, u32[]{:S(2)}) %all-to-all-start.2) | async-done | bytes 1179680 | tf_op jit(solution)/shard_map/all_to_all | solution.py:605
  94.7 2.3 %reduce_packets.1 = (bf16[64,88,128]{2,1,0:T(8,128)(2,1)}, f32[1,512]{1,0:T(1,128)}) custom-call(bf16[64,72,128]{2,1,0:T(8,128)(2,1)S(1)} %all-to-all-done.2.in_ref, bf16[64,88,128]{2,1,0:T(8,128)(2,1)} %copy-done), custom_call_target="tpu_custom_call", output_to_operand_aliasing={{0}: (1, {})} | custom-call | flops 589824 | bytes 2359296 | tf_op jit(solution)/shard_map/reduce_packets/pallas_call | solution.py:431
  97.0 5.3 %all-to-all-start.3 = ((bf16[64,88,128]{2,1,0:T(8,128)(2,1)}), bf16[64,88,128]{2,1,0:T(8,128)(2,1)S(1)}, u32[]{:S(2)}, u32[]{:S(2)}) async-start(bf16[64,88,128]{2,1,0:T(8,128)(2,1)} %get-tuple-element.40), calls=%async_computation.3 | async-start | bytes 2883584 | tf_op jit(solution)/shard_map/all_to_all | solution.py:611
  102.4 6.5 %grad_pass.1 = bf16[3072,512]{1,0:T(8,128)(2,1)} custom-call(bf16[3072,512]{1,0:T(8,128)(2,1)} %get-tuple-element.39.d_preact_ref, bf16[3,512,512]{2,1,0:T(8,128)(2,1)} %w_ref.5, bf16[3072,512]{1,0:T(8,128)(2,1)} %cot_ref.1), custom_call_target="tpu_custom_call" | custom-call | flops 1610612736 | bytes 9437184 | tf_op jit(solution)/shard_map/grad_pass/pallas_call | solution.py:119
  108.9 13.3 %all-to-all-done.3.packets_ref = bf16[64,88,128]{2,1,0:T(8,128)(2,1)S(1)} async-done(((bf16[64,88,128]{2,1,0:T(8,128)(2,1)}), bf16[64,88,128]{2,1,0:T(8,128)(2,1)S(1)}, u32[]{:S(2)}, u32[]{:S(2)}) %all-to-all-start.3) | async-done | bytes 1441824 | tf_op jit(solution)/shard_map/all_to_all | solution.py:611
  122.2 4.0 %collective-permute-start.2 = (bf16[64,88,128]{2,1,0:T(8,128)(2,1)S(1)}, bf16[64,88,128]{2,1,0:T(8,128)(2,1)S(1)}, u32[]{:S(2)}, u32[]{:S(2)}) collective-permute-start(bf16[64,88,128]{2,1,0:T(8,128)(2,1)S(1)} %all-to-all-done.3.packets_ref), channel_id=1, source_target_pairs={{0,1},{1,0},{2,3},{3,2},{4,5},{5,4},{6,7},{7,6},{8,9},{9,8},{10,11... | collective-permute-start | bytes 4325384 | tf_op jit(solution)/shard_map/ppermute | solution.py:614
  126.2 2.7 %unpack_mine.1 = (f32[1536,512]{1,0:T(8,128)}, f32[512,512]{1,0:T(8,128)}, bf16[320,512]{1,0:T(8,128)(2,1)}) custom-call(s32[1]{0:T(128)} %bitcast.core_ref, bf16[64,88,128]{2,1,0:T(8,128)(2,1)S(1)} %all-to-all-done.3.packets_ref, s32[128,3]{1,0:T(8,128)S(1)} %bitcast.10, bf16[320,512]{1,0:T(8,128)(2,1)S(1)} %copy-done.2), custom_call_target="tpu_custom_call" | custom-call | flops 125829120 | bytes 4325376 | tf_op jit(solution)/shard_map/unpack_mine/pallas_call | solution.py:521
  129.0 1.5 %unpack_other.1 = (f32[1536,512]{1,0:T(8,128)}, f32[512,512]{1,0:T(8,128)}) custom-call(s32[1]{0:T(128)} %bitcast.core_ref, bf16[64,88,128]{2,1,0:T(8,128)(2,1)S(1)} %collective-permute-done.2.packets_ref, f32[1536,512]{1,0:T(8,128)} %get-tuple-element.44._, f32[512,512]{1,0:T(8,128)} %get-tuple-element.45.__), custom_call_target="tpu_custom_call", output_to_operand_aliasing={{0}: (2, {}), {1}: (3, {})} | custom-call | flops 720896 | bytes 4325376 | tf_op jit(solution)/shard_map/unpack_other/pallas_call | solution.py:544
  (17 shorter events, 0.5 us)
Async XLA Ops:
  22.2 7.6 %copy-start.1 = (bf16[3,512,512]{2,1,0:T(8,128)(2,1)S(1)}, bf16[3,512,512]{2,1,0:T(8,128)(2,1)}, u32[]{:S(2)}) copy-start(bf16[3,512,512]{2,1,0:T(8,128)(2,1)} %w_ref.5) | copy-start | bytes 4718596
  25.0 21.3 %all-to-all-start.1 = ((bf16[128,24,128]{2,1,0:T(8,128)(2,1)}), bf16[128,24,128]{2,1,0:T(8,128)(2,1)S(1)}, u32[]{:S(2)}, u32[]{:S(2)}) async-start(bf16[128,24,128]{2,1,0:T(8,128)(2,1)} %bitcast.4), calls=%async_computation.1 | async-start | bytes 1572864 | tf_op jit(solution)/shard_map/all_to_all | solution.py:587
  29.8 16.5 %copy-start.3 = (bf16[512,512]{1,0:T(8,128)(2,1)S(1)}, bf16[512,512]{1,0:T(8,128)(2,1)}, u32[]{:S(2)}) copy-start(bf16[512,512]{1,0:T(8,128)(2,1)} %w_out.1) | copy-start | bytes 1572868
  29.8 16.5 %copy-start.4 = (s32[24,128]{1,0:T(8,128)S(1)}, s32[24,128]{1,0:T(8,128)}, u32[]{:S(2)}) copy-start(s32[24,128]{1,0:T(8,128)} %send_ref.1) | copy-start | bytes 36868
  29.8 16.5 %copy-start.5 = (s32[24,128]{1,0:T(8,128)S(1)}, s32[24,128]{1,0:T(8,128)}, u32[]{:S(2)}) copy-start(s32[24,128]{1,0:T(8,128)} %recv_ref.1) | copy-start | bytes 36868
  29.8 16.5 %copy-start.6 = (f32[512]{0:T(512)S(1)}, f32[512]{0:T(512)}, u32[]{:S(2)}) copy-start(f32[512]{0:T(512)} %param.19) | copy-start | bytes 6148
  35.9 1.7 %copy-start.7 = (bf16[4,512,768]{2,1,0:T(8,128)(2,1)}, bf16[4,512,768]{2,1,0:T(8,128)(2,1)S(1)}, u32[]{:S(2)}) copy-start(bf16[4,512,768]{2,1,0:T(8,128)(2,1)S(1)} %get-tuple-element.28.turned_hbm) | copy-start | bytes 9437188
  66.7 3.7 %collective-permute-start = (bf16[64,72,128]{2,1,0:T(8,128)(2,1)S(1)}, bf16[64,72,128]{2,1,0:T(8,128)(2,1)S(1)}, u32[]{:S(2)}, u32[]{:S(2)}) collective-permute-start(bf16[64,72,128]{2,1,0:T(8,128)(2,1)S(1)} %get-tuple-element.31), channel_id=1, source_target_pairs={{0,1},{1,0},{2,3},{3,2},{4,5},{5,4},{6,7},{7,6},{8,9},{9,8},{10,11... | collective-permute-start | bytes 3538952 | tf_op jit(solution)/shard_map/ppermute | solution.py:602
  71.7 23.0 %all-to-all-start.2 = ((bf16[64,72,128]{2,1,0:T(8,128)(2,1)}), bf16[64,72,128]{2,1,0:T(8,128)(2,1)S(1)}, u32[]{:S(2)}, u32[]{:S(2)}) async-start(bf16[64,72,128]{2,1,0:T(8,128)(2,1)} %merge.1), calls=%async_computation.2 | async-start | bytes 2359296 | tf_op jit(solution)/shard_map/all_to_all | solution.py:605
  76.4 2.0 %collective-permute-start.1 = (bf16[64,24,128]{2,1,0:T(8,128)(2,1)S(1)}, bf16[64,24,128]{2,1,0:T(8,128)(2,1)S(1)}, u32[]{:S(2)}, u32[]{:S(2)}) collective-permute-start(bf16[64,24,128]{2,1,0:T(8,128)(2,1)S(1)} %get-tuple-element.37), channel_id=1, source_target_pairs={{0,1},{1,0},{2,3},{3,2},{4,5},{5,4},{6,7},{7,6},{8,9},{9,8},{10,11... | collective-permute-start | bytes 1179656 | tf_op jit(solution)/shard_map/ppermute | solution.py:606
  78.4 1.1 copy-start
  97.0 25.2 %all-to-all-start.3 = ((bf16[64,88,128]{2,1,0:T(8,128)(2,1)}), bf16[64,88,128]{2,1,0:T(8,128)(2,1)S(1)}, u32[]{:S(2)}, u32[]{:S(2)}) async-start(bf16[64,88,128]{2,1,0:T(8,128)(2,1)} %get-tuple-element.40), calls=%async_computation.3 | async-start | bytes 2883584 | tf_op jit(solution)/shard_map/all_to_all | solution.py:611
  102.4 23.8 %copy-start.2 = (bf16[320,512]{1,0:T(8,128)(2,1)S(1)}, bf16[320,512]{1,0:T(8,128)(2,1)}, u32[]{:S(2)}) copy-start(bf16[320,512]{1,0:T(8,128)(2,1)} %cots_ref.1) | copy-start | bytes 983044
  122.2 6.8 %collective-permute-start.2 = (bf16[64,88,128]{2,1,0:T(8,128)(2,1)S(1)}, bf16[64,88,128]{2,1,0:T(8,128)(2,1)S(1)}, u32[]{:S(2)}, u32[]{:S(2)}) collective-permute-start(bf16[64,88,128]{2,1,0:T(8,128)(2,1)S(1)} %all-to-all-done.3.packets_ref), channel_id=1, source_target_pairs={{0,1},{1,0},{2,3},{3,2},{4,5},{5,4},{6,7},{7,6},{8,9},{9,8},{10,11... | collective-permute-start | bytes 4325384 | tf_op jit(solution)/shard_map/ppermute | solution.py:614

commit v6 on v5

--- a/solution.py
+++ b/solution.py
@@ -35,48 +35,62 @@
 def one_hot(left, right):
     return jnp.where(left == right, 1.0, 0.0).astype(BF)
 
-def pick_kernel(asked_ref, feats_hbm, cots_hbm, out_ref, feats, cots, rows, sems):
-    devices, cap = asked_ref.shape
-    nodes, width = feats.shape
-    blocks = width // LANES
-    per = cap * 2 * blocks
+def stage_kernel(feats_hbm, cots_hbm, feats_ref, cots_ref, sems):
     copies = [
-        pltpu.make_async_copy(feats_hbm, feats, sems.at[0]),
-        pltpu.make_async_copy(cots_hbm, cots, sems.at[1]),
+        pltpu.make_async_copy(feats_hbm, feats_ref, sems.at[0]),
+        pltpu.make_async_copy(cots_hbm, cots_ref, sems.at[1]),
     ]
     for copy in copies:
         copy.start()
+    for copy in copies:
+        copy.wait()
+
+
+def stage(feats, cots):
+    return pl.pallas_call(
+        stage_kernel,
+        in_specs=[HBM, HBM],
+        out_specs=[VMEM, VMEM],
+        out_shape=[jax.ShapeDtypeStruct(feats.shape, BF), jax.ShapeDtypeStruct(cots.shape, BF)],
+        scratch_shapes=[pltpu.SemaphoreType.DMA((2,))],
+        compiler_params=pltpu.CompilerParams(vmem_limit_bytes=BIG_VMEM),
+        cost_estimate=cost(0, 8 * feats.size),
+        name="stage",
+    )(in_hbm(feats), in_hbm(cots))
+
+
+def pick_kernel(asked_ref, feats_ref, cots_ref, out_ref, rows):
+    devices, cap = asked_ref.shape
+    nodes, width = feats_ref.shape
+    blocks = width // LANES
+    per = cap * 2 * blocks
     spot = lax.broadcasted_iota(jnp.int32, (devices, nodes), 1)
-    hots = [one_hot(asked_ref[:, k : k + 1], spot) for k in range(cap)]
-    for at, table in enumerate((feats, cots)):
-        copies[at].wait()
-        for k in range(cap):
-            found = dot(hots[k], table[...])
+    for k in range(cap):
+        hot = one_hot(asked_ref[:, k : k + 1], spot)
+        for at, table in enumerate((feats_ref, cots_ref)):
+            found = dot(hot, table[...])
             for j in range(blocks):
                 rows[pl.ds(k * 2 * blocks + at * blocks + j, devices, stride=per), :] = found[
                     :, j * LANES : (j + 1) * LANES
                 ]
     out_ref[...] = rows[...].astype(BF)
 
+
 def pick_rows(asked, feats, cots):
     devices, cap = asked.shape
     width = feats.shape[1]
     total = devices * cap * 2 * width // LANES
     return pl.pallas_call(
         pick_kernel,
-        in_specs=[VMEM, HBM, HBM],
+        in_specs=[VMEM] * 3,
         out_specs=VMEM,
         out_shape=jax.ShapeDtypeStruct((total, LANES), BF),
-        scratch_shapes=[
-            pltpu.VMEM(feats.shape, BF),
-            pltpu.VMEM(cots.shape, BF),
-            pltpu.VMEM((total, LANES), F32),
-            pltpu.SemaphoreType.DMA((2,)),
-        ],
+        scratch_shapes=[pltpu.VMEM((total, LANES), F32)],
         compiler_params=pltpu.CompilerParams(vmem_limit_bytes=BIG_VMEM),
         cost_estimate=cost(4 * devices * cap * feats.size, 4 * total * LANES),
         name="pick_rows",
-    )(asked, in_hbm(feats), in_hbm(cots))
+    )(asked, feats, cots)
+
 
 def slot_ids(position, chips, cap):
     half = cap * chips
@@ -583,7 +597,7 @@
     asked = lax.all_to_all(
         requests.reshape(devices, 1, cap), both, split_axis=0, concat_axis=0, tiled=True
     ).reshape(devices, cap)
-    picked = pick_rows(asked, node_feats, node_cot).reshape(devices, -1, LANES)
+    picked = pick_rows(asked, *stage(node_feats, node_cot)).reshape(devices, -1, LANES)
     rows = lax.all_to_all(picked, both, split_axis=0, concat_axis=0, tiled=True).reshape(-1, LANES)
     pre, turned = prep_pass(edge_feats, w_input, TILE)
     d_preact, own, other, sums = edge_pass(

time: 131 us -> 131 us (level)
  blocking collectives: 20.7 us -> 0 us
  starting transfers between devices: 20.6 us -> 32.1 us
  waiting for transfers between devices: 40.3 us -> 48.5 us
    all_to_all x1 -> x0, blocking collectives: 20.7 us -> none  [on_device(): lax.all_to_all(requests.reshape(devices, 1, cap), both, split_axis=0, con...]
    all_to_all x0 -> x1, starting transfers between devices: none -> 11.5 us  [on_device(): lax.all_to_all(requests.reshape(devices, 1, cap), both, split_axis=0, con...]
    all_to_all x0 -> x1, waiting for transfers between devices: none -> 8.17 us  [on_device(): lax.all_to_all(requests.reshape(devices, 1, cap), both, split_axis=0, con...]
    pallas_call x1 -> x2, Pallas kernels: 2.8 us -> 2.64 us  [the longest x1 1.54 us: pick_rows(): pl.pallas_call(pick_kernel, in_specs=[VMEM] * 3, out_specs=VMEM, out_shap...]
  transfers between devices with their start and end apart: 6 -> 7, of which waited for: 6 -> 7; matrix products, arithmetic and copies ran while one was open for 0% -> 0% of each run, Pallas kernels for 12% -> 13%
where the time goes in v6:
time: 131 us; the launch traced here: 130 us
  waiting for transfers between devices  48.5 us (37%)
  Pallas kernels  44.3 us (34%)
  starting transfers between devices  32.1 us (25%)
  local copies, waits for them, and re-layouts  3.63 us (3%)
    pallas_call x1, Pallas kernels, edge_pass(): pl.pallas_call(functools.partial(edge_kernel, cap), in_specs=[smem()] + [...  20.4 us
    all_to_all x1, waiting for transfers between devices, on_device(): lax.all_to_all(merge(own, got), 'chip', split_axis=0, concat_axis=0, tile...  15.2 us
    all_to_all x1, waiting for transfers between devices, on_device(): lax.all_to_all(pieces, 'chip', split_axis=0, concat_axis=0, tiled=True)  13.3 us
    all_to_all x1, starting transfers between devices, on_device(): lax.all_to_all(requests.reshape(devices, 1, cap), both, split_axis=0, con...  11.5 us
    all_to_all x1, waiting for transfers between devices, on_device(): lax.all_to_all(picked, both, split_axis=0, concat_axis=0, tiled=True)  8.71 us
    all_to_all x1, waiting for transfers between devices, on_device(): lax.all_to_all(requests.reshape(devices, 1, cap), both, split_axis=0, con...  8.17 us
    pallas_call x1, Pallas kernels, grad_pass(): pl.pallas_call(grad_kernel, grid=(edges // tile,), in_specs=[tiles, pl.Bl...  6.5 us
    pallas_call x1, Pallas kernels, prep_pass(): pl.pallas_call(prep_kernel, grid=(tiles,), in_specs=[rows, pl.BlockSpec((...  6.05 us
  transfers between devices with their start and end apart: 7, of which 7 were waited for; matrix products, arithmetic and copies ran while one was open for 0% of the time, Pallas kernels for 13%

profile of v6, /device:TPU:1, one launch (start us, length us, event | category | flops | bytes accessed | tf_op | source)
XLA Modules:
  0.0 130.1 jit_solution(6347411076464488052)
XLA Ops:
  2.2 11.5 %all-to-all-start = ((s32[128,1,3]{2,1,0:T(1,128)}), s32[128,1,3]{2,1,0:T(1,128)S(1)}, u32[]{:S(2)}, u32[]{:S(2)}) async-start(s32[128,1,3]{2,1,0:T(1,128)} %bitcast.2), calls=%async_computation | async-start | bytes 131072 | tf_op jit(solution)/shard_map/all_to_all | solution.py:597
  13.7 1.1 stage.1
  14.8 8.2 %all-to-all-done = s32[128,1,3]{2,1,0:T(1,128)S(1)} async-done(((s32[128,1,3]{2,1,0:T(1,128)}), s32[128,1,3]{2,1,0:T(1,128)S(1)}, u32[]{:S(2)}, u32[]{:S(2)}) %all-to-all-start) | async-done | bytes 1568 | tf_op jit(solution)/shard_map/all_to_all | solution.py:597
  23.0 1.5 %pick_rows.1 = bf16[3072,128]{1,0:T(8,128)(2,1)} custom-call(s32[128,3]{1,0:T(8,128)S(1)} %bitcast.9, bf16[320,512]{1,0:T(8,128)(2,1)S(1)} %get-tuple-element.29.feats_ref, bf16[320,512]{1,0:T(8,128)(2,1)S(1)} %get-tuple-element.30.cots_ref), custom_call_target="tpu_custom_call" | custom-call | flops 251658240 | bytes 1572864 | tf_op jit(solution)/shard_map/pick_rows/pallas_call | solution.py:83
  24.5 4.8 %all-to-all-start.1 = ((bf16[128,24,128]{2,1,0:T(8,128)(2,1)}), bf16[128,24,128]{2,1,0:T(8,128)(2,1)S(1)}, u32[]{:S(2)}, u32[]{:S(2)}) async-start(bf16[128,24,128]{2,1,0:T(8,128)(2,1)} %bitcast.4), calls=%async_computation.1 | async-start | bytes 1572864 | tf_op jit(solution)/shard_map/all_to_all | solution.py:601
  29.3 6.1 %prep_pass.1 = (f32[3072,512]{1,0:T(8,128)}, bf16[4,512,768]{2,1,0:T(8,128)(2,1)S(1)}) custom-call(bf16[3072,512]{1,0:T(8,128)(2,1)} %feats_ref.1, bf16[3,512,512]{2,1,0:T(8,128)(2,1)S(1)} %copy-done.1), custom_call_target="tpu_custom_call" | custom-call | flops 1610612736 | bytes 12582912 | tf_op jit(solution)/shard_map/prep_pass/pallas_call | solution.py:112
  35.4 1.7 %copy-done.7 = bf16[4,512,768]{2,1,0:T(8,128)(2,1)} copy-done((bf16[4,512,768]{2,1,0:T(8,128)(2,1)}, bf16[4,512,768]{2,1,0:T(8,128)(2,1)S(1)}, u32[]{:S(2)}) %copy-start.7) | copy-done | bytes 3145752
  37.0 8.7 %all-to-all-done.1 = bf16[128,24,128]{2,1,0:T(8,128)(2,1)S(1)} async-done(((bf16[128,24,128]{2,1,0:T(8,128)(2,1)}), bf16[128,24,128]{2,1,0:T(8,128)(2,1)S(1)}, u32[]{:S(2)}, u32[]{:S(2)}) %all-to-all-start.1) | async-done | bytes 786464 | tf_op jit(solution)/shard_map/all_to_all | solution.py:601
  45.8 20.4 %edge_pass.1 = (bf16[3072,512]{1,0:T(8,128)(2,1)}, bf16[64,72,128]{2,1,0:T(8,128)(2,1)S(1)}, bf16[64,72,128]{2,1,0:T(8,128)(2,1)S(1)}, bf16[768,512]{1,0:T(8,128)(2,1)S(1)}) custom-call(s32[1]{0:T(128)} %bitcast.core_ref, s32[24,128]{1,0:T(8,128)S(1)} %copy-done.4, s32[24,128]{1,0:T(8,128)S(1)} %copy-done.5, f32[1,512]{1,0:T(1,128)S(1)} %bitcast.11, ...), custom_call_target="tpu_custom_call" | custom-call | flops 12884901888 | bytes 12582912 | tf_op jit(solution)/shard_map/edge_pass/pallas_call | solution.py:322
  66.2 1.2 collective-permute-start
  67.4 0.9 back_rows.1
  68.3 1.6 %collective-permute-done.got_ref = bf16[64,72,128]{2,1,0:T(8,128)(2,1)S(1)} collective-permute-done((bf16[64,72,128]{2,1,0:T(8,128)(2,1)S(1)}, bf16[64,72,128]{2,1,0:T(8,128)(2,1)S(1)}, u32[]{:S(2)}, u32[]{:S(2)}) %collective-permute-start) | collective-permute-done | bytes 1179680 | tf_op jit(solution)/shard_map/ppermute | solution.py:616
  69.9 1.3 merge.1
  71.2 4.7 %all-to-all-start.2 = ((bf16[64,72,128]{2,1,0:T(8,128)(2,1)}), bf16[64,72,128]{2,1,0:T(8,128)(2,1)S(1)}, u32[]{:S(2)}, u32[]{:S(2)}) async-start(bf16[64,72,128]{2,1,0:T(8,128)(2,1)} %merge.1), calls=%async_computation.2 | async-start | bytes 2359296 | tf_op jit(solution)/shard_map/all_to_all | solution.py:619
  76.4 1.3 %collective-permute-done.1.got_ref = bf16[64,24,128]{2,1,0:T(8,128)(2,1)S(1)} collective-permute-done((bf16[64,24,128]{2,1,0:T(8,128)(2,1)S(1)}, bf16[64,24,128]{2,1,0:T(8,128)(2,1)S(1)}, u32[]{:S(2)}, u32[]{:S(2)}) %collective-permute-start.1) | collective-permute-done | bytes 393248 | tf_op jit(solution)/shard_map/ppermute | solution.py:620
  77.9 1.1 copy-done
  79.0 15.2 %all-to-all-done.2.in_ref = bf16[64,72,128]{2,1,0:T(8,128)(2,1)S(1)} async-done(((bf16[64,72,128]{2,1,0:T(8,128)(2,1)}), bf16[64,72,128]{2,1,0:T(8,128)(2,1)S(1)}, u32[]{:S(2)}, u32[]{:S(2)}) %all-to-all-start.2) | async-done | bytes 1179680 | tf_op jit(solution)/shard_map/all_to_all | solution.py:619
  94.2 2.3 %reduce_packets.1 = (bf16[64,88,128]{2,1,0:T(8,128)(2,1)}, f32[1,512]{1,0:T(1,128)}) custom-call(bf16[64,72,128]{2,1,0:T(8,128)(2,1)S(1)} %all-to-all-done.2.in_ref, bf16[64,88,128]{2,1,0:T(8,128)(2,1)} %copy-done), custom_call_target="tpu_custom_call", output_to_operand_aliasing={{0}: (1, {})} | custom-call | flops 589824 | bytes 2359296 | tf_op jit(solution)/shard_map/reduce_packets/pallas_call | solution.py:445
  96.5 5.3 %all-to-all-start.3 = ((bf16[64,88,128]{2,1,0:T(8,128)(2,1)}), bf16[64,88,128]{2,1,0:T(8,128)(2,1)S(1)}, u32[]{:S(2)}, u32[]{:S(2)}) async-start(bf16[64,88,128]{2,1,0:T(8,128)(2,1)} %get-tuple-element.44), calls=%async_computation.3 | async-start | bytes 2883584 | tf_op jit(solution)/shard_map/all_to_all | solution.py:625
  101.9 6.5 %grad_pass.1 = bf16[3072,512]{1,0:T(8,128)(2,1)} custom-call(bf16[3072,512]{1,0:T(8,128)(2,1)} %get-tuple-element.43.d_preact_ref, bf16[3,512,512]{2,1,0:T(8,128)(2,1)} %w_ref.5, bf16[3072,512]{1,0:T(8,128)(2,1)} %cot_ref.1), custom_call_target="tpu_custom_call" | custom-call | flops 1610612736 | bytes 9437184 | tf_op jit(solution)/shard_map/grad_pass/pallas_call | solution.py:133
  108.3 13.3 %all-to-all-done.3.packets_ref = bf16[64,88,128]{2,1,0:T(8,128)(2,1)S(1)} async-done(((bf16[64,88,128]{2,1,0:T(8,128)(2,1)}), bf16[64,88,128]{2,1,0:T(8,128)(2,1)S(1)}, u32[]{:S(2)}, u32[]{:S(2)}) %all-to-all-start.3) | async-done | bytes 1441824 | tf_op jit(solution)/shard_map/all_to_all | solution.py:625
  121.7 4.0 %collective-permute-start.2 = (bf16[64,88,128]{2,1,0:T(8,128)(2,1)S(1)}, bf16[64,88,128]{2,1,0:T(8,128)(2,1)S(1)}, u32[]{:S(2)}, u32[]{:S(2)}) collective-permute-start(bf16[64,88,128]{2,1,0:T(8,128)(2,1)S(1)} %all-to-all-done.3.packets_ref), channel_id=1, source_target_pairs={{0,1},{1,0},{2,3},{3,2},{4,5},{5,4},{6,7},{7,6},{8,9},{9,8},{10,11... | collective-permute-start | bytes 4325384 | tf_op jit(solution)/shard_map/ppermute | solution.py:628
  125.6 2.7 %unpack_mine.1 = (f32[1536,512]{1,0:T(8,128)}, f32[512,512]{1,0:T(8,128)}, bf16[320,512]{1,0:T(8,128)(2,1)}) custom-call(s32[1]{0:T(128)} %bitcast.core_ref, bf16[64,88,128]{2,1,0:T(8,128)(2,1)S(1)} %all-to-all-done.3.packets_ref, s32[128,3]{1,0:T(8,128)S(1)} %bitcast.10, bf16[320,512]{1,0:T(8,128)(2,1)S(1)} %copy-done.2), custom_call_target="tpu_custom_call" | custom-call | flops 125829120 | bytes 4325376 | tf_op jit(solution)/shard_map/unpack_mine/pallas_call | solution.py:535
  128.5 1.5 %unpack_other.1 = (f32[1536,512]{1,0:T(8,128)}, f32[512,512]{1,0:T(8,128)}) custom-call(s32[1]{0:T(128)} %bitcast.core_ref, bf16[64,88,128]{2,1,0:T(8,128)(2,1)S(1)} %collective-permute-done.2.packets_ref, f32[1536,512]{1,0:T(8,128)} %get-tuple-element.48._, f32[512,512]{1,0:T(8,128)} %get-tuple-element.49.__), custom_call_target="tpu_custom_call", output_to_operand_aliasing={{0}: (2, {}), {1}: (3, {})} | custom-call | flops 720896 | bytes 4325376 | tf_op jit(solution)/shard_map/unpack_other/pallas_call | solution.py:558
  (19 shorter events, 2.4 us)
Async XLA Ops:
  2.2 20.8 %all-to-all-start = ((s32[128,1,3]{2,1,0:T(1,128)}), s32[128,1,3]{2,1,0:T(1,128)S(1)}, u32[]{:S(2)}, u32[]{:S(2)}) async-start(s32[128,1,3]{2,1,0:T(1,128)} %bitcast.2), calls=%async_computation | async-start | bytes 131072 | tf_op jit(solution)/shard_map/all_to_all | solution.py:597
  14.8 14.5 %copy-start.1 = (bf16[3,512,512]{2,1,0:T(8,128)(2,1)S(1)}, bf16[3,512,512]{2,1,0:T(8,128)(2,1)}, u32[]{:S(2)}) copy-start(bf16[3,512,512]{2,1,0:T(8,128)(2,1)} %w_ref.5) | copy-start | bytes 4718596
  24.5 21.3 %all-to-all-start.1 = ((bf16[128,24,128]{2,1,0:T(8,128)(2,1)}), bf16[128,24,128]{2,1,0:T(8,128)(2,1)S(1)}, u32[]{:S(2)}, u32[]{:S(2)}) async-start(bf16[128,24,128]{2,1,0:T(8,128)(2,1)} %bitcast.4), calls=%async_computation.1 | async-start | bytes 1572864 | tf_op jit(solution)/shard_map/all_to_all | solution.py:601
  29.3 16.5 %copy-start.3 = (bf16[512,512]{1,0:T(8,128)(2,1)S(1)}, bf16[512,512]{1,0:T(8,128)(2,1)}, u32[]{:S(2)}) copy-start(bf16[512,512]{1,0:T(8,128)(2,1)} %w_out.1) | copy-start | bytes 1572868
  29.3 16.5 %copy-start.4 = (s32[24,128]{1,0:T(8,128)S(1)}, s32[24,128]{1,0:T(8,128)}, u32[]{:S(2)}) copy-start(s32[24,128]{1,0:T(8,128)} %send_ref.1) | copy-start | bytes 36868
  29.3 16.5 %copy-start.5 = (s32[24,128]{1,0:T(8,128)S(1)}, s32[24,128]{1,0:T(8,128)}, u32[]{:S(2)}) copy-start(s32[24,128]{1,0:T(8,128)} %recv_ref.1) | copy-start | bytes 36868
  29.3 16.5 %copy-start.6 = (f32[512]{0:T(512)S(1)}, f32[512]{0:T(512)}, u32[]{:S(2)}) copy-start(f32[512]{0:T(512)} %param.19) | copy-start | bytes 6148
  35.4 1.7 %copy-start.7 = (bf16[4,512,768]{2,1,0:T(8,128)(2,1)}, bf16[4,512,768]{2,1,0:T(8,128)(2,1)S(1)}, u32[]{:S(2)}) copy-start(bf16[4,512,768]{2,1,0:T(8,128)(2,1)S(1)} %get-tuple-element.32.turned_hbm) | copy-start | bytes 9437188
  66.2 3.7 %collective-permute-start = (bf16[64,72,128]{2,1,0:T(8,128)(2,1)S(1)}, bf16[64,72,128]{2,1,0:T(8,128)(2,1)S(1)}, u32[]{:S(2)}, u32[]{:S(2)}) collective-permute-start(bf16[64,72,128]{2,1,0:T(8,128)(2,1)S(1)} %get-tuple-element.35), channel_id=1, source_target_pairs={{0,1},{1,0},{2,3},{3,2},{4,5},{5,4},{6,7},{7,6},{8,9},{9,8},{10,11... | collective-permute-start | bytes 3538952 | tf_op jit(solution)/shard_map/ppermute | solution.py:616
  71.2 23.0 %all-to-all-start.2 = ((bf16[64,72,128]{2,1,0:T(8,128)(2,1)}), bf16[64,72,128]{2,1,0:T(8,128)(2,1)S(1)}, u32[]{:S(2)}, u32[]{:S(2)}) async-start(bf16[64,72,128]{2,1,0:T(8,128)(2,1)} %merge.1), calls=%async_computation.2 | async-start | bytes 2359296 | tf_op jit(solution)/shard_map/all_to_all | solution.py:619
  75.8 2.0 %collective-permute-start.1 = (bf16[64,24,128]{2,1,0:T(8,128)(2,1)S(1)}, bf16[64,24,128]{2,1,0:T(8,128)(2,1)S(1)}, u32[]{:S(2)}, u32[]{:S(2)}) collective-permute-start(bf16[64,24,128]{2,1,0:T(8,128)(2,1)S(1)} %get-tuple-element.41), channel_id=1, source_target_pairs={{0,1},{1,0},{2,3},{3,2},{4,5},{5,4},{6,7},{7,6},{8,9},{9,8},{10,11... | collective-permute-start | bytes 1179656 | tf_op jit(solution)/shard_map/ppermute | solution.py:620
  77.9 1.1 copy-start
  96.5 25.2 %all-to-all-start.3 = ((bf16[64,88,128]{2,1,0:T(8,128)(2,1)}), bf16[64,88,128]{2,1,0:T(8,128)(2,1)S(1)}, u32[]{:S(2)}, u32[]{:S(2)}) async-start(bf16[64,88,128]{2,1,0:T(8,128)(2,1)} %get-tuple-element.44), calls=%async_computation.3 | async-start | bytes 2883584 | tf_op jit(solution)/shard_map/all_to_all | solution.py:625
  101.8 23.8 %copy-start.2 = (bf16[320,512]{1,0:T(8,128)(2,1)S(1)}, bf16[320,512]{1,0:T(8,128)(2,1)}, u32[]{:S(2)}) copy-start(bf16[320,512]{1,0:T(8,128)(2,1)} %cots_ref.1) | copy-start | bytes 983044
  121.7 6.8 %collective-permute-start.2 = (bf16[64,88,128]{2,1,0:T(8,128)(2,1)S(1)}, bf16[64,88,128]{2,1,0:T(8,128)(2,1)S(1)}, u32[]{:S(2)}, u32[]{:S(2)}) collective-permute-start(bf16[64,88,128]{2,1,0:T(8,128)(2,1)S(1)} %all-to-all-done.3.packets_ref), channel_id=1, source_target_pairs={{0,1},{1,0},{2,3},{3,2},{4,5},{5,4},{6,7},{7,6},{8,9},{9,8},{10,11... | collective-permute-start | bytes 4325384 | tf_op jit(solution)/shard_map/ppermute | solution.py:628
